TPU v7x, 512 devices: a whole 4x4x16 slice. The times are simulated.
512 devices in a mesh: leaf: 32 (over y, x, core), front: 16 (over z).
Axes of the slice: x: 4, y: 4, z: 16, core: 2. Of those that a mesh axis runs over, the one named last changes fastest.
Arguments:
- leaf_pivot_block: bfloat16 [32, 2048, 256], P('leaf', 'front'), may hold values from -6 to 6
- leaf_rest_block: bfloat16 [32, 512, 256], P('leaf', 'front'), may hold values from -6 to 6
- node_pivot_block: bfloat16 [32, 2048, 256], P('leaf', 'front'), may hold values from -6 to 6
- node_rest_block: bfloat16 [32, 512, 256], P('leaf', 'front'), may hold values from -6 to 6
- leaf_vectors_pivot: bfloat16 [32, 2, 2048, 2048], P('leaf', None, 'front'), may hold values from -0.125 to 0.125
- leaf_vectors_rest: bfloat16 [32, 2, 512, 2048], P('leaf', None, 'front'), may hold values from -0.125 to 0.125
- node_vectors_pivot: bfloat16 [32, 2, 2048, 2048], P('leaf', None, 'front'), may hold values from -0.125 to 0.125
- node_vectors_rest: bfloat16 [32, 2, 512, 2048], P('leaf', None, 'front'), may hold values from -0.125 to 0.125
- stack_place: int32 [32, 1024], P('leaf'), may hold values from 0 to 2559, as said below
- parent_columns: int32 [32, 2, 512], P('leaf'), may hold values from 0 to 2047, as said below
- coupling: bfloat16 [32, 2, 2048, 512], P('leaf', None, 'front'), may hold values from -0.125 to 0.125
- pivot_inverse: bfloat16 [32, 2, 2048, 2048], P('leaf', None, 'front'), may hold values from -0.125 to 0.125
Outputs:
- solution: bfloat16 [32, 2, 2048, 256], P('leaf', None, 'front')
- remainder: bfloat16 [32, 512, 256], P('leaf', 'front')
Inputs may be any that keep to these rules, and one draw needn't show every extreme that they name: `stack_place`: each group's row holds 1024 distinct stack rows. `parent_columns`: each group's row for each slot holds 512 distinct pivot columns.
All inputs are finite; a program needn't handle non-finite values.
Results may differ from a plain program's by a relative error of at most 0.024.
Values may be sent and summed in bfloat16 or wider, within the bound.
No kernel may reach another device: no remote copies, remote signals or barrier semaphores. Data moves between devices by JAX's collectives and lax.ppermute only.
A program may use at most 64 MiB of HBM per device.

v0:
```python
import jax
import jax.numpy as jnp
from jax import lax
from jax.sharding import PartitionSpec as P

K = 2048
C = 512
LEVELS = 2


def in_one_piece(arrays, axis, dim, along):
    ends, at = ([], 0)
    for a in arrays[:-1]:
        at += a.shape[along]
        ends.append(at)
    both = jnp.concatenate(arrays, axis=along)
    return tuple(jnp.split(lax.all_gather(both, axis, axis=dim, tiled=True), ends, axis=along))


def from_behind(block, axis, distance):
    devices = range(lax.axis_size(axis))
    route = [((i - distance) % len(devices), i) for i in devices]
    return lax.ppermute(block, axis, route)


def laid_out(parts, dim):
    lengths = list(parts.shape[1:])
    lengths[dim] *= parts.shape[0]
    return jnp.moveaxis(parts, 0, dim).reshape(lengths)


def sent_to_all(shard, axis):
    copies = jnp.broadcast_to(shard, (lax.axis_size(axis), *shard.shape))
    return lax.all_to_all(copies, axis, split_axis=0, concat_axis=0, tiled=True)


def gather_directly(shard, axis, dim):
    return laid_out(sent_to_all(shard, axis), dim)


def added(first, second):
    return (first.astype(jnp.float32) + second.astype(jnp.float32)).astype(jnp.bfloat16)


def per_device(
    leaf_pivot_block,
    leaf_rest_block,
    node_pivot_block,
    node_rest_block,
    leaf_vectors_pivot,
    leaf_vectors_rest,
    node_vectors_pivot,
    node_vectors_rest,
    stack_place,
    parent_columns,
    coupling,
    pivot_inverse,
):
    subtree = 2**LEVELS
    front_index = lax.axis_index("front")
    pivot_count = leaf_vectors_pivot.shape[2]
    rest_count = leaf_vectors_rest.shape[2]

    def reflect(block_pivot, block_rest, vectors_pivot, vectors_rest):
        partial_value = jnp.einsum(
            "ik,ir->kr", vectors_pivot[1], block_pivot, preferred_element_type=jnp.float32
        )
        partial_value = partial_value + jnp.einsum(
            "ik,ir->kr", vectors_rest[1], block_rest, preferred_element_type=jnp.float32
        )
        summed = lax.psum(partial_value.astype(jnp.bfloat16), "front")
        pivots = block_pivot - jnp.dot(vectors_pivot[0], summed, preferred_element_type=jnp.float32)
        rest = block_rest - jnp.dot(vectors_rest[0], summed, preferred_element_type=jnp.float32)
        return (pivots.astype(jnp.bfloat16), rest.astype(jnp.bfloat16))

    inverse_map = (
        jnp.full((K + C,), -1, jnp.int32).at[stack_place[0]].set(jnp.arange(2 * C, dtype=jnp.int32))
    )
    pivot_rows = front_index * pivot_count + jnp.arange(pivot_count, dtype=jnp.int32)
    rest_rows = K + front_index * rest_count + jnp.arange(rest_count, dtype=jnp.int32)
    pivot_source = inverse_map[pivot_rows]
    rest_source = inverse_map[rest_rows]

    def assemble(left_part, right_part):
        left_whole, right_whole = in_one_piece((left_part, right_part), "front", 0, 1)
        joined = jnp.concatenate([left_whole, right_whole], axis=0)

        def fill_rows(own_rows, source):
            picked_rows = jnp.take(joined, jnp.maximum(source, 0), axis=0)
            return jnp.where((source >= 0)[:, None], picked_rows, own_rows)

        return (
            fill_rows(node_pivot_block[0], pivot_source),
            fill_rows(node_rest_block[0], rest_source),
        )

    def run_node(left_part, right_part):
        stack_pivots, stack_rest = assemble(left_part, right_part)
        return reflect(stack_pivots, stack_rest, node_vectors_pivot[0], node_vectors_rest[0])

    leaf_pivots, leaf_remainder = reflect(
        leaf_pivot_block[0], leaf_rest_block[0], leaf_vectors_pivot[0], leaf_vectors_rest[0]
    )
    left_part = from_behind(leaf_remainder, "leaf", 1)
    node_pivots, node_remainder = run_node(left_part, leaf_remainder)
    height = 2
    offset = 2 ** (height - 2)
    left_part = from_behind(node_remainder, "leaf", offset)
    right_part = from_behind(node_remainder, "leaf", -offset)
    node_pivots, node_remainder = run_node(left_part, right_part)
    root_part = from_behind(node_remainder, "leaf", -(subtree // 2))
    node_pivots, node_remainder = run_node(root_part, jnp.zeros_like(root_part))
    pivots_all, coupling_all = in_one_piece(
        (jnp.stack([leaf_pivots, node_pivots]), coupling[0]), "front", 1, 2
    )

    def settle(which_slot, parent, columns):
        right_side = pivots_all[which_slot].astype(jnp.float32)
        if parent is not None:
            chosen = jnp.take(parent, columns, axis=0)
            right_side = right_side - jnp.dot(
                coupling_all[which_slot], chosen, preferred_element_type=jnp.float32
            )
        result = jnp.dot(
            pivot_inverse[0, which_slot],
            right_side.astype(jnp.bfloat16),
            preferred_element_type=jnp.float32,
        )
        return result.astype(jnp.bfloat16)

    def fetch_parent(parent_part):
        return gather_directly(parent_part, "front", 0)

    node_solution = settle(1, None, None)
    for height in range(LEVELS, 0, -1):
        if height == LEVELS:
            parent_part = from_behind(node_solution, "leaf", subtree // 2)
        else:
            offset = 2 ** (height - 1)
            lower_part = from_behind(node_solution, "leaf", offset)
            higher_part = from_behind(node_solution, "leaf", -offset)
            parent_part = added(higher_part, lower_part)
        node_solution = settle(1, fetch_parent(parent_part), parent_columns[0, 1])
    from_right = from_behind(node_solution, "leaf", -1)
    parent_part = added(from_right, node_solution)
    leaf_solution = settle(0, fetch_parent(parent_part), parent_columns[0, 0])
    solution = jnp.stack([leaf_solution, node_solution])[None]
    return (solution, node_remainder[None])


def solution(mesh):
    in_specs = (
        P("leaf", "front", None),
        P("leaf", "front", None),
        P("leaf", "front", None),
        P("leaf", "front", None),
        P("leaf", None, "front", None),
        P("leaf", None, "front", None),
        P("leaf", None, "front", None),
        P("leaf", None, "front", None),
        P("leaf", None),
        P("leaf", None, None),
        P("leaf", None, "front", None),
        P("leaf", None, "front", None),
    )
    out_specs = (P("leaf", None, "front", None), P("leaf", "front", None))
    return jax.shard_map(
        per_device, mesh=mesh, in_specs=in_specs, out_specs=out_specs, check_vma=False
    )
```

profile of v0, /device:TPU:24, one launch (start us, length us, event | category | flops | bytes accessed | tf_op | source)
XLA Modules:
  0.0 991.4 jit_solution(9829018714895478358)
XLA Ops:
  10.4 4.3 scatter_custom_fusion
  16.7 136.8 %all-reduce.6.cloned.1.call-done = bf16[2048,256]{1,0:T(8,128)(2,1)} async-done(((bf16[2048,256]{1,0:T(8,128)(2,1)}), bf16[2048,256]{1,0:T(8,128)(2,1)}) %all-reduce.6.cloned.1.call-update) | async-done | bytes 1048592 | tf_op jit(solution)/shard_map/psum | solution.py:71
  157.3 5.1 collective-permute-done
  162.4 31.0 %all_gather.12 = bf16[512,512]{1,0:T(8,128)(2,1)S(1)} all-gather(bf16[32,512]{1,0:T(8,128)(2,1)S(1)} %pad_maximum_fusion.5), channel_id=1, replica_groups=mesh['leaf'=32,'front'=16] {'front'}, dimensions={0}, use_global_device_ids=true | all-gather | bytes 557056 | tf_op jit(solution)/shard_map/all_gather | solution.py:17
  197.1 133.1 %all-reduce.8.cloned.1.call-done = bf16[2048,256]{0,1:T(8,128)(2,1)} async-done(((bf16[2048,256]{0,1:T(8,128)(2,1)}), bf16[2048,256]{0,1:T(8,128)(2,1)}) %all-reduce.8.cloned.1.call-update) | async-done | bytes 1048592 | tf_op jit(solution)/shard_map/psum | solution.py:71
  333.8 5.8 collective-permute-start.2
  341.0 31.2 %all_gather.13 = bf16[512,512]{1,0:T(8,128)(2,1)S(1)} all-gather(bf16[32,512]{1,0:T(8,128)(2,1)S(1)} %pad_maximum_fusion.6), channel_id=1, replica_groups=mesh['leaf'=32,'front'=16] {'front'}, dimensions={0}, use_global_device_ids=true | all-gather | bytes 557056 | tf_op jit(solution)/shard_map/all_gather | solution.py:17
  375.9 132.4 %all-reduce.10.cloned.1.call-done = bf16[2048,256]{0,1:T(8,128)(2,1)} async-done(((bf16[2048,256]{0,1:T(8,128)(2,1)}), bf16[2048,256]{0,1:T(8,128)(2,1)}) %all-reduce.10.cloned.1.call-update) | async-done | bytes 1048592 | tf_op jit(solution)/shard_map/psum | solution.py:71
  510.0 4.9 collective-permute-start.3
  516.3 31.2 %all_gather.14 = bf16[512,512]{1,0:T(8,128)(2,1)S(1)} all-gather(bf16[32,512]{1,0:T(8,128)(2,1)S(1)} %concatenate.25), channel_id=1, replica_groups=mesh['leaf'=32,'front'=16] {'front'}, dimensions={0}, use_global_device_ids=true | all-gather | bytes 557056 | tf_op jit(solution)/shard_map/all_gather | solution.py:17
  552.9 135.1 %all-reduce.12.cloned.1.call-done = bf16[2048,256]{0,1:T(8,128)(2,1)} async-done(((bf16[2048,256]{0,1:T(8,128)(2,1)}), bf16[2048,256]{0,1:T(8,128)(2,1)}) %all-reduce.12.cloned.1.call-update) | async-done | bytes 1048592 | tf_op jit(solution)/shard_map/psum | solution.py:71
  690.7 82.8 %all-gather.2.cloned.1.call-done = bf16[2,2048,768]{2,1,0:T(8,128)(2,1)} async-done(((bf16[2,128,768]{2,1,0:T(8,128)(2,1)}), bf16[2,2048,768]{2,1,0:T(8,128)(2,1)}) %all-gather.2.cloned.1.call-update) | async-done | bytes 6291472 | tf_op jit(solution)/shard_map/all_gather | solution.py:17
  775.2 3.4 collective-permute-start.4
  778.6 4.9 collective-permute-done.4
  784.8 7.6 all-to-all-start
  792.5 48.1 %all-to-all-done = bf16[16,128,256]{2,1,0:T(8,128)(2,1)S(1)} async-done(((bf16[16,128,256]{2,1,0:T(8,128)(2,1)}), bf16[16,128,256]{2,1,0:T(8,128)(2,1)S(1)}, u32[]{:S(2)}, u32[]{:S(2)}) %all-to-all-start) | async-done | bytes 1048608 | tf_op jit(solution)/shard_map/all_to_all | solution.py:34
  842.5 3.3 fusion.21
  847.7 2.4 collective-permute-start.6
  850.1 5.3 collective-permute-done.6
  855.6 56.9 %all_to_all.15 = bf16[16,128,256]{2,1,0:T(8,128)(2,1)S(1)} all-to-all(bf16[16,128,256]{2,1,0:T(8,128)(2,1)S(1)} %broadcast_in_dim.87), channel_id=1, replica_groups=mesh['leaf'=32,'front'=16] {'front'}, dimensions={0} | all-to-all | bytes 2097152 | tf_op jit(solution)/shard_map/all_to_all | solution.py:34
  914.5 3.3 fusion.19
  923.3 9.0 all-to-all-start.2
  933.4 45.5 %all-to-all-done.2 = bf16[16,128,256]{2,1,0:T(8,128)(2,1)S(1)} async-done(((bf16[16,128,256]{2,1,0:T(8,128)(2,1)}), bf16[16,128,256]{2,1,0:T(8,128)(2,1)S(1)}, u32[]{:S(2)}, u32[]{:S(2)}) %all-to-all-start.2) | async-done | bytes 1048608 | tf_op jit(solution)/shard_map/all_to_all | solution.py:34
  980.8 3.3 fusion.22
  (117 shorter events, 50.3 us)
Async XLA Ops:
  7.2 146.3 %all-reduce.6.cloned.1.call-start = ((), (), s32[]{:S(2)}) async-start(), calls=%async_computation.3 | async-start | bytes 2097152 | tf_op jit(solution)/shard_map/psum | solution.py:71
  10.3 146.9 %copy-start.9 = (bf16[1,128,256]{2,1,0:T(8,128)(2,1)S(1)}, bf16[1,128,256]{2,1,0:T(8,128)(2,1)}, u32[]{:S(2)}) copy-start(bf16[1,128,256]{2,1,0:T(8,128)(2,1)} %param.20) | copy-start | bytes 196612
  10.3 319.9 %all-reduce.8.cloned.1.call-start = ((), (), s32[]{:S(2)}) async-start(), calls=%async_computation.4 | async-start | bytes 2097152 | tf_op jit(solution)/shard_map/psum | solution.py:71
  155.0 40.1 %copy-start = (bf16[1,2,128,2048]{3,2,1,0:T(8,128)(2,1)S(1)}, bf16[1,2,128,2048]{3,2,1,0:T(8,128)(2,1)}, u32[]{:S(2)}) copy-start(bf16[1,2,128,2048]{3,2,1,0:T(8,128)(2,1)} %param.24) | copy-start | bytes 3145732
  155.1 7.3 collective-permute-start
  193.4 2.1 copy-start.1
  193.4 2.1 copy-start.4
  197.1 311.2 %all-reduce.10.cloned.1.call-start = ((), (), s32[]{:S(2)}) async-start(), calls=%async_computation.5 | async-start | bytes 2097152 | tf_op jit(solution)/shard_map/psum | solution.py:71
  331.9 7.7 collective-permute-start.1
  333.8 7.2 collective-permute-start.2
  375.9 312.2 %all-reduce.12.cloned.1.call-start = ((), (), s32[]{:S(2)}) async-start(), calls=%async_computation.6 | async-start | bytes 2097152 | tf_op jit(solution)/shard_map/psum | solution.py:71
  510.0 6.3 collective-permute-start.3
  549.6 1.7 copy-start.2
  551.1 222.4 %all-gather.2.cloned.1.call-start = ((), (), s32[]{:S(2)}) async-start(), calls=%async_computation.7 | async-start | bytes 6684672 | tf_op jit(solution)/shard_map/all_gather | solution.py:17
  551.3 138.5 %copy-start.6 = (bf16[1,2,128,512]{3,2,1,0:T(8,128)(2,1)S(1)}, bf16[1,2,128,512]{3,2,1,0:T(8,128)(2,1)}, u32[]{:S(2)}) copy-start(bf16[1,2,128,512]{3,2,1,0:T(8,128)(2,1)} %param.28) | copy-start | bytes 786436
  552.9 220.6 %copy-start.12 = (bf16[1,2,128,2048]{3,2,1,0:T(8,128)(2,1)S(1)}, bf16[1,2,128,2048]{3,2,1,0:T(8,128)(2,1)}, u32[]{:S(2)}) copy-start(bf16[1,2,128,2048]{3,2,1,0:T(8,128)(2,1)} %param.29) | copy-start | bytes 3145732
  775.2 17.2 %copy-start.11 = (s32[1,2,512]{2,1,0:T(2,128)S(1)}, s32[1,2,512]{2,1,0:T(2,128)}, u32[]{:S(2)}) copy-start(s32[1,2,512]{2,1,0:T(2,128)} %param.27) | copy-start | bytes 12292
  775.2 8.3 collective-permute-start.4
  784.8 55.8 %all-to-all-start = ((bf16[16,128,256]{2,1,0:T(8,128)(2,1)}), bf16[16,128,256]{2,1,0:T(8,128)(2,1)S(1)}, u32[]{:S(2)}, u32[]{:S(2)}) async-start(bf16[16,128,256]{2,1,0:T(8,128)(2,1)} %broadcast_in_dim.86), calls=%async_computation | async-start | bytes 2097152 | tf_op jit(solution)/shard_map/all_to_all | solution.py:34
  845.8 4.3 collective-permute-start.5
  847.7 7.7 collective-permute-start.6
  917.8 14.5 %copy-start.3 = (bf16[2048,256]{0,1:T(8,128)(2,1)S(1)}, bf16[2048,256]{0,1:T(8,128)(2,1)}, u32[]{:S(2)}) copy-start(bf16[2048,256]{0,1:T(8,128)(2,1)} %all-reduce.12.cloned.1.call-done) | copy-start | bytes 3145732
  917.8 4.2 collective-permute-start.7
  923.3 55.6 %all-to-all-start.2 = ((bf16[16,128,256]{2,1,0:T(8,128)(2,1)}), bf16[16,128,256]{2,1,0:T(8,128)(2,1)S(1)}, u32[]{:S(2)}, u32[]{:S(2)}) async-start(bf16[16,128,256]{2,1,0:T(8,128)(2,1)} %broadcast_in_dim.88), calls=%async_computation.2 | async-start | bytes 2097152 | tf_op jit(solution)/shard_map/all_to_all | solution.py:34
  (4 other events, 6.4 us)
Sparse Core Ops, SparseCore 0:
  10.4 143.0 all-reduce.5
  197.2 132.9 all-reduce.7
  376.0 132.2 all-reduce.9
  551.3 136.7 all-reduce.11
  690.8 82.6 all-gather.1
where the time goes:
time: 994 us; the launch traced here: 991 us
  waiting for transfers between devices  734 us (74%)
  blocking collectives  150 us (15%)
  starting transfers between devices  41.4 us (4%)
  matrix products  29.4 us (3%)
  local copies, waits for them, and re-layouts  20.8 us (2%)
  between operations  14.5 us (1%)
    psum x4, waiting for transfers between devices, reflect(): summed = lax.psum(partial_value.astype(jnp.bfloat16), 'front')  537 us
    all_to_all x2, waiting for transfers between devices, sent_to_all(): return lax.all_to_all(copies, axis, split_axis=0, concat_axis=0, tiled=True)  93.5 us
    all_gather x3, blocking collectives, in_one_piece(): lax.all_gather(both, axis, axis=dim, tiled=True)  93.5 us
    all_gather x1, waiting for transfers between devices, in_one_piece(): lax.all_gather(both, axis, axis=dim, tiled=True)  82.8 us
    all_to_all x1, blocking collectives, sent_to_all(): return lax.all_to_all(copies, axis, split_axis=0, concat_axis=0, tiled=True)  56.9 us
    ppermute x8, starting transfers between devices, from_behind(): return lax.ppermute(block, axis, route)  24.6 us
    ppermute x8, waiting for transfers between devices, from_behind(): return lax.ppermute(block, axis, route)  20 us
  transfers between devices with their start and end apart: 15, of which 13 were waited for; matrix products, arithmetic and copies ran while one was open for 1% of the time, Pallas kernels for 0%

commit v1 on v0

v1 whole, which is shorter than its diff:
```python
import jax
import jax.numpy as jnp
from jax import lax
from jax.sharding import Mesh
from jax.sharding import PartitionSpec as P

LEVELS = 2
FRONT = ("fa", "fb")
BF16 = jnp.bfloat16
F32 = jnp.float32


def mm(spec, a, b):
    return jnp.einsum(spec, a, b, preferred_element_type=F32)


def from_behind(block, distance):
    count = lax.axis_size("leaf")
    return lax.ppermute(block, "leaf", [((i - distance) % count, i) for i in range(count)])


def exchange(parts, axis):
    return lax.all_to_all(parts, axis, split_axis=0, concat_axis=0, tiled=True)


def to_all(block, axis):
    count = 1
    for name in (axis,) if isinstance(axis, str) else axis:
        count *= lax.axis_size(name)
    return exchange(jnp.broadcast_to(block, (count, *block.shape)), axis)


def total(parts):
    return jnp.sum(parts.astype(F32), axis=0)


def added(first, second):
    return (first.astype(F32) + second.astype(F32)).astype(BF16)


def folded(block):
    half = block.shape[0] // 2
    return jnp.concatenate([block[:half], block[half:]], axis=1)


def unfolded(blocks):
    half = blocks.shape[-1] // 2
    return jnp.concatenate([blocks[..., :half], blocks[..., half:]], axis=-2)


def per_device(
    leaf_pivot_block,
    leaf_rest_block,
    node_pivot_block,
    node_rest_block,
    leaf_vectors_pivot,
    leaf_vectors_rest,
    node_vectors_pivot,
    node_vectors_rest,
    stack_place,
    parent_columns,
    coupling,
    pivot_inverse,
):
    na, nb = lax.axis_size("fa"), lax.axis_size("fb")
    fronts = na * nb
    ia, ib = lax.axis_index("fa"), lax.axis_index("fb")
    me = ia * nb + ib
    kp = leaf_vectors_pivot.shape[2]
    kc = leaf_vectors_rest.shape[2]
    ks = kp + kc
    K, C = kp * fronts, kc * fronts
    R = leaf_pivot_block.shape[2]
    rc = R // fronts
    place = stack_place[0]
    subtree = 2**LEVELS

    def stack_rows(device):
        device = jnp.asarray(device, jnp.int32)
        return jnp.concatenate(
            [
                device * kp + jnp.arange(kp, dtype=jnp.int32),
                K + device * kc + jnp.arange(kc, dtype=jnp.int32),
            ]
        )

    ve_blocks = jnp.concatenate(jnp.split(node_vectors_rest[0, 0], K // C, axis=1), axis=0)
    gathered = lax.all_gather(jnp.concatenate([ve_blocks, coupling[0, 1]], axis=0), FRONT, axis=0)
    ve_all = gathered[:, : kc * (K // C)].reshape(fronts, K // C, kc, C)
    coupling_all = gathered[:, kc * (K // C) :].reshape(K, C)

    node_w = jnp.concatenate([node_vectors_pivot[0, 1], node_vectors_rest[0, 1]], axis=0)
    node_v = jnp.concatenate([node_vectors_pivot[0, 0], node_vectors_rest[0, 0]], axis=0)
    rows = stack_rows(me)
    unit = (rows[:, None] == K + jnp.arange(C, dtype=jnp.int32)[None]).astype(F32)
    product = mm("sbk,dbck->sdc", node_w.reshape(ks, K // C, C), ve_all).reshape(ks, C)
    section_rows = (unit - product).astype(BF16)
    node_reach = mm("pm,mc->pc", pivot_inverse[0, 1], coupling_all).astype(BF16)
    gathered = lax.all_gather(jnp.concatenate([section_rows, node_reach], axis=0), FRONT, axis=0)
    section_all = gathered[:, :ks].reshape(fronts * ks, C)
    node_reach_all = gathered[:, ks:].reshape(K, C)

    leaf_partial = mm("ik,ir->kr", leaf_vectors_pivot[0, 1], leaf_pivot_block[0])
    leaf_partial = leaf_partial + mm("ik,ir->kr", leaf_vectors_rest[0, 1], leaf_rest_block[0])
    part = exchange(leaf_partial.astype(BF16).reshape(nb, K // nb, R), "fb")
    part = exchange(total(part).astype(BF16).reshape(na, kp, R), "fa")
    leaf_y = to_all(to_all(total(part).astype(BF16), "fa").reshape(K // nb, R), "fb").reshape(K, R)
    leaf_pivots = (leaf_pivot_block[0] - mm("pk,kr->pr", leaf_vectors_pivot[0, 0], leaf_y)).astype(BF16)
    leaf_rest = (leaf_rest_block[0] - mm("pk,kr->pr", leaf_vectors_rest[0, 0], leaf_y)).astype(BF16)

    own_hit = rows[:, None] == place[None]
    own = jnp.concatenate([node_pivot_block[0], node_rest_block[0]], axis=0)
    own = jnp.where(jnp.any(own_hit, axis=1)[:, None], jnp.zeros_like(own), own)

    both = jnp.concatenate([leaf_rest, own], axis=0).T.reshape(fronts, rc, kc + ks)
    both = exchange(both, FRONT)
    rest = both[:, :, :kc].transpose(1, 0, 2).reshape(rc, C)
    own_columns = both[:, :, kc:].transpose(1, 0, 2).reshape(rc, fronts * ks)

    blocks = jnp.concatenate([node_w, node_v], axis=0).reshape(2 * ks, nb, K // nb).transpose(1, 0, 2)
    own_folded = folded(own)
    blocks = jnp.concatenate([blocks, jnp.broadcast_to(own_folded, (nb, *own_folded.shape))], axis=1)
    blocks = exchange(blocks, "fb")
    w_block = blocks[:, :ks].reshape(nb * ks, K // nb)
    v_block = blocks[:, ks : 2 * ks].reshape(nb * ks, K // nb)
    own_block = unfolded(blocks[:, 2 * ks :]).reshape(nb * ks, R)
    inverse_block = pivot_inverse[0, 1].reshape(kp, na, K // na).transpose(1, 0, 2)
    inverse_block = exchange(inverse_block, "fa").reshape(na * kp, K // na)
    block_rows = jnp.concatenate([stack_rows(ia * nb + b) for b in range(nb)])
    block_hit = (place[:C, None] == block_rows[None]).astype(BF16)
    w_left = mm("cs,sk->ck", block_hit, w_block).astype(BF16)
    y_own = mm("sr,sk->rk", own_block, w_block)

    device = jnp.where(place < K, place // kp, (place - K) // kc)
    within = jnp.where(place < K, place % kp, kp + (place - K) % kc)
    section_map = jnp.take(section_all, device * ks + within, axis=0)
    section_own = mm("rs,sc->rc", own_columns, section_all)

    def section(left, right):
        children = jnp.concatenate([left, right], axis=1)
        return (section_own + mm("rj,jc->rc", children, section_map)).astype(BF16)

    rest = section(from_behind(rest, 1), rest)
    rest = section(from_behind(rest, 1), from_behind(rest, -1))
    left = to_all(from_behind(rest, -(subtree // 2)), FRONT).reshape(R, C)

    partial_y = (y_own + mm("rc,ck->rk", left, w_left)).astype(BF16)
    part = total(exchange(partial_y.reshape(na, R // na, K // nb), "fa")).astype(BF16)
    y_block = to_all(part, "fa").reshape(R, K // nb)
    part = mm("sk,rk->sr", v_block, y_block).astype(BF16).reshape(nb, ks, R)
    placed = mm("sc,rc->sr", own_hit[:, :C].astype(BF16), left)
    reflected = own.astype(F32) + placed - total(exchange(part, "fb"))
    reflected = reflected.astype(BF16)
    remainder = reflected[kp:]
    pivots = to_all(reflected[:kp], "fb").reshape(nb * kp, R)
    part = mm("mr,pm->rp", pivots, inverse_block).astype(BF16)
    part = total(exchange(part.reshape(na, R // na, na * kp), "fa")).astype(BF16)
    part = exchange(part.reshape(nb, rc, na * kp), "fb")
    top = part.reshape(nb, rc, na, kp).transpose(1, 2, 0, 3).reshape(rc, K)

    wide = jnp.concatenate([coupling[0, 0], folded(leaf_pivots)], axis=0)
    wide, gathered = lax.optimization_barrier((wide, gathered))
    gathered_leaf = lax.all_gather(wide, FRONT, axis=0)
    leaf_coupling_all = gathered_leaf[:, :kp].reshape(K, C)
    leaf_pivots_all = unfolded(gathered_leaf[:, kp:]).reshape(K, R)
    leaf_reach = mm("pm,mc->pc", pivot_inverse[0, 0], leaf_coupling_all).astype(BF16)
    leaf_own = mm("pm,mr->pr", pivot_inverse[0, 0], leaf_pivots_all).astype(BF16)
    wide = jnp.concatenate([leaf_reach, folded(leaf_own)], axis=0)
    gathered_leaf = lax.all_gather(wide, FRONT, axis=0)
    leaf_reach_all = gathered_leaf[:, :kp].reshape(K, C)
    leaf_own_all = unfolded(gathered_leaf[:, kp:]).reshape(K, R)
    mine = (me * rc + jnp.arange(rc, dtype=jnp.int32))[:, None] == jnp.arange(R, dtype=jnp.int32)[None]
    leaf_own_columns = mm("qr,pr->qp", mine.astype(BF16), leaf_own_all)

    pivot_ids = jnp.arange(K, dtype=jnp.int32)[:, None]
    node_pick = (pivot_ids == parent_columns[0, 1][None]).astype(BF16)
    leaf_pick = (pivot_ids == parent_columns[0, 0][None]).astype(BF16)

    def settle(base, parent, pick, reach):
        chosen = mm("rp,pc->rc", parent, pick).astype(BF16)
        return (base - mm("rc,pc->rp", chosen, reach)).astype(BF16)

    node = top
    for height in range(LEVELS, 0, -1):
        if height == LEVELS:
            parent = from_behind(node, subtree // 2)
        else:
            offset = 2 ** (height - 1)
            parent = added(from_behind(node, -offset), from_behind(node, offset))
        node = settle(top.astype(F32), parent, node_pick, node_reach_all)
    parent = added(from_behind(node, -1), node)
    leaf = settle(leaf_own_columns, parent, leaf_pick, leaf_reach_all)
    both = jnp.stack([leaf, node]).reshape(2, rc, fronts, kp).transpose(2, 0, 1, 3)
    both = exchange(both, FRONT)
    both = both.transpose(1, 3, 0, 2).reshape(2, kp, R)
    return (both[None], remainder[None])


def solution(mesh):
    leaves, fronts = mesh.devices.shape
    nb = next(n for n in range(max(1, int(fronts**0.5)), 0, -1) if fronts % n == 0)
    grid = Mesh(mesh.devices.reshape(leaves, fronts // nb, nb), ("leaf", "fa", "fb"))
    rows3 = P("leaf", FRONT, None)
    rows4 = P("leaf", None, FRONT, None)
    in_specs = (
        *([rows3] * 4),
        *([rows4] * 4),
        P("leaf", None),
        P("leaf", None, None),
        rows4,
        rows4,
    )
    return jax.shard_map(
        per_device, mesh=grid, in_specs=in_specs, out_specs=(rows4, rows3), check_vma=False
    )
```

time: 994 us -> 504 us (0.51)
  waiting for transfers between devices: 734 us -> 248 us
  blocking collectives: 150 us -> 106 us
  starting transfers between devices: 41.4 us -> 70.4 us
  local copies, waits for them, and re-layouts: 20.8 us -> 32.8 us
    psum x4 -> x0, waiting for transfers between devices: 537 us -> none  [reflect(): summed = lax.psum(partial_value.astype(jnp.bfloat16), 'front')]
    all_gather x3 -> x0, blocking collectives: 93.5 us -> none  [in_one_piece(): lax.all_gather(both, axis, axis=dim, tiled=True)]
    all_to_all x2 -> x10, waiting for transfers between devices: 93.5 us -> 154 us  [exchange(): return lax.all_to_all(parts, axis, split_axis=0, concat_axis=0, tiled=True)]
    all_to_all x1 -> x5, blocking collectives: 56.9 us -> 106 us  [exchange(): return lax.all_to_all(parts, axis, split_axis=0, concat_axis=0, tiled=True)]
    all_to_all x2 -> x10, starting transfers between devices: 16.6 us -> 44.6 us  [exchange(): return lax.all_to_all(parts, axis, split_axis=0, concat_axis=0, tiled=True)]
    slice x1 -> x19, local copies, waits for them, and re-layouts: 0.01 us -> 14.6 us  [the longest x3 3.66 us: unfolded(): return jnp.concatenate([blocks[..., :half], blocks[..., half:]], axis=-2)]
    ppermute x8, waiting for transfers between devices: 20 us -> 6.73 us  [from_behind(): lax.ppermute(block, 'leaf', [((i - distance) % count, i) for i in range(c...]
    dot_general x18 -> x20, matrix products: 29.4 us -> 20.3 us  [mm(): return jnp.einsum(spec, a, b, preferred_element_type=F32)]
  transfers between devices with their start and end apart: 15 -> 22, of which waited for: 13 -> 15; matrix products, arithmetic and copies ran while one was open for 1% -> 10% of each run, Pallas kernels for 0% -> 0%
where the time goes in v1:
time: 504 us; the launch traced here: 497 us
  waiting for transfers between devices  248 us (49%)
  blocking collectives  106 us (21%)
  starting transfers between devices  70.4 us (14%)
  local copies, waits for them, and re-layouts  32.8 us (7%)
  matrix products  20.3 us (4%)
  between operations  14.7 us (3%)
  other arithmetic  5.3 us (1%)
    all_to_all x10, waiting for transfers between devices, exchange(): return lax.all_to_all(parts, axis, split_axis=0, concat_axis=0, tiled=True)  154 us
    all_to_all x5, blocking collectives, exchange(): return lax.all_to_all(parts, axis, split_axis=0, concat_axis=0, tiled=True)  106 us
    all_gather x1, waiting for transfers between devices, per_device(): lax.all_gather(jnp.concatenate([ve_blocks, coupling[0, 1]], axis=0), FRON...  84.2 us
    all_to_all x10, starting transfers between devices, exchange(): return lax.all_to_all(parts, axis, split_axis=0, concat_axis=0, tiled=True)  44.6 us
    ppermute x8, starting transfers between devices, from_behind(): lax.ppermute(block, 'leaf', [((i - distance) % count, i) for i in range(c...  25.7 us
    dot_general x20, matrix products, mm(): return jnp.einsum(spec, a, b, preferred_element_type=F32)  20.3 us
  transfers between devices with their start and end apart: 22, of which 15 were waited for; matrix products, arithmetic and copies ran while one was open for 10% of the time, Pallas kernels for 0%

profile of v1, /device:TPU:24, one launch (start us, length us, event | category | flops | bytes accessed | tf_op | source)
XLA Modules:
  0.0 497.1 jit_solution(13207365783046542990)
XLA Ops:
  13.0 6.0 %all-to-all-start = ((bf16[4,512,256]{2,1,0:T(8,128)(2,1)}), bf16[4,512,256]{2,1,0:T(8,128)(2,1)S(1)}, u32[]{:S(2)}, u32[]{:S(2)}) async-start(bf16[4,512,256]{2,1,0:T(8,128)(2,1)} %bitcast.5), calls=%async_computation | async-start | bytes 2097152 | tf_op jit(solution)/shard_map/all_to_all | solution.py:23
  19.8 84.2 %all-gather.9.cloned.1.call-done = bf16[4096,512]{1,0:T(8,128)(2,1)} async-done(((bf16[256,512]{1,0:T(8,128)(2,1)}), bf16[4096,512]{1,0:T(8,128)(2,1)}) %all-gather.9.cloned.1.call-update) | async-done | bytes 4194320 | tf_op jit(solution)/shard_map/all_gather | solution.py:88
  109.4 23.6 %all_to_all.75 = bf16[4,128,256]{2,1,0:T(8,128)(2,1)S(1)} all-to-all(bf16[4,128,256]{2,1,0:T(8,128)(2,1)S(1)} %bitcast.193), channel_id=1, replica_groups=mesh['leaf'=32,'fa'=4,'fb'=4] {'fa'}, dimensions={0} | all-to-all | bytes 524288 | tf_op jit(solution)/shard_map/all_to_all | solution.py:23
  133.0 23.8 %all_to_all.76 = bf16[4,128,256]{2,1,0:T(8,128)(2,1)S(1)} all-to-all(bf16[4,128,256]{2,1,0:T(8,128)(2,1)S(1)} %broadcast_in_dim.51), channel_id=1, replica_groups=mesh['leaf'=32,'fa'=4,'fb'=4] {'fa'}, dimensions={0} | all-to-all | bytes 524288 | tf_op jit(solution)/shard_map/all_to_all | solution.py:23
  162.6 33.2 %all-to-all-done.3 = bf16[4,512,256]{2,1,0:T(8,128)(2,1)S(1)} async-done(((bf16[4,512,256]{2,1,0:T(8,128)(2,1)}), bf16[4,512,256]{2,1,0:T(8,128)(2,1)S(1)}, u32[]{:S(2)}, u32[]{:S(2)}) %all-to-all-start.3) | async-done | bytes 1048608 | tf_op jit(solution)/shard_map/all_to_all | solution.py:23
  197.8 4.3 all-to-all-start.4
  203.5 13.0 %all-to-all-done.4 = bf16[16,16,192]{2,1,0:T(8,128)(2,1)S(1)} async-done(((bf16[16,16,192]{2,1,0:T(8,128)(2,1)}), bf16[16,16,192]{2,1,0:T(8,128)(2,1)S(1)}, u32[]{:S(2)}, u32[]{:S(2)}) %all-to-all-start.4) | async-done | bytes 98336 | tf_op jit(solution)/shard_map/all_to_all | solution.py:23
  216.5 4.4 all-to-all-start.6
  230.8 5.1 %gather_fusion = bf16[1024,512]{1,0:T(8,128)(2,1)} fusion(bf16[2560,512]{1,0:T(8,128)(2,1)S(1)} %bitcast.168, s32[1024]{0:T(1024)S(1)} %broadcast_clamp_fusion), kind=kCustom, calls=%fused_computation | custom fusion | bytes 2101248 | tf_op jit(solution)/shard_map/jit(_take)/gather | solution.py:136
  240.4 4.7 collective-permute-start.2
  250.7 6.1 %all-to-all-done.6 = bf16[4,400,512]{2,1,0:T(8,128)(2,1)} async-done(((bf16[4,400,512]{2,1,0:T(8,128)(2,1)}), bf16[4,400,512]{2,1,0:T(8,128)(2,1)}, u32[]{:S(2)}, u32[]{:S(2)}) %all-to-all-start.6) | async-done | bytes 1638432 | tf_op jit(solution)/shard_map/all_to_all | solution.py:23
  257.6 6.8 %all-to-all-start.5 = ((bf16[16,16,512]{2,1,0:T(8,128)(2,1)}), bf16[16,16,512]{2,1,0:T(8,128)(2,1)S(1)}, u32[]{:S(2)}, u32[]{:S(2)}) async-start(bf16[16,16,512]{2,1,0:T(8,128)(2,1)} %broadcast_in_dim.57), calls=%async_computation.5 | async-start | bytes 524288 | tf_op jit(solution)/shard_map/all_to_all | solution.py:23
  268.5 18.1 %all-to-all-done.5 = bf16[16,16,512]{2,1,0:T(8,128)(2,1)S(1)} async-done(((bf16[16,16,512]{2,1,0:T(8,128)(2,1)}), bf16[16,16,512]{2,1,0:T(8,128)(2,1)S(1)}, u32[]{:S(2)}, u32[]{:S(2)}) %all-to-all-start.5) | async-done | bytes 262176 | tf_op jit(solution)/shard_map/all_to_all | solution.py:23
  287.4 28.6 %all_to_all.77 = bf16[4,64,512]{2,1,0:T(8,128)(2,1)S(1)} all-to-all(bf16[4,64,512]{2,1,0:T(8,128)(2,1)S(1)} %bitcast.203), channel_id=1, replica_groups=mesh['leaf'=32,'fa'=4,'fb'=4] {'fa'}, dimensions={0} | all-to-all | bytes 524288 | tf_op jit(solution)/shard_map/all_to_all | solution.py:23
  327.2 11.5 %all-to-all-done.8 = bf16[4,64,512]{2,1,0:T(8,128)(2,1)S(1)} async-done(((bf16[4,64,512]{2,1,0:T(8,128)(2,1)}), bf16[4,64,512]{2,1,0:T(8,128)(2,1)S(1)}, u32[]{:S(2)}, u32[]{:S(2)}) %all-to-all-start.8) | async-done | bytes 262176 | tf_op jit(solution)/shard_map/all_to_all | solution.py:23
  339.9 5.7 %all-to-all-start.9 = ((bf16[4,160,256]{2,1,0:T(8,128)(2,1)}), bf16[4,160,256]{2,1,0:T(8,128)(2,1)S(1)}, u32[]{:S(2)}, u32[]{:S(2)}) async-start(bf16[4,160,256]{2,1,0:T(8,128)(2,1)} %bitcast.53), calls=%async_computation.9 | async-start | bytes 655360 | tf_op jit(solution)/shard_map/all_to_all | solution.py:23
  346.6 12.3 %all-to-all-done.9 = bf16[4,160,256]{2,1,0:T(8,128)(2,1)S(1)} async-done(((bf16[4,160,256]{2,1,0:T(8,128)(2,1)}), bf16[4,160,256]{2,1,0:T(8,128)(2,1)S(1)}, u32[]{:S(2)}, u32[]{:S(2)}) %all-to-all-start.9) | async-done | bytes 327712 | tf_op jit(solution)/shard_map/all_to_all | solution.py:23
  362.7 35.4 %all-to-all-done.11 = bf16[4,128,512]{1,2,0:T(8,128)(2,1)S(1)} async-done(((bf16[4,128,512]{1,2,0:T(8,128)(2,1)}), bf16[4,128,512]{1,2,0:T(8,128)(2,1)S(1)}, u32[]{:S(2)}, u32[]{:S(2)}) %all-to-all-start.11) | async-done | bytes 524320 | tf_op jit(solution)/shard_map/all_to_all | solution.py:23
  402.4 10.8 %all-to-all-done.10 = bf16[4,128,256]{2,1,0:T(8,128)(2,1)S(1)} async-done(((bf16[4,128,256]{2,1,0:T(8,128)(2,1)}), bf16[4,128,256]{2,1,0:T(8,128)(2,1)S(1)}, u32[]{:S(2)}, u32[]{:S(2)}) %all-to-all-start.10) | async-done | bytes 262176 | tf_op jit(solution)/shard_map/all_to_all | solution.py:23
  413.6 20.0 %all_to_all.78 = bf16[4,64,512]{2,1,0:T(8,128)(2,1)S(1)} all-to-all(bf16[4,64,512]{2,1,0:T(8,128)(2,1)S(1)} %bitcast.198), channel_id=1, replica_groups=mesh['leaf'=32,'fa'=4,'fb'=4] {'fa'}, dimensions={0} | all-to-all | bytes 524288 | tf_op jit(solution)/shard_map/all_to_all | solution.py:23
  433.6 9.7 %all_to_all.79 = bf16[4,16,512]{2,1,0:T(8,128)(2,1)S(1)} all-to-all(bf16[4,16,512]{2,1,0:T(8,128)(2,1)S(1)} %bitcast.202), channel_id=1, replica_groups=mesh['leaf'=32,'fa'=4,'fb'=4] {'fb'}, dimensions={0} | all-to-all | bytes 131072 | tf_op jit(solution)/shard_map/all_to_all | solution.py:23
  443.4 7.3 %collective-permute-start.4 = (bf16[16,2048]{1,0:T(8,128)(2,1)S(1)}, bf16[16,2048]{1,0:T(8,128)(2,1)S(1)}, u32[]{:S(2)}, u32[]{:S(2)}) collective-permute-start(bf16[16,2048]{1,0:T(8,128)(2,1)S(1)} %reshape.352), channel_id=1, source_target_pairs={{480,0},{496,16},{0,32},{16,48},{32,64},{48,80},{64,96},{80,112},{... | collective-permute-start | bytes 196616 | tf_op jit(solution)/shard_map/ppermute | solution.py:19
  458.3 5.3 %collective-permute-done.6 = bf16[16,2048]{1,0:T(8,128)(2,1)S(1)} collective-permute-done((bf16[16,2048]{1,0:T(8,128)(2,1)S(1)}, bf16[16,2048]{1,0:T(8,128)(2,1)S(1)}, u32[]{:S(2)}, u32[]{:S(2)}) %collective-permute-start.6) | collective-permute-done | bytes 65568 | tf_op jit(solution)/shard_map/ppermute | solution.py:19
  476.6 13.2 %all-to-all-done.14 = bf16[16,2,16,128]{3,2,1,0:T(8,128)(2,1)S(1)} async-done(((bf16[16,2,16,128]{3,2,1,0:T(8,128)(2,1)}), bf16[16,2,16,128]{3,2,1,0:T(8,128)(2,1)S(1)}, u32[]{:S(2)}, u32[]{:S(2)}) %all-to-all-start.14) | async-done | bytes 131104 | tf_op jit(solution)/shard_map/all_to_all | solution.py:23
  (164 shorter events, 89.5 us)
Async XLA Ops:
  7.2 96.9 %all-gather.9.cloned.1.call-start = ((), (), s32[]{:S(2)}) async-start(), calls=%async_computation.15 | async-start | bytes 4456448 | tf_op jit(solution)/shard_map/all_gather | solution.py:88
  13.0 96.2 %all-to-all-start = ((bf16[4,512,256]{2,1,0:T(8,128)(2,1)}), bf16[4,512,256]{2,1,0:T(8,128)(2,1)S(1)}, u32[]{:S(2)}, u32[]{:S(2)}) async-start(bf16[4,512,256]{2,1,0:T(8,128)(2,1)} %bitcast.5), calls=%async_computation | async-start | bytes 2097152 | tf_op jit(solution)/shard_map/all_to_all | solution.py:23
  19.0 205.2 %all-gather.11.cloned.1.call-start = ((), (), s32[]{:S(2)}) async-start(), calls=%async_computation.16 | async-start | bytes 5013504 | tf_op jit(solution)/shard_map/all_gather | solution.py:99
  157.9 37.9 %all-to-all-start.3 = ((bf16[4,512,256]{2,1,0:T(8,128)(2,1)}), bf16[4,512,256]{2,1,0:T(8,128)(2,1)S(1)}, u32[]{:S(2)}, u32[]{:S(2)}) async-start(bf16[4,512,256]{2,1,0:T(8,128)(2,1)} %broadcast_in_dim.52), calls=%async_computation.3 | async-start | bytes 2097152 | tf_op jit(solution)/shard_map/all_to_all | solution.py:23
  197.8 18.8 %all-to-all-start.4 = ((bf16[16,16,192]{2,1,0:T(8,128)(2,1)}), bf16[16,16,192]{2,1,0:T(8,128)(2,1)S(1)}, u32[]{:S(2)}, u32[]{:S(2)}) async-start(bf16[16,16,192]{2,1,0:T(8,128)(2,1)} %bitcast.37), calls=%async_computation.4 | async-start | bytes 262144 | tf_op jit(solution)/shard_map/all_to_all | solution.py:23
  216.5 40.3 %all-to-all-start.6 = ((bf16[4,400,512]{2,1,0:T(8,128)(2,1)}), bf16[4,400,512]{2,1,0:T(8,128)(2,1)}, u32[]{:S(2)}, u32[]{:S(2)}) async-start(bf16[4,400,512]{2,1,0:T(8,128)(2,1)} %pad_maximum_fusion), calls=%async_computation.6 | async-start | bytes 3276800 | tf_op jit(solution)/shard_map/all_to_all | solution.py:23
  220.9 100.5 %all-gather.13.cloned.1.call-start = ((), (), s32[]{:S(2)}) async-start(), calls=%async_computation.17 | async-start | bytes 3342336 | tf_op jit(solution)/shard_map/all_gather | solution.py:163
  224.6 11.3 %collective-permute-start = (bf16[16,512]{1,0:T(8,128)(2,1)S(1)}, bf16[16,512]{1,0:T(8,128)(2,1)S(1)}, u32[]{:S(2)}, u32[]{:S(2)}) collective-permute-start(bf16[16,512]{1,0:T(8,128)(2,1)S(1)} %reshape.339), channel_id=1, source_target_pairs={{496,0},{0,16},{16,32},{32,48},{48,64},{64,80},{80,96},{96,112},{1... | collective-permute-start | bytes 49160 | tf_op jit(solution)/shard_map/ppermute | solution.py:19
  237.4 7.7 %collective-permute-start.1 = (bf16[16,512]{1,0:T(8,128)(2,1)S(1)}, bf16[16,512]{1,0:T(8,128)(2,1)S(1)}, u32[]{:S(2)}, u32[]{:S(2)}) collective-permute-start(bf16[16,512]{1,0:T(8,128)(2,1)S(1)} %fusion.35), channel_id=1, source_target_pairs={{496,0},{0,16},{16,32},{32,48},{48,64},{64,80},{80,96},{96,112},{1... | collective-permute-start | bytes 49160 | tf_op jit(solution)/shard_map/ppermute | solution.py:19
  240.4 6.2 %collective-permute-start.2 = (bf16[16,512]{1,0:T(8,128)(2,1)S(1)}, bf16[16,512]{1,0:T(8,128)(2,1)S(1)}, u32[]{:S(2)}, u32[]{:S(2)}) collective-permute-start(bf16[16,512]{1,0:T(8,128)(2,1)S(1)} %fusion.35), channel_id=1, source_target_pairs={{16,0},{32,16},{48,32},{64,48},{80,64},{96,80},{112,96},{128,112},... | collective-permute-start | bytes 49160 | tf_op jit(solution)/shard_map/ppermute | solution.py:19
  248.1 8.7 %collective-permute-start.3 = (bf16[16,512]{1,0:T(8,128)(2,1)S(1)}, bf16[16,512]{1,0:T(8,128)(2,1)S(1)}, u32[]{:S(2)}, u32[]{:S(2)}) collective-permute-start(bf16[16,512]{1,0:T(8,128)(2,1)S(1)} %fusion.36), channel_id=1, source_target_pairs={{32,0},{48,16},{64,32},{80,48},{96,64},{112,80},{128,96},{144,112}... | collective-permute-start | bytes 49160 | tf_op jit(solution)/shard_map/ppermute | solution.py:19
  257.6 29.0 %all-to-all-start.5 = ((bf16[16,16,512]{2,1,0:T(8,128)(2,1)}), bf16[16,16,512]{2,1,0:T(8,128)(2,1)S(1)}, u32[]{:S(2)}, u32[]{:S(2)}) async-start(bf16[16,16,512]{2,1,0:T(8,128)(2,1)} %broadcast_in_dim.57), calls=%async_computation.5 | async-start | bytes 524288 | tf_op jit(solution)/shard_map/all_to_all | solution.py:23
  316.7 22.0 %all-to-all-start.8 = ((bf16[4,64,512]{2,1,0:T(8,128)(2,1)}), bf16[4,64,512]{2,1,0:T(8,128)(2,1)S(1)}, u32[]{:S(2)}, u32[]{:S(2)}) async-start(bf16[4,64,512]{2,1,0:T(8,128)(2,1)} %broadcast_in_dim.59), calls=%async_computation.8 | async-start | bytes 524288 | tf_op jit(solution)/shard_map/all_to_all | solution.py:23
  320.1 146.8 %all-gather.15.cloned.1.call-start = ((), (), s32[]{:S(2)}) async-start(), calls=%async_computation.18 | async-start | bytes 3342336 | tf_op jit(solution)/shard_map/all_gather | solution.py:169
  326.5 19.1 %slice-start = ((bf16[1,2,128,2048]{3,2,1,0:T(8,128)(2,1)}), bf16[1,1,128,2048]{3,2,1,0:T(8,128)(2,1)S(1)}, s32[]{:S(2)}) async-start(bf16[1,2,128,2048]{3,2,1,0:T(8,128)(2,1)} %param.23), calls=%async_computation.19 | async-start | bytes 1048576 | tf_op jit(solution)/shard_map/slice | solution.py:98
  339.9 19.0 %all-to-all-start.9 = ((bf16[4,160,256]{2,1,0:T(8,128)(2,1)}), bf16[4,160,256]{2,1,0:T(8,128)(2,1)S(1)}, u32[]{:S(2)}, u32[]{:S(2)}) async-start(bf16[4,160,256]{2,1,0:T(8,128)(2,1)} %bitcast.53), calls=%async_computation.9 | async-start | bytes 655360 | tf_op jit(solution)/shard_map/all_to_all | solution.py:23
  358.9 39.2 %all-to-all-start.11 = ((bf16[4,128,512]{1,2,0:T(8,128)(2,1)}), bf16[4,128,512]{1,2,0:T(8,128)(2,1)S(1)}, u32[]{:S(2)}, u32[]{:S(2)}) async-start(bf16[4,128,512]{1,2,0:T(8,128)(2,1)} %bitcast.56), calls=%async_computation.11 | async-start | bytes 1048576 | tf_op jit(solution)/shard_map/all_to_all | solution.py:23
  362.7 88.0 %copy-start.13 = (s32[1,2,512]{2,1,0:T(2,128)S(1)}, s32[1,2,512]{2,1,0:T(2,128)}, u32[]{:S(2)}) copy-start(s32[1,2,512]{2,1,0:T(2,128)} %param.21) | copy-start | bytes 12292
  398.8 14.4 %all-to-all-start.10 = ((bf16[4,128,256]{2,1,0:T(8,128)(2,1)}), bf16[4,128,256]{2,1,0:T(8,128)(2,1)S(1)}, u32[]{:S(2)}, u32[]{:S(2)}) async-start(bf16[4,128,256]{2,1,0:T(8,128)(2,1)} %broadcast_in_dim.60), calls=%async_computation.10 | async-start | bytes 524288 | tf_op jit(solution)/shard_map/all_to_all | solution.py:23
  443.4 9.2 %collective-permute-start.4 = (bf16[16,2048]{1,0:T(8,128)(2,1)S(1)}, bf16[16,2048]{1,0:T(8,128)(2,1)S(1)}, u32[]{:S(2)}, u32[]{:S(2)}) collective-permute-start(bf16[16,2048]{1,0:T(8,128)(2,1)S(1)} %reshape.352), channel_id=1, source_target_pairs={{480,0},{496,16},{0,32},{16,48},{32,64},{48,80},{64,96},{80,112},{... | collective-permute-start | bytes 196616 | tf_op jit(solution)/shard_map/ppermute | solution.py:19
  453.9 4.4 collective-permute-start.5
  455.9 7.7 %collective-permute-start.6 = (bf16[16,2048]{1,0:T(8,128)(2,1)S(1)}, bf16[16,2048]{1,0:T(8,128)(2,1)S(1)}, u32[]{:S(2)}, u32[]{:S(2)}) collective-permute-start(bf16[16,2048]{1,0:T(8,128)(2,1)S(1)} %fusion.4), channel_id=1, source_target_pairs={{496,0},{0,16},{16,32},{32,48},{48,64},{64,80},{80,96},{96,112},{1... | collective-permute-start | bytes 196616 | tf_op jit(solution)/shard_map/ppermute | solution.py:19
  464.9 5.4 %collective-permute-start.7 = (bf16[16,2048]{1,0:T(8,128)(2,1)S(1)}, bf16[16,2048]{1,0:T(8,128)(2,1)S(1)}, u32[]{:S(2)}, u32[]{:S(2)}) collective-permute-start(bf16[16,2048]{1,0:T(8,128)(2,1)S(1)} %fusion.5), channel_id=1, source_target_pairs={{16,0},{32,16},{48,32},{64,48},{80,64},{96,80},{112,96},{128,112},... | collective-permute-start | bytes 196616 | tf_op jit(solution)/shard_map/ppermute | solution.py:19
  472.4 17.4 %all-to-all-start.14 = ((bf16[16,2,16,128]{3,2,1,0:T(8,128)(2,1)}), bf16[16,2,16,128]{3,2,1,0:T(8,128)(2,1)S(1)}, u32[]{:S(2)}, u32[]{:S(2)}) async-start(bf16[16,2,16,128]{3,2,1,0:T(8,128)(2,1)} %maximum_bitcast_fusion.1), calls=%async_computation.14 | async-start | bytes 262144 | tf_op jit(solution)/shard_map/all_to_all | solution.py:23
  (13 other events, 85.6 us)
Sparse Core Ops, SparseCore 0:
  10.1 93.9 all-gather.8
  109.3 114.9 all-gather.10
  226.3 94.9 all-gather.12
  327.4 103.0 all-gather.14

commit v2 on v1

v2 whole, which is shorter than its diff:
```python
import jax
import jax.numpy as jnp
from jax import lax
from jax.sharding import Mesh
from jax.sharding import PartitionSpec as P

LEVELS = 2
FRONT = ("fa", "fb")
BF16 = jnp.bfloat16
F32 = jnp.float32


def mm(spec, a, b):
    return jnp.einsum(spec, a, b, preferred_element_type=F32)


def from_behind(block, distance):
    count = lax.axis_size("leaf")
    return lax.ppermute(block, "leaf", [((i - distance) % count, i) for i in range(count)])


def exchange(parts, axis):
    return lax.all_to_all(parts, axis, split_axis=0, concat_axis=0, tiled=True)


def to_all(block, axis):
    count = 1
    for name in (axis,) if isinstance(axis, str) else axis:
        count *= lax.axis_size(name)
    return exchange(jnp.broadcast_to(block, (count, *block.shape)), axis)


def total(parts):
    return jnp.sum(parts.astype(F32), axis=0)


def after(block, earlier):
    corner = earlier[(0,) * (earlier.ndim - 1) + (slice(0, 1),)]
    return block + (corner * 0).astype(block.dtype)


def added(first, second):
    return (first.astype(F32) + second.astype(F32)).astype(BF16)


def folded(block):
    half = block.shape[0] // 2
    return jnp.concatenate([block[:half], block[half:]], axis=1)


def unfolded(blocks):
    half = blocks.shape[-1] // 2
    return jnp.concatenate([blocks[..., :half], blocks[..., half:]], axis=-2)


def per_device(
    leaf_pivot_block,
    leaf_rest_block,
    node_pivot_block,
    node_rest_block,
    leaf_vectors_pivot,
    leaf_vectors_rest,
    node_vectors_pivot,
    node_vectors_rest,
    stack_place,
    parent_columns,
    coupling,
    pivot_inverse,
):
    na, nb = lax.axis_size("fa"), lax.axis_size("fb")
    fronts = na * nb
    ia, ib = lax.axis_index("fa"), lax.axis_index("fb")
    me = ia * nb + ib
    kp = leaf_vectors_pivot.shape[2]
    kc = leaf_vectors_rest.shape[2]
    ks = kp + kc
    K, C = kp * fronts, kc * fronts
    R = leaf_pivot_block.shape[2]
    rc = R // fronts
    place = stack_place[0]
    subtree = 2**LEVELS

    def stack_rows(device):
        device = jnp.asarray(device, jnp.int32)
        return jnp.concatenate(
            [
                device * kp + jnp.arange(kp, dtype=jnp.int32),
                K + device * kc + jnp.arange(kc, dtype=jnp.int32),
            ]
        )

    node_w = jnp.concatenate([node_vectors_pivot[0, 1], node_vectors_rest[0, 1]], axis=0)
    node_v = jnp.concatenate([node_vectors_pivot[0, 0], node_vectors_rest[0, 0]], axis=0)
    rows = stack_rows(me)

    own_hit = rows[:, None] == place[None]
    own = jnp.concatenate([node_pivot_block[0], node_rest_block[0]], axis=0)
    own = jnp.where(jnp.any(own_hit, axis=1)[:, None], jnp.zeros_like(own), own)

    blocks = jnp.concatenate([node_w, node_v], axis=0).reshape(2 * ks, nb, K // nb).transpose(1, 0, 2)
    own_folded = folded(own)
    blocks = jnp.concatenate([blocks, jnp.broadcast_to(own_folded, (nb, *own_folded.shape))], axis=1)
    blocks = exchange(blocks, "fb")
    w_block = blocks[:, :ks].reshape(nb * ks, K // nb)
    v_block = blocks[:, ks : 2 * ks].reshape(nb * ks, K // nb)
    own_block = unfolded(blocks[:, 2 * ks :]).reshape(nb * ks, R)

    ve_block = to_all(blocks[:, ks + kp : 2 * ks], "fa").reshape(C, K // nb)
    product = mm("sk,ck->sc", w_block, ve_block).astype(BF16).reshape(nb, ks, C)
    product = total(exchange(product, "fb"))
    unit = (rows[:, None] == K + jnp.arange(C, dtype=jnp.int32)[None]).astype(F32)
    section_rows = (unit - product).astype(BF16)

    leaf_ve = jnp.concatenate(jnp.split(leaf_vectors_rest[0, 0], K // C, axis=1), axis=0)
    gathered = lax.all_gather(jnp.concatenate([section_rows, leaf_ve], axis=0), FRONT, axis=0)
    section_all = gathered[:, :ks].reshape(fronts * ks, C)
    leaf_ve_all = gathered[:, ks:].reshape(fronts, K // C, kc, C)

    leaf_partial = mm("ik,ir->rk", leaf_vectors_pivot[0, 1], leaf_pivot_block[0])
    leaf_partial = leaf_partial + mm("ik,ir->rk", leaf_vectors_rest[0, 1], leaf_rest_block[0])
    part = after(leaf_partial, product).astype(BF16).reshape(nb, R // nb, K)
    part = total(exchange(part, "fb")).astype(BF16)
    leaf_y = total(exchange(part.reshape(na, rc, K), "fa")).astype(BF16)
    both = jnp.concatenate([leaf_rest_block[0], own], axis=0).T.reshape(nb, na, rc, kc + ks)
    both = both.transpose(1, 0, 2, 3).reshape(fronts, rc, kc + ks)
    both = exchange(both, FRONT)
    leaf_rest = both[:, :, :kc].transpose(1, 0, 2).reshape(rc, C)
    own_columns = both[:, :, kc:].transpose(1, 0, 2).reshape(rc, fronts * ks)

    inverse_block = pivot_inverse[0, 1].reshape(kp, na, nb, kp).transpose(2, 0, 1, 3)
    inverse_block = exchange(inverse_block.reshape(nb, kp, na * kp), "fb")
    inverse_block = inverse_block.reshape(nb * kp, na * kp)
    block_rows = jnp.concatenate([stack_rows(ia * nb + b) for b in range(nb)])
    block_hit = (place[:C, None] == block_rows[None]).astype(BF16)
    w_left = mm("cs,sk->ck", block_hit, w_block).astype(BF16)
    y_own = mm("sr,sk->rk", own_block, w_block)

    rest = mm("rbk,dbck->rdc", leaf_y.reshape(rc, K // C, C), leaf_ve_all).reshape(rc, C)
    rest = (after(leaf_rest, inverse_block) - rest).astype(BF16)

    y_folded = jnp.concatenate(jnp.split(leaf_y, K // C, axis=1), axis=0)
    wide = jnp.concatenate([coupling[0, 1], coupling[0, 0], y_folded], axis=0)
    gathered = lax.all_gather(after(wide, inverse_block), FRONT, axis=0)
    node_coupling_all = gathered[:, :kp].reshape(K, C)
    leaf_coupling_all = gathered[:, kp : 2 * kp].reshape(K, C)
    leaf_y_all = gathered[:, 2 * kp :].reshape(na, nb, K // C, rc, C).transpose(1, 0, 3, 2, 4)
    leaf_y_all = leaf_y_all.reshape(R, K)
    node_reach = mm("pm,mc->pc", pivot_inverse[0, 1], node_coupling_all).astype(BF16)
    leaf_reach = mm("pm,mc->pc", pivot_inverse[0, 0], leaf_coupling_all).astype(BF16)
    leaf_pivots = leaf_pivot_block[0] - mm("pk,rk->pr", leaf_vectors_pivot[0, 0], leaf_y_all)
    device = jnp.where(place < K, place // kp, (place - K) // kc)
    within = jnp.where(place < K, place % kp, kp + (place - K) % kc)
    section_map = jnp.take(section_all, device * ks + within, axis=0)
    section_own = mm("rs,sc->rc", own_columns, section_all)

    def section(left, right):
        children = jnp.concatenate([left, right], axis=1)
        return (section_own + mm("rj,jc->rc", children, section_map)).astype(BF16)

    rest = section(from_behind(rest, 1), rest)
    rest = section(from_behind(rest, 1), from_behind(rest, -1))
    left = to_all(from_behind(rest, -(subtree // 2)), FRONT)
    left = left.reshape(na, nb, rc, C).transpose(1, 0, 2, 3).reshape(R, C)

    partial_y = (y_own + mm("rc,ck->rk", left, w_left)).astype(BF16)
    part = total(exchange(partial_y.reshape(na, R // na, K // nb), "fa")).astype(BF16)
    y_block = to_all(part, "fa").reshape(R, K // nb)
    part = mm("sk,rk->sr", v_block, y_block).astype(BF16).reshape(nb, ks, R)
    placed = mm("sc,rc->sr", own_hit[:, :C].astype(BF16), left)
    reflected = own.astype(F32) + placed - total(exchange(part, "fb"))
    reflected = reflected.astype(BF16)
    remainder = reflected[kp:]
    pivots = to_all(reflected[:kp], "fa").reshape(na * kp, R)
    part = mm("mr,pm->rp", pivots, inverse_block).astype(BF16)
    part = total(exchange(part.reshape(nb, R // nb, nb * kp), "fb")).astype(BF16)
    part = exchange(part.reshape(na, rc, nb * kp), "fa")
    top = part.transpose(1, 0, 2).reshape(rc, K)

    wide = jnp.concatenate([node_reach, leaf_reach, folded(leaf_pivots.astype(BF16))], axis=0)
    gathered = lax.all_gather(after(wide, y_block), FRONT, axis=0)
    node_reach_all = gathered[:, :kp].reshape(K, C)
    leaf_reach_all = gathered[:, kp : 2 * kp].reshape(K, C)
    leaf_pivots_all = unfolded(gathered[:, 2 * kp :]).reshape(K, R)
    leaf_own = mm("pm,mr->pr", pivot_inverse[0, 0], leaf_pivots_all)

    pivot_ids = jnp.arange(K, dtype=jnp.int32)[:, None]
    node_pick = (pivot_ids == parent_columns[0, 1][None]).astype(BF16)
    leaf_pick = (pivot_ids == parent_columns[0, 0][None]).astype(BF16)

    def reached(parent, pick, reach):
        chosen = mm("rp,pc->rc", parent, pick).astype(BF16)
        return mm("rc,pc->rp", chosen, reach)

    node = top
    for height in range(LEVELS, 0, -1):
        if height == LEVELS:
            parent = from_behind(node, subtree // 2)
        else:
            offset = 2 ** (height - 1)
            parent = added(from_behind(node, -offset), from_behind(node, offset))
        node = (top - reached(parent, node_pick, node_reach_all)).astype(BF16)
    parent = added(from_behind(node, -1), node)
    leaf = reached(parent, leaf_pick, leaf_reach_all).astype(BF16)
    both = jnp.stack([leaf, node]).reshape(2, rc, fronts, kp).transpose(2, 0, 1, 3)
    both = exchange(both, FRONT).reshape(na, nb, 2, rc, kp)
    both = both.transpose(2, 4, 1, 0, 3).reshape(2, kp, R)
    leaf = (leaf_own - both[0]).astype(BF16)
    return (jnp.stack([leaf, both[1]])[None], remainder[None])


def solution(mesh):
    leaves, fronts = mesh.devices.shape
    nb = next(n for n in range(max(1, int(fronts**0.5)), 0, -1) if fronts % n == 0)
    grid = Mesh(mesh.devices.reshape(leaves, fronts // nb, nb), ("leaf", "fa", "fb"))
    rows3 = P("leaf", FRONT, None)
    rows4 = P("leaf", None, FRONT, None)
    in_specs = (
        *([rows3] * 4),
        *([rows4] * 4),
        P("leaf", None),
        P("leaf", None, None),
        rows4,
        rows4,
    )
    return jax.shard_map(
        per_device, mesh=grid, in_specs=in_specs, out_specs=(rows4, rows3), check_vma=False
    )
```

time: 504 us -> 508 us (level)
  waiting for transfers between devices: 248 us -> 196 us
  blocking collectives: 106 us -> 144 us
  starting transfers between devices: 70.4 us -> 89 us
    all_gather x4 -> x3, waiting for transfers between devices: 87.7 us -> 18.2 us  [the longest x1 18.2 us: per_device(): gathered = lax.all_gather(after(wide, y_block), FRONT, axis=0)]
    all_to_all x5 -> x6, blocking collectives: 106 us -> 144 us  [exchange(): return lax.all_to_all(parts, axis, split_axis=0, concat_axis=0, tiled=True)]
    all_to_all x10 -> x9, starting transfers between devices: 44.6 us -> 59.3 us  [exchange(): return lax.all_to_all(parts, axis, split_axis=0, concat_axis=0, tiled=True)]
    all_to_all x10 -> x9, waiting for transfers between devices: 154 us -> 165 us  [exchange(): return lax.all_to_all(parts, axis, split_axis=0, concat_axis=0, tiled=True)]
    ppermute x8, waiting for transfers between devices: 6.73 us -> 12.7 us  [from_behind(): lax.ppermute(block, 'leaf', [((i - distance) % count, i) for i in range(c...]
    slice x10 -> x16, local copies, waits for them, and re-layouts: 8.85 us -> 13.4 us  [the longest x1 4.69 us: per_device(): leaf_reach_all = gathered[:, kp:2 * kp].reshape(K, C)]
    dot_general x20 -> x19, matrix products: 20.3 us -> 24.3 us  [mm(): return jnp.einsum(spec, a, b, preferred_element_type=F32)]
  transfers between devices with their start and end apart: 22 -> 20, of which waited for: 15 -> 14; matrix products, arithmetic and copies ran while one was open for 10% -> 7% of each run, Pallas kernels for 0% -> 0%
where the time goes in v2:
time: 508 us; the launch traced here: 506 us
  waiting for transfers between devices  196 us (39%)
  blocking collectives  144 us (28%)
  starting transfers between devices  89 us (18%)
  local copies, waits for them, and re-layouts  29.2 us (6%)
  matrix products  24.3 us (5%)
  between operations  16.6 us (3%)
  other arithmetic  7.16 us (1%)
    all_to_all x9, waiting for transfers between devices, exchange(): return lax.all_to_all(parts, axis, split_axis=0, concat_axis=0, tiled=True)  165 us
    all_to_all x6, blocking collectives, exchange(): return lax.all_to_all(parts, axis, split_axis=0, concat_axis=0, tiled=True)  144 us
    all_to_all x9, starting transfers between devices, exchange(): return lax.all_to_all(parts, axis, split_axis=0, concat_axis=0, tiled=True)  59.3 us
    ppermute x8, starting transfers between devices, from_behind(): lax.ppermute(block, 'leaf', [((i - distance) % count, i) for i in range(c...  29.7 us
    dot_general x19, matrix products, mm(): return jnp.einsum(spec, a, b, preferred_element_type=F32)  24.3 us
    all_gather x1, waiting for transfers between devices, per_device(): gathered = lax.all_gather(after(wide, y_block), FRONT, axis=0)  18.2 us
    ppermute x8, waiting for transfers between devices, from_behind(): lax.ppermute(block, 'leaf', [((i - distance) % count, i) for i in range(c...  12.7 us
  transfers between devices with their start and end apart: 20, of which 14 were waited for; matrix products, arithmetic and copies ran while one was open for 7% of the time, Pallas kernels for 0%

profile of v2, /device:TPU:24, one launch (start us, length us, event | category | flops | bytes accessed | tf_op | source)
XLA Modules:
  0.0 506.0 jit_solution(1107976348986805831)
XLA Ops:
  12.4 44.1 %all_to_all.75 = bf16[4,400,512]{2,1,0:T(8,128)(2,1)S(1)} all-to-all(bf16[4,400,512]{2,1,0:T(8,128)(2,1)S(1)} %pad_maximum_fusion), channel_id=1, replica_groups=mesh['leaf'=32,'fa'=4,'fb'=4] {'fb'}, dimensions={0} | all-to-all | bytes 3276800 | tf_op jit(solution)/shard_map/all_to_all | solution.py:23
  57.4 12.4 %all-to-all-start.1 = ((bf16[4,4,32,512]{3,2,1,0:T(8,128)(2,1)}), bf16[4,4,32,512]{3,2,1,0:T(8,128)(2,1)S(1)}, u32[]{:S(2)}, u32[]{:S(2)}) async-start(bf16[4,4,32,512]{3,2,1,0:T(8,128)(2,1)} %broadcast_in_dim.56), calls=%async_computation.1 | async-start | bytes 1048576 | tf_op jit(solution)/shard_map/all_to_all | solution.py:23
  70.8 26.2 %all-to-all-done.1 = bf16[4,4,32,512]{3,2,1,0:T(8,128)(2,1)S(1)} async-done(((bf16[4,4,32,512]{3,2,1,0:T(8,128)(2,1)}), bf16[4,4,32,512]{3,2,1,0:T(8,128)(2,1)S(1)}, u32[]{:S(2)}, u32[]{:S(2)}) %all-to-all-start.1) | async-done | bytes 524320 | tf_op jit(solution)/shard_map/all_to_all | solution.py:23
  98.4 7.0 %all-to-all-start.2 = ((bf16[4,160,512]{2,1,0:T(8,128)(2,1)}), bf16[4,160,512]{2,1,0:T(8,128)(2,1)S(1)}, u32[]{:S(2)}, u32[]{:S(2)}) async-start(bf16[4,160,512]{2,1,0:T(8,128)(2,1)} %bitcast.14), calls=%async_computation.2 | async-start | bytes 1310720 | tf_op jit(solution)/shard_map/all_to_all | solution.py:23
  105.4 14.3 %all-to-all-done.2 = bf16[4,160,512]{2,1,0:T(8,128)(2,1)S(1)} async-done(((bf16[4,160,512]{2,1,0:T(8,128)(2,1)}), bf16[4,160,512]{2,1,0:T(8,128)(2,1)S(1)}, u32[]{:S(2)}, u32[]{:S(2)}) %all-to-all-start.2) | async-done | bytes 655392 | tf_op jit(solution)/shard_map/all_to_all | solution.py:23
  129.7 30.8 %all-to-all-done.3 = bf16[4,64,2048]{2,1,0:T(8,128)(2,1)S(1)} async-done(((bf16[4,64,2048]{2,1,0:T(8,128)(2,1)}), bf16[4,64,2048]{2,1,0:T(8,128)(2,1)S(1)}, u32[]{:S(2)}, u32[]{:S(2)}) %all-to-all-start.3) | async-done | bytes 1048608 | tf_op jit(solution)/shard_map/all_to_all | solution.py:23
  164.9 17.7 %all-to-all-done.5 = bf16[4,128,512]{1,2,0:T(8,128)(2,1)S(1)} async-done(((bf16[4,128,512]{1,2,0:T(8,128)(2,1)}), bf16[4,128,512]{1,2,0:T(8,128)(2,1)S(1)}, u32[]{:S(2)}, u32[]{:S(2)}) %all-to-all-start.5) | async-done | bytes 524320 | tf_op jit(solution)/shard_map/all_to_all | solution.py:23
  182.6 10.4 %all-to-all-start.4 = ((bf16[4,16,2048]{2,1,0:T(8,128)(2,1)}), bf16[4,16,2048]{2,1,0:T(8,128)(2,1)S(1)}, u32[]{:S(2)}, u32[]{:S(2)}) async-start(bf16[4,16,2048]{2,1,0:T(8,128)(2,1)} %bitcast.17), calls=%async_computation.4 | async-start | bytes 524288 | tf_op jit(solution)/shard_map/all_to_all | solution.py:23
  194.5 19.5 %all-to-all-done.4 = bf16[4,16,2048]{2,1,0:T(8,128)(2,1)S(1)} async-done(((bf16[4,16,2048]{2,1,0:T(8,128)(2,1)}), bf16[4,16,2048]{2,1,0:T(8,128)(2,1)S(1)}, u32[]{:S(2)}, u32[]{:S(2)}) %all-to-all-start.4) | async-done | bytes 262176 | tf_op jit(solution)/shard_map/all_to_all | solution.py:23
  220.2 13.0 %all-to-all-done.6 = bf16[16,16,192]{2,1,0:T(8,128)(2,1)S(1)} async-done(((bf16[16,16,192]{2,1,0:T(8,128)(2,1)}), bf16[16,16,192]{2,1,0:T(8,128)(2,1)S(1)}, u32[]{:S(2)}, u32[]{:S(2)}) %all-to-all-start.6) | async-done | bytes 98336 | tf_op jit(solution)/shard_map/all_to_all | solution.py:23
  245.8 5.7 %collective-permute-start.2 = (bf16[16,512]{1,0:T(8,128)(2,1)S(1)}, bf16[16,512]{1,0:T(8,128)(2,1)S(1)}, u32[]{:S(2)}, u32[]{:S(2)}) collective-permute-start(bf16[16,512]{1,0:T(8,128)(2,1)S(1)} %fusion.36), channel_id=1, source_target_pairs={{16,0},{32,16},{48,32},{64,48},{80,64},{96,80},{112,96},{128,112},... | collective-permute-start | bytes 49160 | tf_op jit(solution)/shard_map/ppermute | solution.py:19
  266.8 7.1 %all-to-all-start.7 = ((bf16[16,16,512]{2,1,0:T(8,128)(2,1)}), bf16[16,16,512]{2,1,0:T(8,128)(2,1)S(1)}, u32[]{:S(2)}, u32[]{:S(2)}) async-start(bf16[16,16,512]{2,1,0:T(8,128)(2,1)} %broadcast_in_dim.59), calls=%async_computation.7 | async-start | bytes 524288 | tf_op jit(solution)/shard_map/all_to_all | solution.py:23
  275.3 18.4 %all-to-all-done.7 = bf16[16,16,512]{2,1,0:T(8,128)(2,1)S(1)} async-done(((bf16[16,16,512]{2,1,0:T(8,128)(2,1)}), bf16[16,16,512]{2,1,0:T(8,128)(2,1)S(1)}, u32[]{:S(2)}, u32[]{:S(2)}) %all-to-all-start.7) | async-done | bytes 262176 | tf_op jit(solution)/shard_map/all_to_all | solution.py:23
  295.7 27.2 %all_to_all.76 = bf16[4,64,512]{2,1,0:T(8,128)(2,1)S(1)} all-to-all(bf16[4,64,512]{2,1,0:T(8,128)(2,1)S(1)} %bitcast.245), channel_id=1, replica_groups=mesh['leaf'=32,'fa'=4,'fb'=4] {'fa'}, dimensions={0} | all-to-all | bytes 524288 | tf_op jit(solution)/shard_map/all_to_all | solution.py:23
  323.0 21.9 %all_to_all.77 = bf16[4,64,512]{2,1,0:T(8,128)(2,1)S(1)} all-to-all(bf16[4,64,512]{2,1,0:T(8,128)(2,1)S(1)} %broadcast_in_dim.60), channel_id=1, replica_groups=mesh['leaf'=32,'fa'=4,'fb'=4] {'fa'}, dimensions={0} | all-to-all | bytes 524288 | tf_op jit(solution)/shard_map/all_to_all | solution.py:23
  353.3 11.9 %all_to_all.78 = bf16[4,160,256]{2,1,0:T(8,128)(2,1)S(1)} all-to-all(bf16[4,160,256]{2,1,0:T(8,128)(2,1)S(1)} %bitcast.229), channel_id=1, replica_groups=mesh['leaf'=32,'fa'=4,'fb'=4] {'fb'}, dimensions={0} | all-to-all | bytes 655360 | tf_op jit(solution)/shard_map/all_to_all | solution.py:23
  366.4 24.6 %all_to_all.79 = bf16[4,128,256]{2,1,0:T(8,128)(2,1)S(1)} all-to-all(bf16[4,128,256]{2,1,0:T(8,128)(2,1)S(1)} %broadcast_in_dim.61), channel_id=1, replica_groups=mesh['leaf'=32,'fa'=4,'fb'=4] {'fa'}, dimensions={0} | all-to-all | bytes 524288 | tf_op jit(solution)/shard_map/all_to_all | solution.py:23
  391.3 13.8 %all_to_all.80 = bf16[4,64,512]{2,1,0:T(8,128)(2,1)S(1)} all-to-all(bf16[4,64,512]{2,1,0:T(8,128)(2,1)S(1)} %bitcast.237), channel_id=1, replica_groups=mesh['leaf'=32,'fa'=4,'fb'=4] {'fb'}, dimensions={0} | all-to-all | bytes 524288 | tf_op jit(solution)/shard_map/all_to_all | solution.py:23
  409.1 13.5 %all-to-all-done.13 = bf16[4,16,512]{2,1,0:T(8,128)(2,1)S(1)} async-done(((bf16[4,16,512]{2,1,0:T(8,128)(2,1)}), bf16[4,16,512]{2,1,0:T(8,128)(2,1)S(1)}, u32[]{:S(2)}, u32[]{:S(2)}) %all-to-all-start.13) | async-done | bytes 65568 | tf_op jit(solution)/shard_map/all_to_all | solution.py:23
  427.0 18.2 %all-gather.7.cloned.1.call-done = bf16[16,320,512]{2,1,0:T(8,128)(2,1)} async-done(((bf16[1,320,512]{2,1,0:T(8,128)(2,1)}), bf16[16,320,512]{2,1,0:T(8,128)(2,1)}) %all-gather.7.cloned.1.call-update) | async-done | bytes 5242896 | tf_op jit(solution)/shard_map/all_gather | solution.py:180
  454.8 5.8 %collective-permute-start.5 = (bf16[16,2048]{1,0:T(8,128)(2,1)S(1)}, bf16[16,2048]{1,0:T(8,128)(2,1)S(1)}, u32[]{:S(2)}, u32[]{:S(2)}) collective-permute-start(bf16[16,2048]{1,0:T(8,128)(2,1)S(1)} %fusion.5), channel_id=1, source_target_pairs={{16,0},{32,16},{48,32},{64,48},{80,64},{96,80},{112,96},{128,112},... | collective-permute-start | bytes 196616 | tf_op jit(solution)/shard_map/ppermute | solution.py:19
  465.4 5.8 %collective-permute-start.7 = (bf16[16,2048]{1,0:T(8,128)(2,1)S(1)}, bf16[16,2048]{1,0:T(8,128)(2,1)S(1)}, u32[]{:S(2)}, u32[]{:S(2)}) collective-permute-start(bf16[16,2048]{1,0:T(8,128)(2,1)S(1)} %fusion.6), channel_id=1, source_target_pairs={{16,0},{32,16},{48,32},{64,48},{80,64},{96,80},{112,96},{128,112},... | collective-permute-start | bytes 196616 | tf_op jit(solution)/shard_map/ppermute | solution.py:19
  476.8 7.5 %all-to-all-start.14 = ((bf16[16,2,16,128]{3,2,1,0:T(8,128)(2,1)}), bf16[16,2,16,128]{3,2,1,0:T(8,128)(2,1)S(1)}, u32[]{:S(2)}, u32[]{:S(2)}) async-start(bf16[16,2,16,128]{3,2,1,0:T(8,128)(2,1)} %maximum_bitcast_fusion.1), calls=%async_computation.14 | async-start | bytes 262144 | tf_op jit(solution)/shard_map/all_to_all | solution.py:23
  486.3 11.8 %all-to-all-done.14 = bf16[16,2,16,128]{3,2,1,0:T(8,128)(2,1)S(1)} async-done(((bf16[16,2,16,128]{3,2,1,0:T(8,128)(2,1)}), bf16[16,2,16,128]{3,2,1,0:T(8,128)(2,1)S(1)}, u32[]{:S(2)}, u32[]{:S(2)}) %all-to-all-start.14) | async-done | bytes 131104 | tf_op jit(solution)/shard_map/all_to_all | solution.py:23
  (176 shorter events, 100.7 us)
Async XLA Ops:
  57.4 39.6 %all-to-all-start.1 = ((bf16[4,4,32,512]{3,2,1,0:T(8,128)(2,1)}), bf16[4,4,32,512]{3,2,1,0:T(8,128)(2,1)S(1)}, u32[]{:S(2)}, u32[]{:S(2)}) async-start(bf16[4,4,32,512]{3,2,1,0:T(8,128)(2,1)} %broadcast_in_dim.56), calls=%async_computation.1 | async-start | bytes 1048576 | tf_op jit(solution)/shard_map/all_to_all | solution.py:23
  70.8 48.9 %copy-start.7 = (bf16[4,160,512]{2,1,0:T(8,128)(2,1)}, bf16[4,160,512]{2,1,0:T(8,128)(2,1)S(1)}, u32[]{:S(2)}) copy-start(bf16[4,160,512]{2,1,0:T(8,128)(2,1)S(1)} %get-tuple-element.19) | copy-start | bytes 1966084
  70.8 34.6 %copy-start.9 = (bf16[1,2,32,2048]{3,2,1,0:T(8,128)(2,1)S(1)}, bf16[1,2,32,2048]{3,2,1,0:T(8,128)(2,1)}, u32[]{:S(2)}) copy-start(bf16[1,2,32,2048]{3,2,1,0:T(8,128)(2,1)} %param.17) | copy-start | bytes 786436
  98.4 21.4 %all-to-all-start.2 = ((bf16[4,160,512]{2,1,0:T(8,128)(2,1)}), bf16[4,160,512]{2,1,0:T(8,128)(2,1)S(1)}, u32[]{:S(2)}, u32[]{:S(2)}) async-start(bf16[4,160,512]{2,1,0:T(8,128)(2,1)} %bitcast.14), calls=%async_computation.2 | async-start | bytes 1310720 | tf_op jit(solution)/shard_map/all_to_all | solution.py:23
  105.4 128.0 %all-gather.9.cloned.1.call-start = ((), (), s32[]{:S(2)}) async-start(), calls=%async_computation.17 | async-start | bytes 5013504 | tf_op jit(solution)/shard_map/all_gather | solution.py:115
  124.9 35.6 %all-to-all-start.3 = ((bf16[4,64,2048]{2,1,0:T(8,128)(2,1)}), bf16[4,64,2048]{2,1,0:T(8,128)(2,1)S(1)}, u32[]{:S(2)}, u32[]{:S(2)}) async-start(bf16[4,64,2048]{2,1,0:T(8,128)(2,1)} %bitcast.16), calls=%async_computation.3 | async-start | bytes 2097152 | tf_op jit(solution)/shard_map/all_to_all | solution.py:23
  128.8 64.2 %copy-start.10 = (bf16[1,2,128,512]{3,2,1,0:T(8,128)(2,1)S(1)}, bf16[1,2,128,512]{3,2,1,0:T(8,128)(2,1)}, u32[]{:S(2)}) copy-start(bf16[1,2,128,512]{3,2,1,0:T(8,128)(2,1)} %param.22) | copy-start | bytes 786436
  160.6 22.1 %all-to-all-start.5 = ((bf16[4,128,512]{1,2,0:T(8,128)(2,1)}), bf16[4,128,512]{1,2,0:T(8,128)(2,1)S(1)}, u32[]{:S(2)}, u32[]{:S(2)}) async-start(bf16[4,128,512]{1,2,0:T(8,128)(2,1)} %bitcast.24), calls=%async_computation.5 | async-start | bytes 1048576 | tf_op jit(solution)/shard_map/all_to_all | solution.py:23
  182.6 31.3 %all-to-all-start.4 = ((bf16[4,16,2048]{2,1,0:T(8,128)(2,1)}), bf16[4,16,2048]{2,1,0:T(8,128)(2,1)S(1)}, u32[]{:S(2)}, u32[]{:S(2)}) async-start(bf16[4,16,2048]{2,1,0:T(8,128)(2,1)} %bitcast.17), calls=%async_computation.4 | async-start | bytes 524288 | tf_op jit(solution)/shard_map/all_to_all | solution.py:23
  193.0 153.0 %all-gather.5.cloned.1.call-start = ((), (), s32[]{:S(2)}) async-start(), calls=%async_computation.15 | async-start | bytes 5570560 | tf_op jit(solution)/shard_map/all_gather | solution.py:143
  215.6 17.6 %all-to-all-start.6 = ((bf16[16,16,192]{2,1,0:T(8,128)(2,1)}), bf16[16,16,192]{2,1,0:T(8,128)(2,1)S(1)}, u32[]{:S(2)}, u32[]{:S(2)}) async-start(bf16[16,16,192]{2,1,0:T(8,128)(2,1)} %bitcast.44), calls=%async_computation.6 | async-start | bytes 262144 | tf_op jit(solution)/shard_map/all_to_all | solution.py:23
  236.1 8.0 %collective-permute-start = (bf16[16,512]{1,0:T(8,128)(2,1)S(1)}, bf16[16,512]{1,0:T(8,128)(2,1)S(1)}, u32[]{:S(2)}, u32[]{:S(2)}) collective-permute-start(bf16[16,512]{1,0:T(8,128)(2,1)S(1)} %fusion.35), channel_id=1, source_target_pairs={{496,0},{0,16},{16,32},{32,48},{48,64},{64,80},{80,96},{96,112},{1... | collective-permute-start | bytes 49160 | tf_op jit(solution)/shard_map/ppermute | solution.py:19
  245.8 7.7 %collective-permute-start.2 = (bf16[16,512]{1,0:T(8,128)(2,1)S(1)}, bf16[16,512]{1,0:T(8,128)(2,1)S(1)}, u32[]{:S(2)}, u32[]{:S(2)}) collective-permute-start(bf16[16,512]{1,0:T(8,128)(2,1)S(1)} %fusion.36), channel_id=1, source_target_pairs={{16,0},{32,16},{48,32},{64,48},{80,64},{96,80},{112,96},{128,112},... | collective-permute-start | bytes 49160 | tf_op jit(solution)/shard_map/ppermute | solution.py:19
  251.5 7.2 %collective-permute-start.1 = (bf16[16,512]{1,0:T(8,128)(2,1)S(1)}, bf16[16,512]{1,0:T(8,128)(2,1)S(1)}, u32[]{:S(2)}, u32[]{:S(2)}) collective-permute-start(bf16[16,512]{1,0:T(8,128)(2,1)S(1)} %fusion.36), channel_id=1, source_target_pairs={{496,0},{0,16},{16,32},{32,48},{48,64},{64,80},{80,96},{96,112},{1... | collective-permute-start | bytes 49160 | tf_op jit(solution)/shard_map/ppermute | solution.py:19
  260.3 5.8 %collective-permute-start.3 = (bf16[16,512]{1,0:T(8,128)(2,1)S(1)}, bf16[16,512]{1,0:T(8,128)(2,1)S(1)}, u32[]{:S(2)}, u32[]{:S(2)}) collective-permute-start(bf16[16,512]{1,0:T(8,128)(2,1)S(1)} %fusion.37), channel_id=1, source_target_pairs={{32,0},{48,16},{64,32},{80,48},{96,64},{112,80},{128,96},{144,112}... | collective-permute-start | bytes 49160 | tf_op jit(solution)/shard_map/ppermute | solution.py:19
  266.8 27.0 %all-to-all-start.7 = ((bf16[16,16,512]{2,1,0:T(8,128)(2,1)}), bf16[16,16,512]{2,1,0:T(8,128)(2,1)S(1)}, u32[]{:S(2)}, u32[]{:S(2)}) async-start(bf16[16,16,512]{2,1,0:T(8,128)(2,1)} %broadcast_in_dim.59), calls=%async_computation.7 | async-start | bytes 524288 | tf_op jit(solution)/shard_map/all_to_all | solution.py:23
  273.9 171.4 %all-gather.7.cloned.1.call-start = ((), (), s32[]{:S(2)}) async-start(), calls=%async_computation.16 | async-start | bytes 5570560 | tf_op jit(solution)/shard_map/all_gather | solution.py:180
  365.2 43.9 %copy-start.15 = (s32[1,2,512]{2,1,0:T(2,128)S(1)}, s32[1,2,512]{2,1,0:T(2,128)}, u32[]{:S(2)}) copy-start(s32[1,2,512]{2,1,0:T(2,128)} %param.21) | copy-start | bytes 12292
  405.8 16.8 %all-to-all-start.13 = ((bf16[4,16,512]{2,1,0:T(8,128)(2,1)}), bf16[4,16,512]{2,1,0:T(8,128)(2,1)S(1)}, u32[]{:S(2)}, u32[]{:S(2)}) async-start(bf16[4,16,512]{2,1,0:T(8,128)(2,1)} %bitcast.70), calls=%async_computation.13 | async-start | bytes 131072 | tf_op jit(solution)/shard_map/all_to_all | solution.py:23
  422.6 27.3 %collective-permute-start.4 = (bf16[16,2048]{1,0:T(8,128)(2,1)S(1)}, bf16[16,2048]{1,0:T(8,128)(2,1)S(1)}, u32[]{:S(2)}, u32[]{:S(2)}) collective-permute-start(bf16[16,2048]{1,0:T(8,128)(2,1)S(1)} %bitcast.252), channel_id=1, source_target_pairs={{480,0},{496,16},{0,32},{16,48},{32,64},{48,80},{64,96},{80,112},{... | collective-permute-start | bytes 196616 | tf_op jit(solution)/shard_map/ppermute | solution.py:19
  452.9 7.7 %collective-permute-start.6 = (bf16[16,2048]{1,0:T(8,128)(2,1)S(1)}, bf16[16,2048]{1,0:T(8,128)(2,1)S(1)}, u32[]{:S(2)}, u32[]{:S(2)}) collective-permute-start(bf16[16,2048]{1,0:T(8,128)(2,1)S(1)} %fusion.5), channel_id=1, source_target_pairs={{496,0},{0,16},{16,32},{32,48},{48,64},{64,80},{80,96},{96,112},{1... | collective-permute-start | bytes 196616 | tf_op jit(solution)/shard_map/ppermute | solution.py:19
  454.8 7.6 %collective-permute-start.5 = (bf16[16,2048]{1,0:T(8,128)(2,1)S(1)}, bf16[16,2048]{1,0:T(8,128)(2,1)S(1)}, u32[]{:S(2)}, u32[]{:S(2)}) collective-permute-start(bf16[16,2048]{1,0:T(8,128)(2,1)S(1)} %fusion.5), channel_id=1, source_target_pairs={{16,0},{32,16},{48,32},{64,48},{80,64},{96,80},{112,96},{128,112},... | collective-permute-start | bytes 196616 | tf_op jit(solution)/shard_map/ppermute | solution.py:19
  465.4 7.7 %collective-permute-start.7 = (bf16[16,2048]{1,0:T(8,128)(2,1)S(1)}, bf16[16,2048]{1,0:T(8,128)(2,1)S(1)}, u32[]{:S(2)}, u32[]{:S(2)}) collective-permute-start(bf16[16,2048]{1,0:T(8,128)(2,1)S(1)} %fusion.6), channel_id=1, source_target_pairs={{16,0},{32,16},{48,32},{64,48},{80,64},{96,80},{112,96},{128,112},... | collective-permute-start | bytes 196616 | tf_op jit(solution)/shard_map/ppermute | solution.py:19
  476.8 21.4 %all-to-all-start.14 = ((bf16[16,2,16,128]{3,2,1,0:T(8,128)(2,1)}), bf16[16,2,16,128]{3,2,1,0:T(8,128)(2,1)S(1)}, u32[]{:S(2)}, u32[]{:S(2)}) async-start(bf16[16,2,16,128]{3,2,1,0:T(8,128)(2,1)} %maximum_bitcast_fusion.1), calls=%async_computation.14 | async-start | bytes 262144 | tf_op jit(solution)/shard_map/all_to_all | solution.py:23
  (14 other events, 148.8 us)
Sparse Core Ops, SparseCore 0:
  120.9 110.7 all-gather.8
  233.7 108.5 all-gather.4
  353.1 92.1 all-gather.6

commit v3 on v2

--- a/solution.py
+++ b/solution.py
@@ -97,35 +97,41 @@
     own = jnp.concatenate([node_pivot_block[0], node_rest_block[0]], axis=0)
     own = jnp.where(jnp.any(own_hit, axis=1)[:, None], jnp.zeros_like(own), own)
 
+    node_ve_all = lax.all_gather(node_vectors_rest[0, 0], FRONT, axis=0, tiled=True)
+
+    leaf_partial = mm("ik,ir->kr", leaf_vectors_pivot[0, 1], leaf_pivot_block[0])
+    leaf_partial = leaf_partial + mm("ik,ir->kr", leaf_vectors_rest[0, 1], leaf_rest_block[0])
+    part = exchange(leaf_partial.astype(BF16).reshape(nb, K // nb, R), "fb")
+    part = exchange(total(part).astype(BF16).reshape(na, kp, R), "fa")
+    leaf_y = total(part).astype(BF16)
+
+    both = jnp.concatenate([leaf_rest_block[0], own], axis=0).T.reshape(nb, na, rc, kc + ks)
+    leaf_ve = leaf_vectors_rest[0, 0].reshape(kc // rc, rc, nb, na, kp).transpose(2, 3, 1, 0, 4)
+    leaf_ve = leaf_ve.reshape(nb, na, rc, kc // rc * kp)
+    both = jnp.concatenate([both, leaf_ve], axis=3).transpose(1, 0, 2, 3)
+    both = exchange(both.reshape(fronts, rc, both.shape[3]), FRONT)
+    leaf_rest = both[:, :, :kc].transpose(1, 0, 2).reshape(rc, C)
+    own_columns = both[:, :, kc : kc + ks].transpose(1, 0, 2).reshape(rc, fronts * ks)
+    leaf_ve = both[:, :, kc + ks :].reshape(fronts, rc, kc // rc, kp).transpose(0, 2, 1, 3).reshape(C, kp)
+    part = mm("kr,ck->rc", leaf_y, leaf_ve).astype(BF16)
+    part = part.reshape(nb, na, rc, C).transpose(1, 0, 2, 3).reshape(fronts, rc, C)
+    rest = (leaf_rest - total(exchange(part, FRONT))).astype(BF16)
+
+    product = mm("sk,ck->sc", node_w, node_ve_all)
+    unit = (rows[:, None] == K + jnp.arange(C, dtype=jnp.int32)[None]).astype(F32)
+    section_rows = (after(unit, leaf_y) - product).astype(BF16)
+
+    gathered = lax.all_gather(jnp.concatenate([section_rows, coupling[0, 1]], axis=0), FRONT, axis=0)
+    section_all = gathered[:, :ks].reshape(fronts * ks, C)
+    node_coupling_all = gathered[:, ks:].reshape(K, C)
+
     blocks = jnp.concatenate([node_w, node_v], axis=0).reshape(2 * ks, nb, K // nb).transpose(1, 0, 2)
     own_folded = folded(own)
     blocks = jnp.concatenate([blocks, jnp.broadcast_to(own_folded, (nb, *own_folded.shape))], axis=1)
-    blocks = exchange(blocks, "fb")
+    blocks = exchange(after(blocks, rest), "fb")
     w_block = blocks[:, :ks].reshape(nb * ks, K // nb)
     v_block = blocks[:, ks : 2 * ks].reshape(nb * ks, K // nb)
     own_block = unfolded(blocks[:, 2 * ks :]).reshape(nb * ks, R)
-
-    ve_block = to_all(blocks[:, ks + kp : 2 * ks], "fa").reshape(C, K // nb)
-    product = mm("sk,ck->sc", w_block, ve_block).astype(BF16).reshape(nb, ks, C)
-    product = total(exchange(product, "fb"))
-    unit = (rows[:, None] == K + jnp.arange(C, dtype=jnp.int32)[None]).astype(F32)
-    section_rows = (unit - product).astype(BF16)
-
-    leaf_ve = jnp.concatenate(jnp.split(leaf_vectors_rest[0, 0], K // C, axis=1), axis=0)
-    gathered = lax.all_gather(jnp.concatenate([section_rows, leaf_ve], axis=0), FRONT, axis=0)
-    section_all = gathered[:, :ks].reshape(fronts * ks, C)
-    leaf_ve_all = gathered[:, ks:].reshape(fronts, K // C, kc, C)
-
-    leaf_partial = mm("ik,ir->rk", leaf_vectors_pivot[0, 1], leaf_pivot_block[0])
-    leaf_partial = leaf_partial + mm("ik,ir->rk", leaf_vectors_rest[0, 1], leaf_rest_block[0])
-    part = after(leaf_partial, product).astype(BF16).reshape(nb, R // nb, K)
-    part = total(exchange(part, "fb")).astype(BF16)
-    leaf_y = total(exchange(part.reshape(na, rc, K), "fa")).astype(BF16)
-    both = jnp.concatenate([leaf_rest_block[0], own], axis=0).T.reshape(nb, na, rc, kc + ks)
-    both = both.transpose(1, 0, 2, 3).reshape(fronts, rc, kc + ks)
-    both = exchange(both, FRONT)
-    leaf_rest = both[:, :, :kc].transpose(1, 0, 2).reshape(rc, C)
-    own_columns = both[:, :, kc:].transpose(1, 0, 2).reshape(rc, fronts * ks)
 
     inverse_block = pivot_inverse[0, 1].reshape(kp, na, nb, kp).transpose(2, 0, 1, 3)
     inverse_block = exchange(inverse_block.reshape(nb, kp, na * kp), "fb")
@@ -135,23 +141,18 @@
     w_left = mm("cs,sk->ck", block_hit, w_block).astype(BF16)
     y_own = mm("sr,sk->rk", own_block, w_block)
 
-    rest = mm("rbk,dbck->rdc", leaf_y.reshape(rc, K // C, C), leaf_ve_all).reshape(rc, C)
-    rest = (after(leaf_rest, inverse_block) - rest).astype(BF16)
-
-    y_folded = jnp.concatenate(jnp.split(leaf_y, K // C, axis=1), axis=0)
-    wide = jnp.concatenate([coupling[0, 1], coupling[0, 0], y_folded], axis=0)
-    gathered = lax.all_gather(after(wide, inverse_block), FRONT, axis=0)
-    node_coupling_all = gathered[:, :kp].reshape(K, C)
+    rest = after(rest, inverse_block)
+    node_reach = mm("pm,mc->pc", after(pivot_inverse[0, 1], rest), node_coupling_all).astype(BF16)
+    wide = jnp.concatenate([node_reach, coupling[0, 0], folded(leaf_y)], axis=0)
+    gathered = lax.all_gather(wide, FRONT, axis=0)
+    node_reach_all = gathered[:, :kp].reshape(K, C)
     leaf_coupling_all = gathered[:, kp : 2 * kp].reshape(K, C)
-    leaf_y_all = gathered[:, 2 * kp :].reshape(na, nb, K // C, rc, C).transpose(1, 0, 3, 2, 4)
-    leaf_y_all = leaf_y_all.reshape(R, K)
-    node_reach = mm("pm,mc->pc", pivot_inverse[0, 1], node_coupling_all).astype(BF16)
-    leaf_reach = mm("pm,mc->pc", pivot_inverse[0, 0], leaf_coupling_all).astype(BF16)
-    leaf_pivots = leaf_pivot_block[0] - mm("pk,rk->pr", leaf_vectors_pivot[0, 0], leaf_y_all)
+    leaf_y_all = unfolded(gathered[:, 2 * kp :]).reshape(na, nb, kp, R).transpose(1, 0, 2, 3).reshape(K, R)
+
     device = jnp.where(place < K, place // kp, (place - K) // kc)
     within = jnp.where(place < K, place % kp, kp + (place - K) % kc)
-    section_map = jnp.take(section_all, device * ks + within, axis=0)
-    section_own = mm("rs,sc->rc", own_columns, section_all)
+    section_map = jnp.take(section_all, after(device * ks + within, rest[0]), axis=0)
+    section_own = mm("rs,sc->rc", after(own_columns, rest), section_all)
 
     def section(left, right):
         children = jnp.concatenate([left, right], axis=1)
@@ -176,11 +177,12 @@
     part = exchange(part.reshape(na, rc, nb * kp), "fa")
     top = part.transpose(1, 0, 2).reshape(rc, K)
 
-    wide = jnp.concatenate([node_reach, leaf_reach, folded(leaf_pivots.astype(BF16))], axis=0)
+    leaf_reach = mm("pm,mc->pc", pivot_inverse[0, 0], leaf_coupling_all).astype(BF16)
+    leaf_pivots = leaf_pivot_block[0] - mm("pk,kr->pr", leaf_vectors_pivot[0, 0], leaf_y_all)
+    wide = jnp.concatenate([leaf_reach, folded(leaf_pivots.astype(BF16))], axis=0)
     gathered = lax.all_gather(after(wide, y_block), FRONT, axis=0)
-    node_reach_all = gathered[:, :kp].reshape(K, C)
-    leaf_reach_all = gathered[:, kp : 2 * kp].reshape(K, C)
-    leaf_pivots_all = unfolded(gathered[:, 2 * kp :]).reshape(K, R)
+    leaf_reach_all = gathered[:, :kp].reshape(K, C)
+    leaf_pivots_all = unfolded(gathered[:, kp:]).reshape(K, R)
     leaf_own = mm("pm,mr->pr", pivot_inverse[0, 0], leaf_pivots_all)
 
     pivot_ids = jnp.arange(K, dtype=jnp.int32)[:, None]

time: 508 us -> 480 us (0.945)
  blocking collectives: 144 us -> 112 us
  starting transfers between devices: 89 us -> 83.1 us
    all_gather x2 -> x3, waiting for transfers between devices: 0.04 us -> 46.7 us  [the longest x1 27 us: per_device(): lax.all_gather(jnp.concatenate([section_rows, coupling[0, 1]], axis=0), F...]
    all_to_all x6, blocking collectives: 144 us -> 112 us  [exchange(): return lax.all_to_all(parts, axis, split_axis=0, concat_axis=0, tiled=True)]
    all_to_all x9 -> x8, waiting for transfers between devices: 165 us -> 137 us  [exchange(): return lax.all_to_all(parts, axis, split_axis=0, concat_axis=0, tiled=True)]
    all_gather x1, waiting for transfers between devices: 18.2 us -> 0.02 us  [per_device(): gathered = lax.all_gather(after(wide, y_block), FRONT, axis=0)]
    all_to_all x9 -> x8, starting transfers between devices: 59.3 us -> 54.8 us  [exchange(): return lax.all_to_all(parts, axis, split_axis=0, concat_axis=0, tiled=True)]
  transfers between devices with their start and end apart: 20 -> 20, of which waited for: 14 -> 14; matrix products, arithmetic and copies ran while one was open for 7% -> 9% of each run, Pallas kernels for 0% -> 0%
where the time goes in v3:
time: 480 us; the launch traced here: 474 us
  waiting for transfers between devices  198 us (41%)
  blocking collectives  112 us (23%)
  starting transfers between devices  83.1 us (17%)
  local copies, waits for them, and re-layouts  33 us (7%)
  matrix products  22.5 us (5%)
  between operations  18 us (4%)
  other arithmetic  7.79 us (2%)
    all_to_all x8, waiting for transfers between devices, exchange(): return lax.all_to_all(parts, axis, split_axis=0, concat_axis=0, tiled=True)  137 us
    all_to_all x6, blocking collectives, exchange(): return lax.all_to_all(parts, axis, split_axis=0, concat_axis=0, tiled=True)  112 us
    all_to_all x8, starting transfers between devices, exchange(): return lax.all_to_all(parts, axis, split_axis=0, concat_axis=0, tiled=True)  54.8 us
    ppermute x8, starting transfers between devices, from_behind(): lax.ppermute(block, 'leaf', [((i - distance) % count, i) for i in range(c...  28.2 us
    all_gather x1, waiting for transfers between devices, per_device(): lax.all_gather(jnp.concatenate([section_rows, coupling[0, 1]], axis=0), F...  27 us
    dot_general x19, matrix products, mm(): return jnp.einsum(spec, a, b, preferred_element_type=F32)  22.5 us
    all_gather x1, waiting for transfers between devices, per_device(): lax.all_gather(node_vectors_rest[0, 0], FRONT, axis=0, tiled=True)  19.7 us
    ppermute x8, waiting for transfers between devices, from_behind(): lax.ppermute(block, 'leaf', [((i - distance) % count, i) for i in range(c...  14.1 us
  transfers between devices with their start and end apart: 20, of which 14 were waited for; matrix products, arithmetic and copies ran while one was open for 9% of the time, Pallas kernels for 0%

profile of v3, /device:TPU:24, one launch (start us, length us, event | category | flops | bytes accessed | tf_op | source)
XLA Modules:
  0.0 474.3 jit_solution(8745666717476803848)
XLA Ops:
  10.2 5.9 %all-to-all-start.1 = ((bf16[4,512,256]{2,1,0:T(8,128)(2,1)}), bf16[4,512,256]{2,1,0:T(8,128)(2,1)S(1)}, u32[]{:S(2)}, u32[]{:S(2)}) async-start(bf16[4,512,256]{2,1,0:T(8,128)(2,1)} %bitcast.13), calls=%async_computation.1 | async-start | bytes 2097152 | tf_op jit(solution)/shard_map/all_to_all | solution.py:23
  16.8 26.4 %all-to-all-done.1 = bf16[4,512,256]{2,1,0:T(8,128)(2,1)S(1)} async-done(((bf16[4,512,256]{2,1,0:T(8,128)(2,1)}), bf16[4,512,256]{2,1,0:T(8,128)(2,1)S(1)}, u32[]{:S(2)}, u32[]{:S(2)}) %all-to-all-start.1) | async-done | bytes 1048608 | tf_op jit(solution)/shard_map/all_to_all | solution.py:23
  44.2 14.7 %all-to-all-start.2 = ((bf16[4,128,256]{2,1,0:T(8,128)(2,1)}), bf16[4,128,256]{2,1,0:T(8,128)(2,1)S(1)}, u32[]{:S(2)}, u32[]{:S(2)}) async-start(bf16[4,128,256]{2,1,0:T(8,128)(2,1)} %bitcast.14), calls=%async_computation.2 | async-start | bytes 524288 | tf_op jit(solution)/shard_map/all_to_all | solution.py:23
  61.4 18.7 %all-to-all-done.2 = bf16[4,128,256]{2,1,0:T(8,128)(2,1)S(1)} async-done(((bf16[4,128,256]{2,1,0:T(8,128)(2,1)}), bf16[4,128,256]{2,1,0:T(8,128)(2,1)S(1)}, u32[]{:S(2)}, u32[]{:S(2)}) %all-to-all-start.2) | async-done | bytes 262176 | tf_op jit(solution)/shard_map/all_to_all | solution.py:23
  81.4 19.7 %all-gather.10.cloned.1.call-done = bf16[1,1,512,2048]{3,2,1,0:T(8,128)(2,1)} async-done(((bf16[1,1,32,2048]{3,2,1,0:T(8,128)(2,1)}), bf16[1,1,512,2048]{3,2,1,0:T(8,128)(2,1)}) %all-gather.10.cloned.1.call-update) | async-done | bytes 2097168 | tf_op jit(solution)/shard_map/all_gather | solution.py:100
  106.6 7.8 %all-to-all-start = ((bf16[16,16,448]{2,1,0:T(8,128)(2,1)}), bf16[16,16,448]{2,1,0:T(8,128)(2,1)S(1)}, u32[]{:S(2)}, u32[]{:S(2)}) async-start(bf16[16,16,448]{2,1,0:T(8,128)(2,1)} %bitcast.8), calls=%async_computation | async-start | bytes 524288 | tf_op jit(solution)/shard_map/all_to_all | solution.py:23
  115.9 12.4 %all-to-all-done = bf16[16,16,448]{2,1,0:T(8,128)(2,1)S(1)} async-done(((bf16[16,16,448]{2,1,0:T(8,128)(2,1)}), bf16[16,16,448]{2,1,0:T(8,128)(2,1)S(1)}, u32[]{:S(2)}, u32[]{:S(2)}) %all-to-all-start) | async-done | bytes 229408 | tf_op jit(solution)/shard_map/all_to_all | solution.py:23
  128.3 6.5 %all-to-all-start.4 = ((bf16[4,128,512]{2,1,0:T(8,128)(2,1)}), bf16[4,128,512]{2,1,0:T(8,128)(2,1)S(1)}, u32[]{:S(2)}, u32[]{:S(2)}) async-start(bf16[4,128,512]{2,1,0:T(8,128)(2,1)} %reshape.409), calls=%async_computation.4 | async-start | bytes 1048576 | tf_op jit(solution)/shard_map/all_to_all | solution.py:23
  135.9 15.1 %all-to-all-done.4 = bf16[4,128,512]{2,1,0:T(8,128)(2,1)S(1)} async-done(((bf16[4,128,512]{2,1,0:T(8,128)(2,1)}), bf16[4,128,512]{2,1,0:T(8,128)(2,1)S(1)}, u32[]{:S(2)}, u32[]{:S(2)}) %all-to-all-start.4) | async-done | bytes 524320 | tf_op jit(solution)/shard_map/all_to_all | solution.py:23
  151.0 6.5 %all-to-all-start.3 = ((bf16[16,16,512]{2,1,0:T(8,128)(2,1)}), bf16[16,16,512]{2,1,0:T(8,128)(2,1)S(1)}, u32[]{:S(2)}, u32[]{:S(2)}) async-start(bf16[16,16,512]{2,1,0:T(8,128)(2,1)} %bitcast.19), calls=%async_computation.3 | async-start | bytes 524288 | tf_op jit(solution)/shard_map/all_to_all | solution.py:23
  159.0 15.7 %all-to-all-done.3 = bf16[16,16,512]{2,1,0:T(8,128)(2,1)S(1)} async-done(((bf16[16,16,512]{2,1,0:T(8,128)(2,1)}), bf16[16,16,512]{2,1,0:T(8,128)(2,1)S(1)}, u32[]{:S(2)}, u32[]{:S(2)}) %all-to-all-start.3) | async-done | bytes 262176 | tf_op jit(solution)/shard_map/all_to_all | solution.py:23
  175.9 27.0 %all-gather.12.cloned.1.call-done = bf16[4608,512]{1,0:T(8,128)(2,1)} async-done(((bf16[288,512]{1,0:T(8,128)(2,1)}), bf16[4608,512]{1,0:T(8,128)(2,1)}) %all-gather.12.cloned.1.call-update) | async-done | bytes 4718608 | tf_op jit(solution)/shard_map/all_gather | solution.py:124
  228.0 5.8 %collective-permute-start.2 = (bf16[16,512]{1,0:T(8,128)(2,1)S(1)}, bf16[16,512]{1,0:T(8,128)(2,1)S(1)}, u32[]{:S(2)}, u32[]{:S(2)}) collective-permute-start(bf16[16,512]{1,0:T(8,128)(2,1)S(1)} %fusion.40), channel_id=1, source_target_pairs={{16,0},{32,16},{48,32},{64,48},{80,64},{96,80},{112,96},{128,112},... | collective-permute-start | bytes 49160 | tf_op jit(solution)/shard_map/ppermute | solution.py:19
  244.4 21.8 %all-to-all-done.5 = bf16[4,400,512]{2,1,0:T(8,128)(2,1)} async-done(((bf16[4,400,512]{2,1,0:T(8,128)(2,1)}), bf16[4,400,512]{2,1,0:T(8,128)(2,1)}, u32[]{:S(2)}, u32[]{:S(2)}) %all-to-all-start.5) | async-done | bytes 1638432 | tf_op jit(solution)/shard_map/all_to_all | solution.py:23
  275.7 16.0 %all-to-all-done.6 = bf16[16,16,512]{2,1,0:T(8,128)(2,1)S(1)} async-done(((bf16[16,16,512]{2,1,0:T(8,128)(2,1)}), bf16[16,16,512]{2,1,0:T(8,128)(2,1)S(1)}, u32[]{:S(2)}, u32[]{:S(2)}) %all-to-all-start.6) | async-done | bytes 262176 | tf_op jit(solution)/shard_map/all_to_all | solution.py:23
  292.5 27.2 %all_to_all.70 = bf16[4,64,512]{2,1,0:T(8,128)(2,1)S(1)} all-to-all(bf16[4,64,512]{2,1,0:T(8,128)(2,1)S(1)} %bitcast.235), channel_id=1, replica_groups=mesh['leaf'=32,'fa'=4,'fb'=4] {'fa'}, dimensions={0} | all-to-all | bytes 524288 | tf_op jit(solution)/shard_map/all_to_all | solution.py:23
  319.8 19.5 %all_to_all.71 = bf16[4,64,512]{2,1,0:T(8,128)(2,1)S(1)} all-to-all(bf16[4,64,512]{2,1,0:T(8,128)(2,1)S(1)} %broadcast_in_dim.58), channel_id=1, replica_groups=mesh['leaf'=32,'fa'=4,'fb'=4] {'fa'}, dimensions={0} | all-to-all | bytes 524288 | tf_op jit(solution)/shard_map/all_to_all | solution.py:23
  348.9 12.5 %all_to_all.72 = bf16[4,160,256]{2,1,0:T(8,128)(2,1)S(1)} all-to-all(bf16[4,160,256]{2,1,0:T(8,128)(2,1)S(1)} %bitcast.219), channel_id=1, replica_groups=mesh['leaf'=32,'fa'=4,'fb'=4] {'fb'}, dimensions={0} | all-to-all | bytes 655360 | tf_op jit(solution)/shard_map/all_to_all | solution.py:23
  363.2 26.0 %all_to_all.73 = bf16[4,128,256]{2,1,0:T(8,128)(2,1)S(1)} all-to-all(bf16[4,128,256]{2,1,0:T(8,128)(2,1)S(1)} %broadcast_in_dim.59), channel_id=1, replica_groups=mesh['leaf'=32,'fa'=4,'fb'=4] {'fa'}, dimensions={0} | all-to-all | bytes 524288 | tf_op jit(solution)/shard_map/all_to_all | solution.py:23
  389.5 11.4 %all_to_all.74 = bf16[4,64,512]{2,1,0:T(8,128)(2,1)S(1)} all-to-all(bf16[4,64,512]{2,1,0:T(8,128)(2,1)S(1)} %bitcast.227), channel_id=1, replica_groups=mesh['leaf'=32,'fa'=4,'fb'=4] {'fb'}, dimensions={0} | all-to-all | bytes 524288 | tf_op jit(solution)/shard_map/all_to_all | solution.py:23
  400.9 15.8 %all_to_all.75 = bf16[4,16,512]{2,1,0:T(8,128)(2,1)S(1)} all-to-all(bf16[4,16,512]{2,1,0:T(8,128)(2,1)S(1)} %bitcast.234), channel_id=1, replica_groups=mesh['leaf'=32,'fa'=4,'fb'=4] {'fa'}, dimensions={0} | all-to-all | bytes 131072 | tf_op jit(solution)/shard_map/all_to_all | solution.py:23
  430.1 5.8 %collective-permute-start.5 = (bf16[16,2048]{1,0:T(8,128)(2,1)S(1)}, bf16[16,2048]{1,0:T(8,128)(2,1)S(1)}, u32[]{:S(2)}, u32[]{:S(2)}) collective-permute-start(bf16[16,2048]{1,0:T(8,128)(2,1)S(1)} %fusion.4), channel_id=1, source_target_pairs={{16,0},{32,16},{48,32},{64,48},{80,64},{96,80},{112,96},{128,112},... | collective-permute-start | bytes 196616 | tf_op jit(solution)/shard_map/ppermute | solution.py:19
  439.1 5.8 %collective-permute-start.7 = (bf16[16,2048]{1,0:T(8,128)(2,1)S(1)}, bf16[16,2048]{1,0:T(8,128)(2,1)S(1)}, u32[]{:S(2)}, u32[]{:S(2)}) collective-permute-start(bf16[16,2048]{1,0:T(8,128)(2,1)S(1)} %fusion.5), channel_id=1, source_target_pairs={{16,0},{32,16},{48,32},{64,48},{80,64},{96,80},{112,96},{128,112},... | collective-permute-start | bytes 196616 | tf_op jit(solution)/shard_map/ppermute | solution.py:19
  456.0 10.4 %all-to-all-done.13 = bf16[16,2,16,128]{3,2,1,0:T(8,128)(2,1)S(1)} async-done(((bf16[16,2,16,128]{3,2,1,0:T(8,128)(2,1)}), bf16[16,2,16,128]{3,2,1,0:T(8,128)(2,1)S(1)}, u32[]{:S(2)}, u32[]{:S(2)}) %all-to-all-start.13) | async-done | bytes 131104 | tf_op jit(solution)/shard_map/all_to_all | solution.py:23
  (181 shorter events, 102.1 us)
Async XLA Ops:
  10.2 33.0 %all-to-all-start.1 = ((bf16[4,512,256]{2,1,0:T(8,128)(2,1)}), bf16[4,512,256]{2,1,0:T(8,128)(2,1)S(1)}, u32[]{:S(2)}, u32[]{:S(2)}) async-start(bf16[4,512,256]{2,1,0:T(8,128)(2,1)} %bitcast.13), calls=%async_computation.1 | async-start | bytes 2097152 | tf_op jit(solution)/shard_map/all_to_all | solution.py:23
  16.1 84.9 %all-gather.10.cloned.1.call-start = ((), (), s32[]{:S(2)}) async-start(), calls=%async_computation.15 | async-start | bytes 2228224 | tf_op jit(solution)/shard_map/all_gather | solution.py:100
  44.2 36.0 %all-to-all-start.2 = ((bf16[4,128,256]{2,1,0:T(8,128)(2,1)}), bf16[4,128,256]{2,1,0:T(8,128)(2,1)S(1)}, u32[]{:S(2)}, u32[]{:S(2)}) async-start(bf16[4,128,256]{2,1,0:T(8,128)(2,1)} %bitcast.14), calls=%async_computation.2 | async-start | bytes 524288 | tf_op jit(solution)/shard_map/all_to_all | solution.py:23
  58.8 144.1 %all-gather.12.cloned.1.call-start = ((), (), s32[]{:S(2)}) async-start(), calls=%async_computation.16 | async-start | bytes 5013504 | tf_op jit(solution)/shard_map/all_gather | solution.py:124
  106.6 21.8 %all-to-all-start = ((bf16[16,16,448]{2,1,0:T(8,128)(2,1)}), bf16[16,16,448]{2,1,0:T(8,128)(2,1)S(1)}, u32[]{:S(2)}, u32[]{:S(2)}) async-start(bf16[16,16,448]{2,1,0:T(8,128)(2,1)} %bitcast.8), calls=%async_computation | async-start | bytes 524288 | tf_op jit(solution)/shard_map/all_to_all | solution.py:23
  128.3 22.7 %all-to-all-start.4 = ((bf16[4,128,512]{2,1,0:T(8,128)(2,1)}), bf16[4,128,512]{2,1,0:T(8,128)(2,1)S(1)}, u32[]{:S(2)}, u32[]{:S(2)}) async-start(bf16[4,128,512]{2,1,0:T(8,128)(2,1)} %reshape.409), calls=%async_computation.4 | async-start | bytes 1048576 | tf_op jit(solution)/shard_map/all_to_all | solution.py:23
  151.0 53.8 %copy-start.2 = (bf16[4,128,512]{2,1,0:T(8,128)(2,1)}, bf16[4,128,512]{2,1,0:T(8,128)(2,1)S(1)}, u32[]{:S(2)}) copy-start(bf16[4,128,512]{2,1,0:T(8,128)(2,1)S(1)} %all-to-all-done.4) | copy-start | bytes 1572868
  151.0 23.6 %all-to-all-start.3 = ((bf16[16,16,512]{2,1,0:T(8,128)(2,1)}), bf16[16,16,512]{2,1,0:T(8,128)(2,1)S(1)}, u32[]{:S(2)}, u32[]{:S(2)}) async-start(bf16[16,16,512]{2,1,0:T(8,128)(2,1)} %bitcast.19), calls=%async_computation.3 | async-start | bytes 524288 | tf_op jit(solution)/shard_map/all_to_all | solution.py:23
  157.5 182.9 %all-gather.14.cloned.1.call-start = ((), (), s32[]{:S(2)}) async-start(), calls=%async_computation.17 | async-start | bytes 5570560 | tf_op jit(solution)/shard_map/all_gather | solution.py:147
  210.4 55.8 %all-to-all-start.5 = ((bf16[4,400,512]{2,1,0:T(8,128)(2,1)}), bf16[4,400,512]{2,1,0:T(8,128)(2,1)}, u32[]{:S(2)}, u32[]{:S(2)}) async-start(bf16[4,400,512]{2,1,0:T(8,128)(2,1)} %maximum_add_fusion), calls=%async_computation.5 | async-start | bytes 3276800 | tf_op jit(solution)/shard_map/all_to_all | solution.py:23
  214.9 11.5 %collective-permute-start = (bf16[16,512]{1,0:T(8,128)(2,1)S(1)}, bf16[16,512]{1,0:T(8,128)(2,1)S(1)}, u32[]{:S(2)}, u32[]{:S(2)}) collective-permute-start(bf16[16,512]{1,0:T(8,128)(2,1)S(1)} %get-tuple-element.14), channel_id=1, source_target_pairs={{496,0},{0,16},{16,32},{32,48},{48,64},{64,80},{80,96},{96,112},{1... | collective-permute-start | bytes 49160 | tf_op jit(solution)/shard_map/ppermute | solution.py:19
  228.0 7.7 %collective-permute-start.2 = (bf16[16,512]{1,0:T(8,128)(2,1)S(1)}, bf16[16,512]{1,0:T(8,128)(2,1)S(1)}, u32[]{:S(2)}, u32[]{:S(2)}) collective-permute-start(bf16[16,512]{1,0:T(8,128)(2,1)S(1)} %fusion.40), channel_id=1, source_target_pairs={{16,0},{32,16},{48,32},{64,48},{80,64},{96,80},{112,96},{128,112},... | collective-permute-start | bytes 49160 | tf_op jit(solution)/shard_map/ppermute | solution.py:19
  233.7 7.2 %collective-permute-start.1 = (bf16[16,512]{1,0:T(8,128)(2,1)S(1)}, bf16[16,512]{1,0:T(8,128)(2,1)S(1)}, u32[]{:S(2)}, u32[]{:S(2)}) collective-permute-start(bf16[16,512]{1,0:T(8,128)(2,1)S(1)} %fusion.40), channel_id=1, source_target_pairs={{496,0},{0,16},{16,32},{32,48},{48,64},{64,80},{80,96},{96,112},{1... | collective-permute-start | bytes 49160 | tf_op jit(solution)/shard_map/ppermute | solution.py:19
  242.5 23.8 %collective-permute-start.3 = (bf16[16,512]{1,0:T(8,128)(2,1)S(1)}, bf16[16,512]{1,0:T(8,128)(2,1)S(1)}, u32[]{:S(2)}, u32[]{:S(2)}) collective-permute-start(bf16[16,512]{1,0:T(8,128)(2,1)S(1)} %fusion.41), channel_id=1, source_target_pairs={{32,0},{48,16},{64,32},{80,48},{96,64},{112,80},{128,96},{144,112}... | collective-permute-start | bytes 49160 | tf_op jit(solution)/shard_map/ppermute | solution.py:19
  267.0 24.7 %all-to-all-start.6 = ((bf16[16,16,512]{2,1,0:T(8,128)(2,1)}), bf16[16,16,512]{2,1,0:T(8,128)(2,1)S(1)}, u32[]{:S(2)}, u32[]{:S(2)}) async-start(bf16[16,16,512]{2,1,0:T(8,128)(2,1)} %broadcast_in_dim.57), calls=%async_computation.6 | async-start | bytes 524288 | tf_op jit(solution)/shard_map/all_to_all | solution.py:23
  271.5 173.4 %all-gather.8.cloned.1.call-start = ((), (), s32[]{:S(2)}) async-start(), calls=%async_computation.14 | async-start | bytes 3342336 | tf_op jit(solution)/shard_map/all_gather | solution.py:183
  348.5 40.6 %copy-start.3 = (bf16[4,128,512]{2,1,0:T(8,128)(2,1)S(1)}, bf16[4,128,512]{2,1,0:T(8,128)(2,1)}, u32[]{:S(2)}) copy-start(bf16[4,128,512]{2,1,0:T(8,128)(2,1)} %copy-done.2) | copy-start | bytes 1572868
  361.4 58.5 %copy-start.18 = (s32[1,2,512]{2,1,0:T(2,128)S(1)}, s32[1,2,512]{2,1,0:T(2,128)}, u32[]{:S(2)}) copy-start(s32[1,2,512]{2,1,0:T(2,128)} %param.21) | copy-start | bytes 12292
  389.5 48.2 %copy-start.4 = (bf16[16,128,512]{2,1,0:T(8,128)(2,1)S(1)}, bf16[16,128,512]{2,1,0:T(8,128)(2,1)}, u32[]{:S(2)}) copy-start(bf16[16,128,512]{2,1,0:T(8,128)(2,1)} %get-tuple-element.17) | copy-start | bytes 6291460
  416.7 8.5 %collective-permute-start.4 = (bf16[16,2048]{1,0:T(8,128)(2,1)S(1)}, bf16[16,2048]{1,0:T(8,128)(2,1)S(1)}, u32[]{:S(2)}, u32[]{:S(2)}) collective-permute-start(bf16[16,2048]{1,0:T(8,128)(2,1)S(1)} %bitcast.242), channel_id=1, source_target_pairs={{480,0},{496,16},{0,32},{16,48},{32,64},{48,80},{64,96},{80,112},{... | collective-permute-start | bytes 196616 | tf_op jit(solution)/shard_map/ppermute | solution.py:19
  428.1 7.7 %collective-permute-start.6 = (bf16[16,2048]{1,0:T(8,128)(2,1)S(1)}, bf16[16,2048]{1,0:T(8,128)(2,1)S(1)}, u32[]{:S(2)}, u32[]{:S(2)}) collective-permute-start(bf16[16,2048]{1,0:T(8,128)(2,1)S(1)} %fusion.4), channel_id=1, source_target_pairs={{496,0},{0,16},{16,32},{32,48},{48,64},{64,80},{80,96},{96,112},{1... | collective-permute-start | bytes 196616 | tf_op jit(solution)/shard_map/ppermute | solution.py:19
  430.1 7.6 %collective-permute-start.5 = (bf16[16,2048]{1,0:T(8,128)(2,1)S(1)}, bf16[16,2048]{1,0:T(8,128)(2,1)S(1)}, u32[]{:S(2)}, u32[]{:S(2)}) collective-permute-start(bf16[16,2048]{1,0:T(8,128)(2,1)S(1)} %fusion.4), channel_id=1, source_target_pairs={{16,0},{32,16},{48,32},{64,48},{80,64},{96,80},{112,96},{128,112},... | collective-permute-start | bytes 196616 | tf_op jit(solution)/shard_map/ppermute | solution.py:19
  439.1 7.7 %collective-permute-start.7 = (bf16[16,2048]{1,0:T(8,128)(2,1)S(1)}, bf16[16,2048]{1,0:T(8,128)(2,1)S(1)}, u32[]{:S(2)}, u32[]{:S(2)}) collective-permute-start(bf16[16,2048]{1,0:T(8,128)(2,1)S(1)} %fusion.5), channel_id=1, source_target_pairs={{16,0},{32,16},{48,32},{64,48},{80,64},{96,80},{112,96},{128,112},... | collective-permute-start | bytes 196616 | tf_op jit(solution)/shard_map/ppermute | solution.py:19
  448.8 17.5 %all-to-all-start.13 = ((bf16[16,2,16,128]{3,2,1,0:T(8,128)(2,1)}), bf16[16,2,16,128]{3,2,1,0:T(8,128)(2,1)S(1)}, u32[]{:S(2)}, u32[]{:S(2)}) async-start(bf16[16,2,16,128]{3,2,1,0:T(8,128)(2,1)} %maximum_bitcast_fusion.1), calls=%async_computation.13 | async-start | bytes 262144 | tf_op jit(solution)/shard_map/all_to_all | solution.py:23
  (18 other events, 67.8 us)
Sparse Core Ops, SparseCore 0:
  19.0 81.9 all-gather.9
  104.4 98.4 all-gather.11
  206.6 129.0 all-gather.13
  348.6 81.1 all-gather.7

commit v4 on v2

--- a/solution.py
+++ b/solution.py
@@ -76,7 +76,7 @@
     ks = kp + kc
     K, C = kp * fronts, kc * fronts
     R = leaf_pivot_block.shape[2]
-    rc = R // fronts
+    rc, rb = R // fronts, R // nb
     place = stack_place[0]
     subtree = 2**LEVELS
 
@@ -97,70 +97,75 @@
     own = jnp.concatenate([node_pivot_block[0], node_rest_block[0]], axis=0)
     own = jnp.where(jnp.any(own_hit, axis=1)[:, None], jnp.zeros_like(own), own)
 
+    wide = jnp.concatenate([node_vectors_rest[0, 0], leaf_vectors_rest[0, 0]], axis=0)
+    gathered = lax.all_gather(wide, FRONT, axis=0)
+    node_ve_all = gathered[:, :kc].reshape(C, K)
+    leaf_ve_all = gathered[:, kc:].reshape(C, K)
+
+    leaf_partial = mm("ir,ik->rk", leaf_pivot_block[0], leaf_vectors_pivot[0, 1])
+    leaf_partial = leaf_partial + mm("ir,ik->rk", leaf_rest_block[0], leaf_vectors_rest[0, 1])
+    leaf_part = total(exchange(leaf_partial.astype(BF16).reshape(nb, rb, K), "fb")).astype(BF16)
+    leaf_y = total(exchange(leaf_part.reshape(rb, na, K // na).transpose(1, 0, 2), "fa")).astype(BF16)
+
+    both = jnp.concatenate([leaf_rest_block[0], own], axis=0).T.reshape(nb, rb, kc + ks)
+    both = exchange(both, "fb")
+    leaf_rest = both[:, :, :kc].transpose(1, 0, 2).reshape(rb, nb * kc)
+    own_columns = both[:, :, kc:].transpose(1, 0, 2).reshape(rb, nb * ks)
+
     blocks = jnp.concatenate([node_w, node_v], axis=0).reshape(2 * ks, nb, K // nb).transpose(1, 0, 2)
     own_folded = folded(own)
     blocks = jnp.concatenate([blocks, jnp.broadcast_to(own_folded, (nb, *own_folded.shape))], axis=1)
-    blocks = exchange(blocks, "fb")
+    blocks = exchange(after(blocks, both), "fb")
     w_block = blocks[:, :ks].reshape(nb * ks, K // nb)
     v_block = blocks[:, ks : 2 * ks].reshape(nb * ks, K // nb)
     own_block = unfolded(blocks[:, 2 * ks :]).reshape(nb * ks, R)
 
-    ve_block = to_all(blocks[:, ks + kp : 2 * ks], "fa").reshape(C, K // nb)
-    product = mm("sk,ck->sc", w_block, ve_block).astype(BF16).reshape(nb, ks, C)
-    product = total(exchange(product, "fb"))
+    product = mm("sk,ck->sc", node_w, node_ve_all)
     unit = (rows[:, None] == K + jnp.arange(C, dtype=jnp.int32)[None]).astype(F32)
-    section_rows = (unit - product).astype(BF16)
-
-    leaf_ve = jnp.concatenate(jnp.split(leaf_vectors_rest[0, 0], K // C, axis=1), axis=0)
-    gathered = lax.all_gather(jnp.concatenate([section_rows, leaf_ve], axis=0), FRONT, axis=0)
-    section_all = gathered[:, :ks].reshape(fronts * ks, C)
-    leaf_ve_all = gathered[:, ks:].reshape(fronts, K // C, kc, C)
-
-    leaf_partial = mm("ik,ir->rk", leaf_vectors_pivot[0, 1], leaf_pivot_block[0])
-    leaf_partial = leaf_partial + mm("ik,ir->rk", leaf_vectors_rest[0, 1], leaf_rest_block[0])
-    part = after(leaf_partial, product).astype(BF16).reshape(nb, R // nb, K)
-    part = total(exchange(part, "fb")).astype(BF16)
-    leaf_y = total(exchange(part.reshape(na, rc, K), "fa")).astype(BF16)
-    both = jnp.concatenate([leaf_rest_block[0], own], axis=0).T.reshape(nb, na, rc, kc + ks)
-    both = both.transpose(1, 0, 2, 3).reshape(fronts, rc, kc + ks)
-    both = exchange(both, FRONT)
-    leaf_rest = both[:, :, :kc].transpose(1, 0, 2).reshape(rc, C)
-    own_columns = both[:, :, kc:].transpose(1, 0, 2).reshape(rc, fronts * ks)
-
-    inverse_block = pivot_inverse[0, 1].reshape(kp, na, nb, kp).transpose(2, 0, 1, 3)
-    inverse_block = exchange(inverse_block.reshape(nb, kp, na * kp), "fb")
-    inverse_block = inverse_block.reshape(nb * kp, na * kp)
+    section_rows = (after(after(unit, leaf_y), blocks) - product).astype(BF16)
+    section_block = to_all(section_rows, "fb").reshape(nb * ks, C)
     block_rows = jnp.concatenate([stack_rows(ia * nb + b) for b in range(nb)])
-    block_hit = (place[:C, None] == block_rows[None]).astype(BF16)
-    w_left = mm("cs,sk->ck", block_hit, w_block).astype(BF16)
-    y_own = mm("sr,sk->rk", own_block, w_block)
-
-    rest = mm("rbk,dbck->rdc", leaf_y.reshape(rc, K // C, C), leaf_ve_all).reshape(rc, C)
-    rest = (after(leaf_rest, inverse_block) - rest).astype(BF16)
-
-    y_folded = jnp.concatenate(jnp.split(leaf_y, K // C, axis=1), axis=0)
-    wide = jnp.concatenate([coupling[0, 1], coupling[0, 0], y_folded], axis=0)
-    gathered = lax.all_gather(after(wide, inverse_block), FRONT, axis=0)
+    block_hit = (place[:, None] == block_rows[None]).astype(BF16)
+
+    wide = jnp.concatenate([coupling[0, 1], coupling[0, 0], leaf_y], axis=0)
+    gathered = lax.all_gather(after(wide, section_rows), FRONT, axis=0)
     node_coupling_all = gathered[:, :kp].reshape(K, C)
     leaf_coupling_all = gathered[:, kp : 2 * kp].reshape(K, C)
-    leaf_y_all = gathered[:, 2 * kp :].reshape(na, nb, K // C, rc, C).transpose(1, 0, 3, 2, 4)
-    leaf_y_all = leaf_y_all.reshape(R, K)
-    node_reach = mm("pm,mc->pc", pivot_inverse[0, 1], node_coupling_all).astype(BF16)
-    leaf_reach = mm("pm,mc->pc", pivot_inverse[0, 0], leaf_coupling_all).astype(BF16)
-    leaf_pivots = leaf_pivot_block[0] - mm("pk,rk->pr", leaf_vectors_pivot[0, 0], leaf_y_all)
-    device = jnp.where(place < K, place // kp, (place - K) // kc)
-    within = jnp.where(place < K, place % kp, kp + (place - K) % kc)
-    section_map = jnp.take(section_all, device * ks + within, axis=0)
-    section_own = mm("rs,sc->rc", own_columns, section_all)
+    leaf_y_all = gathered[:, 2 * kp :].reshape(na, nb, rb, K // na).transpose(1, 2, 0, 3).reshape(R, K)
+
+    def summed(part):
+        return total(to_all(part.astype(BF16), "fa")).astype(BF16)
+
+    is_mine = jnp.arange(C, dtype=jnp.int32) // (nb * kc) == ia
+    part = jnp.where(is_mine[None], jnp.tile(leaf_rest.astype(F32), (1, na)), 0.0)
+    rest = summed(part - mm("rk,ck->rc", leaf_part, leaf_ve_all))
+    section_map = mm("js,sc->jc", block_hit, section_block).astype(BF16)
+    section_own = mm("rs,sc->rc", own_columns, section_block)
 
     def section(left, right):
         children = jnp.concatenate([left, right], axis=1)
-        return (section_own + mm("rj,jc->rc", children, section_map)).astype(BF16)
-
-    rest = section(from_behind(rest, 1), rest)
+        return summed(section_own + mm("rj,jc->rc", children, section_map))
+
+    inverse_block = pivot_inverse[0, 1].reshape(kp, na, nb, kp).transpose(2, 0, 1, 3)
+    inverse_block = after(inverse_block.reshape(nb, kp, na * kp), rest)
+    inverse_block = exchange(inverse_block, "fb").reshape(nb * kp, na * kp)
+
+    rest = section(after(from_behind(rest, 1), inverse_block), rest)
     rest = section(from_behind(rest, 1), from_behind(rest, -1))
-    left = to_all(from_behind(rest, -(subtree // 2)), FRONT)
-    left = left.reshape(na, nb, rc, C).transpose(1, 0, 2, 3).reshape(R, C)
+    w_left = mm("cs,sk->ck", block_hit[:C], w_block).astype(BF16)
+    y_own = mm("sr,sk->rk", own_block, w_block)
+    left = to_all(from_behind(rest, -(subtree // 2)), "fb").reshape(R, C)
+
+    node_reach = mm("pm,mc->pc", after(pivot_inverse[0, 1], rest), node_coupling_all).astype(BF16)
+    leaf_reach = mm("pm,mc->pc", after(pivot_inverse[0, 0], rest), leaf_coupling_all).astype(BF16)
+    leaf_pivots = mm("pk,rk->pr", after(leaf_vectors_pivot[0, 0], rest), leaf_y_all)
+    leaf_pivots = (leaf_pivot_block[0] - leaf_pivots).astype(BF16)
+    wide = jnp.concatenate([node_reach, leaf_reach, folded(leaf_pivots)], axis=0)
+    gathered = lax.all_gather(wide, FRONT, axis=0)
+    node_reach_all = gathered[:, :kp].reshape(K, C)
+    leaf_reach_all = gathered[:, kp : 2 * kp].reshape(K, C)
+    leaf_pivots_all = unfolded(gathered[:, 2 * kp :]).reshape(K, R)
+    leaf_own = mm("pm,mr->pr", pivot_inverse[0, 0], leaf_pivots_all)
 
     partial_y = (y_own + mm("rc,ck->rk", left, w_left)).astype(BF16)
     part = total(exchange(partial_y.reshape(na, R // na, K // nb), "fa")).astype(BF16)
@@ -175,13 +180,6 @@
     part = total(exchange(part.reshape(nb, R // nb, nb * kp), "fb")).astype(BF16)
     part = exchange(part.reshape(na, rc, nb * kp), "fa")
     top = part.transpose(1, 0, 2).reshape(rc, K)
-
-    wide = jnp.concatenate([node_reach, leaf_reach, folded(leaf_pivots.astype(BF16))], axis=0)
-    gathered = lax.all_gather(after(wide, y_block), FRONT, axis=0)
-    node_reach_all = gathered[:, :kp].reshape(K, C)
-    leaf_reach_all = gathered[:, kp : 2 * kp].reshape(K, C)
-    leaf_pivots_all = unfolded(gathered[:, 2 * kp :]).reshape(K, R)
-    leaf_own = mm("pm,mr->pr", pivot_inverse[0, 0], leaf_pivots_all)
 
     pivot_ids = jnp.arange(K, dtype=jnp.int32)[:, None]
     node_pick = (pivot_ids == parent_columns[0, 1][None]).astype(BF16)

time: 508 us -> 498 us (0.980); the launches traced: 506 us -> 490 us
  waiting for transfers between devices: 196 us -> 163 us
  blocking collectives: 144 us -> 167 us
  starting transfers between devices: 89 us -> 78.4 us
    all_to_all x6 -> x8, blocking collectives: 144 us -> 167 us  [exchange(): return lax.all_to_all(parts, axis, split_axis=0, concat_axis=0, tiled=True)]
    all_gather x3, waiting for transfers between devices: 18.2 us -> 0.06 us  [the longest x2 0.04 us: per_device(): gathered = lax.all_gather(wide, FRONT, axis=0)]
    all_to_all x9, waiting for transfers between devices: 165 us -> 150 us  [exchange(): return lax.all_to_all(parts, axis, split_axis=0, concat_axis=0, tiled=True)]
    all_to_all x9, starting transfers between devices: 59.3 us -> 48.7 us  [exchange(): return lax.all_to_all(parts, axis, split_axis=0, concat_axis=0, tiled=True)]
    gather x1 -> x0, local copies, waits for them, and re-layouts: 5.1 us -> none  [per_device(): section_map = jnp.take(section_all, device * ks + within, axis=0)]
    dot_general x19 -> x20, matrix products: 24.3 us -> 20.1 us  [mm(): return jnp.einsum(spec, a, b, preferred_element_type=F32)]
  transfers between devices with their start and end apart: 20 -> 20, of which waited for: 14 -> 14; matrix products, arithmetic and copies ran while one was open for 7% -> 8% of each run, Pallas kernels for 0% -> 0%
where the time goes in v4:
time: 498 us; the launch traced here: 490 us
  blocking collectives  167 us (34%)
  waiting for transfers between devices  163 us (33%)
  starting transfers between devices  78.4 us (16%)
  local copies, waits for them, and re-layouts  31.2 us (6%)
  matrix products  20.1 us (4%)
  between operations  19.3 us (4%)
  other arithmetic  10.6 us (2%)
    all_to_all x8, blocking collectives, exchange(): return lax.all_to_all(parts, axis, split_axis=0, concat_axis=0, tiled=True)  167 us
    all_to_all x9, waiting for transfers between devices, exchange(): return lax.all_to_all(parts, axis, split_axis=0, concat_axis=0, tiled=True)  150 us
    all_to_all x9, starting transfers between devices, exchange(): return lax.all_to_all(parts, axis, split_axis=0, concat_axis=0, tiled=True)  48.7 us
    ppermute x8, starting transfers between devices, from_behind(): lax.ppermute(block, 'leaf', [((i - distance) % count, i) for i in range(c...  29.7 us
    dot_general x20, matrix products, mm(): return jnp.einsum(spec, a, b, preferred_element_type=F32)  20.1 us
    ppermute x8, waiting for transfers between devices, from_behind(): lax.ppermute(block, 'leaf', [((i - distance) % count, i) for i in range(c...  13.2 us
  transfers between devices with their start and end apart: 20, of which 14 were waited for; matrix products, arithmetic and copies ran while one was open for 8% of the time, Pallas kernels for 0%

profile of v4, /device:TPU:24, one launch (start us, length us, event | category | flops | bytes accessed | tf_op | source)
XLA Modules:
  0.0 490.0 jit_solution(1522112626548726634)
XLA Ops:
  10.2 6.0 %all-to-all-start.1 = ((bf16[4,64,2048]{2,1,0:T(8,128)(2,1)}), bf16[4,64,2048]{2,1,0:T(8,128)(2,1)S(1)}, u32[]{:S(2)}, u32[]{:S(2)}) async-start(bf16[4,64,2048]{2,1,0:T(8,128)(2,1)} %bitcast.10), calls=%async_computation.1 | async-start | bytes 2097152 | tf_op jit(solution)/shard_map/all_to_all | solution.py:23
  19.6 24.5 %all-to-all-done.1 = bf16[4,64,2048]{2,1,0:T(8,128)(2,1)S(1)} async-done(((bf16[4,64,2048]{2,1,0:T(8,128)(2,1)}), bf16[4,64,2048]{2,1,0:T(8,128)(2,1)S(1)}, u32[]{:S(2)}, u32[]{:S(2)}) %all-to-all-start.1) | async-done | bytes 1048608 | tf_op jit(solution)/shard_map/all_to_all | solution.py:23
  48.6 5.3 %all-to-all-done = bf16[4,64,192]{2,1,0:T(8,128)(2,1)S(1)} async-done(((bf16[4,64,192]{2,1,0:T(8,128)(2,1)}), bf16[4,64,192]{2,1,0:T(8,128)(2,1)S(1)}, u32[]{:S(2)}, u32[]{:S(2)}) %all-to-all-start) | async-done | bytes 98336 | tf_op jit(solution)/shard_map/all_to_all | solution.py:23
  53.9 16.1 %all-to-all-start.2 = ((bf16[4,64,512]{2,1,0:T(8,128)(2,1)}), bf16[4,64,512]{2,1,0:T(8,128)(2,1)S(1)}, u32[]{:S(2)}, u32[]{:S(2)}) async-start(bf16[4,64,512]{2,1,0:T(8,128)(2,1)} %copy.76), calls=%async_computation.2 | async-start | bytes 524288 | tf_op jit(solution)/shard_map/all_to_all | solution.py:23
  76.9 15.5 %all-to-all-done.2 = bf16[4,64,512]{2,1,0:T(8,128)(2,1)S(1)} async-done(((bf16[4,64,512]{2,1,0:T(8,128)(2,1)}), bf16[4,64,512]{2,1,0:T(8,128)(2,1)S(1)}, u32[]{:S(2)}, u32[]{:S(2)}) %all-to-all-start.2) | async-done | bytes 262176 | tf_op jit(solution)/shard_map/all_to_all | solution.py:23
  99.9 40.6 %all-to-all-done.3 = bf16[4,400,512]{2,1,0:T(8,128)(2,1)S(1)} async-done(((bf16[4,400,512]{2,1,0:T(8,128)(2,1)}), bf16[4,400,512]{2,1,0:T(8,128)(2,1)S(1)}, u32[]{:S(2)}, u32[]{:S(2)}) %all-to-all-start.3) | async-done | bytes 1638432 | tf_op jit(solution)/shard_map/all_to_all | solution.py:23
  149.9 23.7 %all_to_all.85 = bf16[4,64,512]{2,1,0:T(8,128)(2,1)S(1)} all-to-all(bf16[4,64,512]{2,1,0:T(8,128)(2,1)S(1)} %broadcast_in_dim.75), channel_id=1, replica_groups=mesh['leaf'=32,'fa'=4,'fb'=4] {'fa'}, dimensions={0} | all-to-all | bytes 524288 | tf_op jit(solution)/shard_map/all_to_all | solution.py:23
  182.4 19.3 %all-to-all-done.4 = bf16[4,160,512]{2,1,0:T(8,128)(2,1)S(1)} async-done(((bf16[4,160,512]{2,1,0:T(8,128)(2,1)}), bf16[4,160,512]{2,1,0:T(8,128)(2,1)S(1)}, u32[]{:S(2)}, u32[]{:S(2)}) %all-to-all-start.4) | async-done | bytes 655392 | tf_op jit(solution)/shard_map/all_to_all | solution.py:23
  201.7 4.2 all-to-all-start.6
  209.4 14.8 %all-to-all-done.6 = bf16[4,128,512]{2,1,0:T(8,128)(2,1)S(1)} async-done(((bf16[4,128,512]{2,1,0:T(8,128)(2,1)}), bf16[4,128,512]{2,1,0:T(8,128)(2,1)S(1)}, u32[]{:S(2)}, u32[]{:S(2)}) %all-to-all-start.6) | async-done | bytes 524320 | tf_op jit(solution)/shard_map/all_to_all | solution.py:23
  225.7 25.0 %all_to_all.86 = bf16[4,64,512]{2,1,0:T(8,128)(2,1)S(1)} all-to-all(bf16[4,64,512]{2,1,0:T(8,128)(2,1)S(1)} %broadcast_in_dim.76), channel_id=1, replica_groups=mesh['leaf'=32,'fa'=4,'fb'=4] {'fa'}, dimensions={0} | all-to-all | bytes 524288 | tf_op jit(solution)/shard_map/all_to_all | solution.py:23
  255.1 5.3 %collective-permute-done.1 = bf16[64,512]{1,0:T(8,128)(2,1)S(1)} collective-permute-done((bf16[64,512]{1,0:T(8,128)(2,1)S(1)}, bf16[64,512]{1,0:T(8,128)(2,1)S(1)}, u32[]{:S(2)}, u32[]{:S(2)}) %collective-permute-start.1) | collective-permute-done | bytes 65568 | tf_op jit(solution)/shard_map/ppermute | solution.py:19
  260.7 20.4 %all_to_all.87 = bf16[4,64,512]{2,1,0:T(8,128)(2,1)S(1)} all-to-all(bf16[4,64,512]{2,1,0:T(8,128)(2,1)S(1)} %broadcast_in_dim.77), channel_id=1, replica_groups=mesh['leaf'=32,'fa'=4,'fb'=4] {'fa'}, dimensions={0} | all-to-all | bytes 524288 | tf_op jit(solution)/shard_map/all_to_all | solution.py:23
  303.7 6.2 %all-to-all-done.9 = bf16[4,64,512]{2,1,0:T(8,128)(2,1)S(1)} async-done(((bf16[4,64,512]{2,1,0:T(8,128)(2,1)}), bf16[4,64,512]{2,1,0:T(8,128)(2,1)S(1)}, u32[]{:S(2)}, u32[]{:S(2)}) %all-to-all-start.9) | async-done | bytes 262176 | tf_op jit(solution)/shard_map/all_to_all | solution.py:23
  312.1 23.4 %all_to_all.88 = bf16[4,64,512]{2,1,0:T(8,128)(2,1)S(1)} all-to-all(bf16[4,64,512]{2,1,0:T(8,128)(2,1)S(1)} %bitcast.195), channel_id=1, replica_groups=mesh['leaf'=32,'fa'=4,'fb'=4] {'fa'}, dimensions={0} | all-to-all | bytes 524288 | tf_op jit(solution)/shard_map/all_to_all | solution.py:23
  335.6 23.3 %all_to_all.89 = bf16[4,64,512]{2,1,0:T(8,128)(2,1)S(1)} all-to-all(bf16[4,64,512]{2,1,0:T(8,128)(2,1)S(1)} %broadcast_in_dim.79), channel_id=1, replica_groups=mesh['leaf'=32,'fa'=4,'fb'=4] {'fa'}, dimensions={0} | all-to-all | bytes 524288 | tf_op jit(solution)/shard_map/all_to_all | solution.py:23
  359.2 16.4 %all_to_all.90 = bf16[4,160,256]{2,1,0:T(8,128)(2,1)S(1)} all-to-all(bf16[4,160,256]{2,1,0:T(8,128)(2,1)S(1)} %bitcast.181), channel_id=1, replica_groups=mesh['leaf'=32,'fa'=4,'fb'=4] {'fb'}, dimensions={0} | all-to-all | bytes 655360 | tf_op jit(solution)/shard_map/all_to_all | solution.py:23
  375.9 23.0 %all_to_all.91 = bf16[4,128,256]{2,1,0:T(8,128)(2,1)S(1)} all-to-all(bf16[4,128,256]{2,1,0:T(8,128)(2,1)S(1)} %broadcast_in_dim.80), channel_id=1, replica_groups=mesh['leaf'=32,'fa'=4,'fb'=4] {'fa'}, dimensions={0} | all-to-all | bytes 524288 | tf_op jit(solution)/shard_map/all_to_all | solution.py:23
  399.3 11.7 %all_to_all.92 = bf16[4,64,512]{2,1,0:T(8,128)(2,1)S(1)} all-to-all(bf16[4,64,512]{2,1,0:T(8,128)(2,1)S(1)} %bitcast.188), channel_id=1, replica_groups=mesh['leaf'=32,'fa'=4,'fb'=4] {'fb'}, dimensions={0} | all-to-all | bytes 524288 | tf_op jit(solution)/shard_map/all_to_all | solution.py:23
  415.0 13.0 %all-to-all-done.15 = bf16[4,16,512]{2,1,0:T(8,128)(2,1)S(1)} async-done(((bf16[4,16,512]{2,1,0:T(8,128)(2,1)}), bf16[4,16,512]{2,1,0:T(8,128)(2,1)S(1)}, u32[]{:S(2)}, u32[]{:S(2)}) %all-to-all-start.15) | async-done | bytes 65568 | tf_op jit(solution)/shard_map/all_to_all | solution.py:23
  428.0 6.1 %collective-permute-start.4 = (bf16[16,2048]{1,0:T(8,128)(2,1)S(1)}, bf16[16,2048]{1,0:T(8,128)(2,1)S(1)}, u32[]{:S(2)}, u32[]{:S(2)}) collective-permute-start(bf16[16,2048]{1,0:T(8,128)(2,1)S(1)} %bitcast.202), channel_id=1, source_target_pairs={{480,0},{496,16},{0,32},{16,48},{32,64},{48,80},{64,96},{80,112},{... | collective-permute-start | bytes 196616 | tf_op jit(solution)/shard_map/ppermute | solution.py:19
  444.9 5.8 %collective-permute-start.5 = (bf16[16,2048]{1,0:T(8,128)(2,1)S(1)}, bf16[16,2048]{1,0:T(8,128)(2,1)S(1)}, u32[]{:S(2)}, u32[]{:S(2)}) collective-permute-start(bf16[16,2048]{1,0:T(8,128)(2,1)S(1)} %fusion.4), channel_id=1, source_target_pairs={{16,0},{32,16},{48,32},{64,48},{80,64},{96,80},{112,96},{128,112},... | collective-permute-start | bytes 196616 | tf_op jit(solution)/shard_map/ppermute | solution.py:19
  455.5 5.8 %collective-permute-start.7 = (bf16[16,2048]{1,0:T(8,128)(2,1)S(1)}, bf16[16,2048]{1,0:T(8,128)(2,1)S(1)}, u32[]{:S(2)}, u32[]{:S(2)}) collective-permute-start(bf16[16,2048]{1,0:T(8,128)(2,1)S(1)} %fusion.5), channel_id=1, source_target_pairs={{16,0},{32,16},{48,32},{64,48},{80,64},{96,80},{112,96},{128,112},... | collective-permute-start | bytes 196616 | tf_op jit(solution)/shard_map/ppermute | solution.py:19
  471.1 11.1 %all-to-all-done.16 = bf16[16,2,16,128]{3,2,1,0:T(8,128)(2,1)S(1)} async-done(((bf16[16,2,16,128]{3,2,1,0:T(8,128)(2,1)}), bf16[16,2,16,128]{3,2,1,0:T(8,128)(2,1)S(1)}, u32[]{:S(2)}, u32[]{:S(2)}) %all-to-all-start.16) | async-done | bytes 131104 | tf_op jit(solution)/shard_map/all_to_all | solution.py:23
  (196 shorter events, 104.3 us)
Async XLA Ops:
  10.2 33.9 %all-to-all-start.1 = ((bf16[4,64,2048]{2,1,0:T(8,128)(2,1)}), bf16[4,64,2048]{2,1,0:T(8,128)(2,1)S(1)}, u32[]{:S(2)}, u32[]{:S(2)}) async-start(bf16[4,64,2048]{2,1,0:T(8,128)(2,1)} %bitcast.10), calls=%async_computation.1 | async-start | bytes 2097152 | tf_op jit(solution)/shard_map/all_to_all | solution.py:23
  16.3 125.5 %all-gather.8.cloned.1.call-start = ((), (), s32[]{:S(2)}) async-start(), calls=%async_computation.18 | async-start | bytes 4456448 | tf_op jit(solution)/shard_map/all_gather | solution.py:101
  17.8 52.3 %copy-start.5 = (bf16[1,2,128,2048]{3,2,1,0:T(8,128)(2,1)S(1)}, bf16[1,2,128,2048]{3,2,1,0:T(8,128)(2,1)}, u32[]{:S(2)}) copy-start(bf16[1,2,128,2048]{3,2,1,0:T(8,128)(2,1)} %param.18) | copy-start | bytes 3145732
  44.1 9.8 %all-to-all-start = ((bf16[4,64,192]{2,1,0:T(8,128)(2,1)}), bf16[4,64,192]{2,1,0:T(8,128)(2,1)S(1)}, u32[]{:S(2)}, u32[]{:S(2)}) async-start(bf16[4,64,192]{2,1,0:T(8,128)(2,1)} %bitcast.5), calls=%async_computation | async-start | bytes 262144 | tf_op jit(solution)/shard_map/all_to_all | solution.py:23
  53.9 38.4 %all-to-all-start.2 = ((bf16[4,64,512]{2,1,0:T(8,128)(2,1)}), bf16[4,64,512]{2,1,0:T(8,128)(2,1)S(1)}, u32[]{:S(2)}, u32[]{:S(2)}) async-start(bf16[4,64,512]{2,1,0:T(8,128)(2,1)} %copy.76), calls=%async_computation.2 | async-start | bytes 524288 | tf_op jit(solution)/shard_map/all_to_all | solution.py:23
  92.4 48.1 %all-to-all-start.3 = ((bf16[4,400,512]{2,1,0:T(8,128)(2,1)}), bf16[4,400,512]{2,1,0:T(8,128)(2,1)S(1)}, u32[]{:S(2)}, u32[]{:S(2)}) async-start(bf16[4,400,512]{2,1,0:T(8,128)(2,1)} %maximum_add_fusion), calls=%async_computation.3 | async-start | bytes 3276800 | tf_op jit(solution)/shard_map/all_to_all | solution.py:23
  96.3 186.1 %all-gather.6.cloned.1.call-start = ((), (), s32[]{:S(2)}) async-start(), calls=%async_computation.17 | async-start | bytes 5570560 | tf_op jit(solution)/shard_map/all_gather | solution.py:131
  149.9 30.9 %copy-start.2 = (bf16[1,2,128,2048]{3,2,1,0:T(8,128)(2,1)S(1)}, bf16[1,2,128,2048]{3,2,1,0:T(8,128)(2,1)}, u32[]{:S(2)}) copy-start(bf16[1,2,128,2048]{3,2,1,0:T(8,128)(2,1)} %param.23) | copy-start | bytes 3145732
  175.5 26.2 %all-to-all-start.4 = ((bf16[4,160,512]{2,1,0:T(8,128)(2,1)}), bf16[4,160,512]{2,1,0:T(8,128)(2,1)S(1)}, u32[]{:S(2)}, u32[]{:S(2)}) async-start(bf16[4,160,512]{2,1,0:T(8,128)(2,1)} %broadcast_in_dim.72), calls=%async_computation.4 | async-start | bytes 1310720 | tf_op jit(solution)/shard_map/all_to_all | solution.py:23
  201.7 22.5 %all-to-all-start.6 = ((bf16[4,128,512]{2,1,0:T(8,128)(2,1)}), bf16[4,128,512]{2,1,0:T(8,128)(2,1)S(1)}, u32[]{:S(2)}, u32[]{:S(2)}) async-start(bf16[4,128,512]{2,1,0:T(8,128)(2,1)} %add.262), calls=%async_computation.6 | async-start | bytes 1048576 | tf_op jit(solution)/shard_map/all_to_all | solution.py:23
  205.9 228.2 %all-gather.10.cloned.1.call-start = ((), (), s32[]{:S(2)}) async-start(), calls=%async_computation.19 | async-start | bytes 5570560 | tf_op jit(solution)/shard_map/all_gather | solution.py:164
  206.1 19.3 %collective-permute-start = (bf16[64,512]{1,0:T(8,128)(2,1)S(1)}, bf16[64,512]{1,0:T(8,128)(2,1)S(1)}, u32[]{:S(2)}, u32[]{:S(2)}) collective-permute-start(bf16[64,512]{1,0:T(8,128)(2,1)S(1)} %reduce_sum.95), channel_id=1, source_target_pairs={{496,0},{0,16},{16,32},{32,48},{48,64},{64,80},{80,96},{96,112},{1... | collective-permute-start | bytes 196616 | tf_op jit(solution)/shard_map/ppermute | solution.py:19
  250.7 4.3 collective-permute-start.2
  252.7 7.7 %collective-permute-start.1 = (bf16[64,512]{1,0:T(8,128)(2,1)S(1)}, bf16[64,512]{1,0:T(8,128)(2,1)S(1)}, u32[]{:S(2)}, u32[]{:S(2)}) collective-permute-start(bf16[64,512]{1,0:T(8,128)(2,1)S(1)} %reduce_sum.96), channel_id=1, source_target_pairs={{496,0},{0,16},{16,32},{32,48},{48,64},{64,80},{80,96},{96,112},{1... | collective-permute-start | bytes 196616 | tf_op jit(solution)/shard_map/ppermute | solution.py:19
  289.2 6.2 %collective-permute-start.3 = (bf16[64,512]{1,0:T(8,128)(2,1)S(1)}, bf16[64,512]{1,0:T(8,128)(2,1)S(1)}, u32[]{:S(2)}, u32[]{:S(2)}) collective-permute-start(bf16[64,512]{1,0:T(8,128)(2,1)S(1)} %reduce_sum.97), channel_id=1, source_target_pairs={{32,0},{48,16},{64,32},{80,48},{96,64},{112,80},{128,96},{144,112}... | collective-permute-start | bytes 196616 | tf_op jit(solution)/shard_map/ppermute | solution.py:19
  296.1 13.8 %all-to-all-start.9 = ((bf16[4,64,512]{2,1,0:T(8,128)(2,1)}), bf16[4,64,512]{2,1,0:T(8,128)(2,1)S(1)}, u32[]{:S(2)}, u32[]{:S(2)}) async-start(bf16[4,64,512]{2,1,0:T(8,128)(2,1)} %broadcast_in_dim.78), calls=%async_computation.9 | async-start | bytes 524288 | tf_op jit(solution)/shard_map/all_to_all | solution.py:23
  312.1 63.5 %copy-start.12 = (pred[160,1024]{1,0:T(32,128)(4,1)S(1)}, pred[160,1024]{1,0:T(32,128)(4,1)}, u32[]{:S(2)}) copy-start(pred[160,1024]{1,0:T(32,128)(4,1)} %get-tuple-element.37) | copy-start | bytes 491524
  375.6 39.4 %copy-start.25 = (s32[1,2,512]{2,1,0:T(2,128)S(1)}, s32[1,2,512]{2,1,0:T(2,128)}, u32[]{:S(2)}) copy-start(s32[1,2,512]{2,1,0:T(2,128)} %param.21) | copy-start | bytes 12292
  411.7 16.3 %all-to-all-start.15 = ((bf16[4,16,512]{2,1,0:T(8,128)(2,1)}), bf16[4,16,512]{2,1,0:T(8,128)(2,1)S(1)}, u32[]{:S(2)}, u32[]{:S(2)}) async-start(bf16[4,16,512]{2,1,0:T(8,128)(2,1)} %bitcast.59), calls=%async_computation.15 | async-start | bytes 131072 | tf_op jit(solution)/shard_map/all_to_all | solution.py:23
  428.0 12.1 %collective-permute-start.4 = (bf16[16,2048]{1,0:T(8,128)(2,1)S(1)}, bf16[16,2048]{1,0:T(8,128)(2,1)S(1)}, u32[]{:S(2)}, u32[]{:S(2)}) collective-permute-start(bf16[16,2048]{1,0:T(8,128)(2,1)S(1)} %bitcast.202), channel_id=1, source_target_pairs={{480,0},{496,16},{0,32},{16,48},{32,64},{48,80},{64,96},{80,112},{... | collective-permute-start | bytes 196616 | tf_op jit(solution)/shard_map/ppermute | solution.py:19
  443.0 7.7 %collective-permute-start.6 = (bf16[16,2048]{1,0:T(8,128)(2,1)S(1)}, bf16[16,2048]{1,0:T(8,128)(2,1)S(1)}, u32[]{:S(2)}, u32[]{:S(2)}) collective-permute-start(bf16[16,2048]{1,0:T(8,128)(2,1)S(1)} %fusion.4), channel_id=1, source_target_pairs={{496,0},{0,16},{16,32},{32,48},{48,64},{64,80},{80,96},{96,112},{1... | collective-permute-start | bytes 196616 | tf_op jit(solution)/shard_map/ppermute | solution.py:19
  444.9 7.6 %collective-permute-start.5 = (bf16[16,2048]{1,0:T(8,128)(2,1)S(1)}, bf16[16,2048]{1,0:T(8,128)(2,1)S(1)}, u32[]{:S(2)}, u32[]{:S(2)}) collective-permute-start(bf16[16,2048]{1,0:T(8,128)(2,1)S(1)} %fusion.4), channel_id=1, source_target_pairs={{16,0},{32,16},{48,32},{64,48},{80,64},{96,80},{112,96},{128,112},... | collective-permute-start | bytes 196616 | tf_op jit(solution)/shard_map/ppermute | solution.py:19
  455.5 7.7 %collective-permute-start.7 = (bf16[16,2048]{1,0:T(8,128)(2,1)S(1)}, bf16[16,2048]{1,0:T(8,128)(2,1)S(1)}, u32[]{:S(2)}, u32[]{:S(2)}) collective-permute-start(bf16[16,2048]{1,0:T(8,128)(2,1)S(1)} %fusion.5), channel_id=1, source_target_pairs={{16,0},{32,16},{48,32},{64,48},{80,64},{96,80},{112,96},{128,112},... | collective-permute-start | bytes 196616 | tf_op jit(solution)/shard_map/ppermute | solution.py:19
  465.3 16.9 %all-to-all-start.16 = ((bf16[16,2,16,128]{3,2,1,0:T(8,128)(2,1)}), bf16[16,2,16,128]{3,2,1,0:T(8,128)(2,1)S(1)}, u32[]{:S(2)}, u32[]{:S(2)}) async-start(bf16[16,2,16,128]{3,2,1,0:T(8,128)(2,1)} %maximum_bitcast_fusion.1), calls=%async_computation.16 | async-start | bytes 262144 | tf_op jit(solution)/shard_map/all_to_all | solution.py:23
  (24 other events, 177.7 us)
Sparse Core Ops, SparseCore 0:
  19.2 107.6 all-gather.7
  148.2 113.7 all-gather.5
  289.3 112.4 all-gather.9

commit v5 on v4

--- a/solution.py
+++ b/solution.py
@@ -105,7 +105,6 @@
     leaf_partial = mm("ir,ik->rk", leaf_pivot_block[0], leaf_vectors_pivot[0, 1])
     leaf_partial = leaf_partial + mm("ir,ik->rk", leaf_rest_block[0], leaf_vectors_rest[0, 1])
     leaf_part = total(exchange(leaf_partial.astype(BF16).reshape(nb, rb, K), "fb")).astype(BF16)
-    leaf_y = total(exchange(leaf_part.reshape(rb, na, K // na).transpose(1, 0, 2), "fa")).astype(BF16)
 
     both = jnp.concatenate([leaf_rest_block[0], own], axis=0).T.reshape(nb, rb, kc + ks)
     both = exchange(both, "fb")
@@ -115,30 +114,36 @@
     blocks = jnp.concatenate([node_w, node_v], axis=0).reshape(2 * ks, nb, K // nb).transpose(1, 0, 2)
     own_folded = folded(own)
     blocks = jnp.concatenate([blocks, jnp.broadcast_to(own_folded, (nb, *own_folded.shape))], axis=1)
-    blocks = exchange(after(blocks, both), "fb")
+    blocks = exchange(after(after(blocks, both), leaf_part), "fb")
     w_block = blocks[:, :ks].reshape(nb * ks, K // nb)
     v_block = blocks[:, ks : 2 * ks].reshape(nb * ks, K // nb)
     own_block = unfolded(blocks[:, 2 * ks :]).reshape(nb * ks, R)
 
+    inverse_block = pivot_inverse[0, 1].reshape(kp, na, nb, kp).transpose(2, 0, 1, 3)
+    inverse_block = after(inverse_block.reshape(nb, kp, na * kp), blocks)
+    inverse_block = exchange(inverse_block, "fb").reshape(nb * kp, na * kp)
+
     product = mm("sk,ck->sc", node_w, node_ve_all)
     unit = (rows[:, None] == K + jnp.arange(C, dtype=jnp.int32)[None]).astype(F32)
-    section_rows = (after(after(unit, leaf_y), blocks) - product).astype(BF16)
+    section_rows = (after(unit, inverse_block) - product).astype(BF16)
     section_block = to_all(section_rows, "fb").reshape(nb * ks, C)
     block_rows = jnp.concatenate([stack_rows(ia * nb + b) for b in range(nb)])
     block_hit = (place[:, None] == block_rows[None]).astype(BF16)
 
+    def summed(part):
+        return total(to_all(part.astype(BF16), "fa")).astype(BF16)
+
+    is_mine = jnp.arange(C, dtype=jnp.int32) // (nb * kc) == ia
+    part = jnp.where(is_mine[None], jnp.tile(leaf_rest.astype(F32), (1, na)), 0.0)
+    rest = summed(part - mm("rk,ck->rc", leaf_part, leaf_ve_all))
+    leaf_y = after(leaf_part, section_rows).reshape(rb, na, K // na).transpose(1, 0, 2)
+    leaf_y = lax.psum_scatter(leaf_y, "fa", scatter_dimension=0)
     wide = jnp.concatenate([coupling[0, 1], coupling[0, 0], leaf_y], axis=0)
-    gathered = lax.all_gather(after(wide, section_rows), FRONT, axis=0)
+    gathered = lax.all_gather(after(after(wide, rest), section_block), FRONT, axis=0)
     node_coupling_all = gathered[:, :kp].reshape(K, C)
     leaf_coupling_all = gathered[:, kp : 2 * kp].reshape(K, C)
     leaf_y_all = gathered[:, 2 * kp :].reshape(na, nb, rb, K // na).transpose(1, 2, 0, 3).reshape(R, K)
 
-    def summed(part):
-        return total(to_all(part.astype(BF16), "fa")).astype(BF16)
-
-    is_mine = jnp.arange(C, dtype=jnp.int32) // (nb * kc) == ia
-    part = jnp.where(is_mine[None], jnp.tile(leaf_rest.astype(F32), (1, na)), 0.0)
-    rest = summed(part - mm("rk,ck->rc", leaf_part, leaf_ve_all))
     section_map = mm("js,sc->jc", block_hit, section_block).astype(BF16)
     section_own = mm("rs,sc->rc", own_columns, section_block)
 
@@ -146,19 +151,17 @@
         children = jnp.concatenate([left, right], axis=1)
         return summed(section_own + mm("rj,jc->rc", children, section_map))
 
-    inverse_block = pivot_inverse[0, 1].reshape(kp, na, nb, kp).transpose(2, 0, 1, 3)
-    inverse_block = after(inverse_block.reshape(nb, kp, na * kp), rest)
-    inverse_block = exchange(inverse_block, "fb").reshape(nb * kp, na * kp)
-
-    rest = section(after(from_behind(rest, 1), inverse_block), rest)
+    rest = section(from_behind(rest, 1), rest)
     rest = section(from_behind(rest, 1), from_behind(rest, -1))
     w_left = mm("cs,sk->ck", block_hit[:C], w_block).astype(BF16)
     y_own = mm("sr,sk->rk", own_block, w_block)
     left = to_all(from_behind(rest, -(subtree // 2)), "fb").reshape(R, C)
 
-    node_reach = mm("pm,mc->pc", after(pivot_inverse[0, 1], rest), node_coupling_all).astype(BF16)
-    leaf_reach = mm("pm,mc->pc", after(pivot_inverse[0, 0], rest), leaf_coupling_all).astype(BF16)
-    leaf_pivots = mm("pk,rk->pr", after(leaf_vectors_pivot[0, 0], rest), leaf_y_all)
+    partial_y = (y_own + mm("rc,ck->rk", left, w_left)).astype(BF16)
+    part = total(exchange(partial_y.reshape(na, R // na, K // nb), "fa")).astype(BF16)
+    node_reach = mm("pm,mc->pc", after(pivot_inverse[0, 1], part), node_coupling_all).astype(BF16)
+    leaf_reach = mm("pm,mc->pc", after(pivot_inverse[0, 0], part), leaf_coupling_all).astype(BF16)
+    leaf_pivots = mm("pk,rk->pr", after(leaf_vectors_pivot[0, 0], part), leaf_y_all)
     leaf_pivots = (leaf_pivot_block[0] - leaf_pivots).astype(BF16)
     wide = jnp.concatenate([node_reach, leaf_reach, folded(leaf_pivots)], axis=0)
     gathered = lax.all_gather(wide, FRONT, axis=0)
@@ -167,8 +170,6 @@
     leaf_pivots_all = unfolded(gathered[:, 2 * kp :]).reshape(K, R)
     leaf_own = mm("pm,mr->pr", pivot_inverse[0, 0], leaf_pivots_all)
 
-    partial_y = (y_own + mm("rc,ck->rk", left, w_left)).astype(BF16)
-    part = total(exchange(partial_y.reshape(na, R // na, K // nb), "fa")).astype(BF16)
     y_block = to_all(part, "fa").reshape(R, K // nb)
     part = mm("sk,rk->sr", v_block, y_block).astype(BF16).reshape(nb, ks, R)
     placed = mm("sc,rc->sr", own_hit[:, :C].astype(BF16), left)

time: 498 us -> 507 us (1.018)
  blocking collectives: 167 us -> 210 us
  waiting for transfers between devices: 163 us -> 135 us
  starting transfers between devices: 78.4 us -> 67 us
    all_to_all x9 -> x8, waiting for transfers between devices: 150 us -> 70.6 us  [exchange(): return lax.all_to_all(parts, axis, split_axis=0, concat_axis=0, tiled=True)]
    all_to_all x8, blocking collectives: 167 us -> 210 us  [exchange(): return lax.all_to_all(parts, axis, split_axis=0, concat_axis=0, tiled=True)]
    all_gather x2, waiting for transfers between devices: 0.04 us -> 26.9 us  [per_device(): gathered = lax.all_gather(wide, FRONT, axis=0)]
    reduce_scatter x0 -> x1, waiting for transfers between devices: none -> 21.6 us  [per_device(): leaf_y = lax.psum_scatter(leaf_y, 'fa', scatter_dimension=0)]
    all_to_all x9 -> x8, starting transfers between devices: 48.7 us -> 41 us  [exchange(): return lax.all_to_all(parts, axis, split_axis=0, concat_axis=0, tiled=True)]
  transfers between devices with their start and end apart: 20 -> 20, of which waited for: 14 -> 15; matrix products, arithmetic and copies ran while one was open for 8% -> 9% of each run, Pallas kernels for 0% -> 0%
where the time goes in v5:
time: 507 us; the launch traced here: 504 us
  blocking collectives  210 us (41%)
  waiting for transfers between devices  135 us (27%)
  starting transfers between devices  67 us (13%)
  local copies, waits for them, and re-layouts  35 us (7%)
  matrix products  24.2 us (5%)
  between operations  19.9 us (4%)
  other arithmetic  12.9 us (3%)
    all_to_all x8, blocking collectives, exchange(): return lax.all_to_all(parts, axis, split_axis=0, concat_axis=0, tiled=True)  210 us
    all_to_all x8, waiting for transfers between devices, exchange(): return lax.all_to_all(parts, axis, split_axis=0, concat_axis=0, tiled=True)  70.6 us
    all_to_all x8, starting transfers between devices, exchange(): return lax.all_to_all(parts, axis, split_axis=0, concat_axis=0, tiled=True)  41 us
    all_gather x2, waiting for transfers between devices, per_device(): gathered = lax.all_gather(wide, FRONT, axis=0)  26.9 us
    ppermute x8, starting transfers between devices, from_behind(): lax.ppermute(block, 'leaf', [((i - distance) % count, i) for i in range(c...  25.9 us
    dot_general x20, matrix products, mm(): return jnp.einsum(spec, a, b, preferred_element_type=F32)  24.2 us
    reduce_scatter x1, waiting for transfers between devices, per_device(): leaf_y = lax.psum_scatter(leaf_y, 'fa', scatter_dimension=0)  21.6 us
    ppermute x8, waiting for transfers between devices, from_behind(): lax.ppermute(block, 'leaf', [((i - distance) % count, i) for i in range(c...  15.4 us
  transfers between devices with their start and end apart: 20, of which 15 were waited for; matrix products, arithmetic and copies ran while one was open for 9% of the time, Pallas kernels for 0%

profile of v5, /device:TPU:24, one launch (start us, length us, event | category | flops | bytes accessed | tf_op | source)
XLA Modules:
  0.0 503.5 jit_solution(9465907863355923262)
XLA Ops:
  11.2 5.9 %all-to-all-start = ((bf16[4,64,192]{2,1,0:T(8,128)(2,1)}), bf16[4,64,192]{2,1,0:T(8,128)(2,1)S(1)}, u32[]{:S(2)}, u32[]{:S(2)}) async-start(bf16[4,64,192]{2,1,0:T(8,128)(2,1)} %bitcast.9), calls=%async_computation | async-start | bytes 262144 | tf_op jit(solution)/shard_map/all_to_all | solution.py:23
  36.5 14.8 %all-to-all-done.1 = bf16[4,64,2048]{2,1,0:T(8,128)(2,1)S(1)} async-done(((bf16[4,64,2048]{2,1,0:T(8,128)(2,1)}), bf16[4,64,2048]{2,1,0:T(8,128)(2,1)S(1)}, u32[]{:S(2)}, u32[]{:S(2)}) %all-to-all-start.1) | async-done | bytes 1048608 | tf_op jit(solution)/shard_map/all_to_all | solution.py:23
  53.1 58.2 %all_to_all.80 = bf16[4,400,512]{2,1,0:T(8,128)(2,1)S(1)} all-to-all(bf16[4,400,512]{2,1,0:T(8,128)(2,1)S(1)} %fusion.9), channel_id=1, replica_groups=mesh['leaf'=32,'fa'=4,'fb'=4] {'fb'}, dimensions={0} | all-to-all | bytes 3276800 | tf_op jit(solution)/shard_map/all_to_all | solution.py:23
  119.6 24.2 %all-gather.8.cloned.1.call-done = bf16[1024,2048]{1,0:T(8,128)(2,1)} async-done(((bf16[64,2048]{1,0:T(8,128)(2,1)}), bf16[1024,2048]{1,0:T(8,128)(2,1)}) %all-gather.8.cloned.1.call-update) | async-done | bytes 4194320 | tf_op jit(solution)/shard_map/all_gather | solution.py:101
  143.8 4.1 fusion.86
  149.5 8.2 %all-to-all-start.5 = ((bf16[4,64,512]{2,1,0:T(8,128)(2,1)}), bf16[4,64,512]{2,1,0:T(8,128)(2,1)}, u32[]{:S(2)}, u32[]{:S(2)}) async-start(bf16[4,64,512]{2,1,0:T(8,128)(2,1)} %broadcast_in_dim.76), calls=%async_computation.5 | async-start | bytes 524288 | tf_op jit(solution)/shard_map/all_to_all | solution.py:23
  161.6 11.3 %all-to-all-done.5 = bf16[4,64,512]{2,1,0:T(8,128)(2,1)} async-done(((bf16[4,64,512]{2,1,0:T(8,128)(2,1)}), bf16[4,64,512]{2,1,0:T(8,128)(2,1)}, u32[]{:S(2)}, u32[]{:S(2)}) %all-to-all-start.5) | async-done | bytes 262176 | tf_op jit(solution)/shard_map/all_to_all | solution.py:23
  173.8 6.3 %all-to-all-start.4 = ((bf16[4,160,512]{2,1,0:T(8,128)(2,1)}), bf16[4,160,512]{2,1,0:T(8,128)(2,1)S(1)}, u32[]{:S(2)}, u32[]{:S(2)}) async-start(bf16[4,160,512]{2,1,0:T(8,128)(2,1)} %broadcast_in_dim.73), calls=%async_computation.4 | async-start | bytes 1310720 | tf_op jit(solution)/shard_map/all_to_all | solution.py:23
  185.6 8.3 %all-to-all-done.4 = bf16[4,160,512]{2,1,0:T(8,128)(2,1)S(1)} async-done(((bf16[4,160,512]{2,1,0:T(8,128)(2,1)}), bf16[4,160,512]{2,1,0:T(8,128)(2,1)S(1)}, u32[]{:S(2)}, u32[]{:S(2)}) %all-to-all-start.4) | async-done | bytes 655392 | tf_op jit(solution)/shard_map/all_to_all | solution.py:23
  195.1 21.6 %reduce-scatter.2.cloned.1.call-done = bf16[1,64,512]{2,1,0:T(8,128)(2,1)} async-done(((bf16[4,64,512]{2,1,0:T(8,128)(2,1)}), bf16[1,64,512]{2,1,0:T(8,128)(2,1)}) %reduce-scatter.2.cloned.1.call-update) | async-done | bytes 65552 | tf_op jit(solution)/shard_map/reduce_scatter | solution.py:140
  227.5 28.7 %all_to_all.81 = bf16[4,64,512]{2,1,0:T(8,128)(2,1)S(1)} all-to-all(bf16[4,64,512]{2,1,0:T(8,128)(2,1)S(1)} %broadcast_in_dim.77), channel_id=1, replica_groups=mesh['leaf'=32,'fa'=4,'fb'=4] {'fa'}, dimensions={0} | all-to-all | bytes 524288 | tf_op jit(solution)/shard_map/all_to_all | solution.py:23
  261.0 5.8 %collective-permute-done.1 = bf16[64,512]{1,0:T(8,128)(2,1)S(1)} collective-permute-done((bf16[64,512]{1,0:T(8,128)(2,1)S(1)}, bf16[64,512]{1,0:T(8,128)(2,1)S(1)}, u32[]{:S(2)}, u32[]{:S(2)}) %collective-permute-start.1) | collective-permute-done | bytes 65568 | tf_op jit(solution)/shard_map/ppermute | solution.py:19
  267.1 24.6 %all_to_all.82 = bf16[4,64,512]{2,1,0:T(8,128)(2,1)S(1)} all-to-all(bf16[4,64,512]{2,1,0:T(8,128)(2,1)S(1)} %broadcast_in_dim.78), channel_id=1, replica_groups=mesh['leaf'=32,'fa'=4,'fb'=4] {'fa'}, dimensions={0} | all-to-all | bytes 524288 | tf_op jit(solution)/shard_map/all_to_all | solution.py:23
  304.7 8.4 %all-to-all-done.8 = bf16[4,64,512]{2,1,0:T(8,128)(2,1)S(1)} async-done(((bf16[4,64,512]{2,1,0:T(8,128)(2,1)}), bf16[4,64,512]{2,1,0:T(8,128)(2,1)S(1)}, u32[]{:S(2)}, u32[]{:S(2)}) %all-to-all-start.8) | async-done | bytes 262176 | tf_op jit(solution)/shard_map/all_to_all | solution.py:23
  315.1 20.7 %all_to_all.83 = bf16[4,64,512]{2,1,0:T(8,128)(2,1)S(1)} all-to-all(bf16[4,64,512]{2,1,0:T(8,128)(2,1)S(1)} %bitcast.201), channel_id=1, replica_groups=mesh['leaf'=32,'fa'=4,'fb'=4] {'fa'}, dimensions={0} | all-to-all | bytes 524288 | tf_op jit(solution)/shard_map/all_to_all | solution.py:23
  343.9 20.3 %all_to_all.84 = bf16[4,64,512]{2,1,0:T(8,128)(2,1)S(1)} all-to-all(bf16[4,64,512]{2,1,0:T(8,128)(2,1)S(1)} %broadcast_in_dim.80), channel_id=1, replica_groups=mesh['leaf'=32,'fa'=4,'fb'=4] {'fa'}, dimensions={0} | all-to-all | bytes 524288 | tf_op jit(solution)/shard_map/all_to_all | solution.py:23
  364.5 18.4 %all_to_all.85 = bf16[4,160,256]{2,1,0:T(8,128)(2,1)S(1)} all-to-all(bf16[4,160,256]{2,1,0:T(8,128)(2,1)S(1)} %bitcast.187), channel_id=1, replica_groups=mesh['leaf'=32,'fa'=4,'fb'=4] {'fb'}, dimensions={0} | all-to-all | bytes 655360 | tf_op jit(solution)/shard_map/all_to_all | solution.py:23
  383.3 25.7 %all_to_all.86 = bf16[4,128,256]{2,1,0:T(8,128)(2,1)S(1)} all-to-all(bf16[4,128,256]{2,1,0:T(8,128)(2,1)S(1)} %broadcast_in_dim.81), channel_id=1, replica_groups=mesh['leaf'=32,'fa'=4,'fb'=4] {'fa'}, dimensions={0} | all-to-all | bytes 524288 | tf_op jit(solution)/shard_map/all_to_all | solution.py:23
  409.4 13.4 %all_to_all.87 = bf16[4,64,512]{2,1,0:T(8,128)(2,1)S(1)} all-to-all(bf16[4,64,512]{2,1,0:T(8,128)(2,1)S(1)} %bitcast.195), channel_id=1, replica_groups=mesh['leaf'=32,'fa'=4,'fb'=4] {'fb'}, dimensions={0} | all-to-all | bytes 524288 | tf_op jit(solution)/shard_map/all_to_all | solution.py:23
  426.8 13.6 %all-to-all-done.14 = bf16[4,16,512]{2,1,0:T(8,128)(2,1)S(1)} async-done(((bf16[4,16,512]{2,1,0:T(8,128)(2,1)}), bf16[4,16,512]{2,1,0:T(8,128)(2,1)S(1)}, u32[]{:S(2)}, u32[]{:S(2)}) %all-to-all-start.14) | async-done | bytes 65568 | tf_op jit(solution)/shard_map/all_to_all | solution.py:23
  453.8 5.8 %collective-permute-start.5 = (bf16[16,2048]{1,0:T(8,128)(2,1)S(1)}, bf16[16,2048]{1,0:T(8,128)(2,1)S(1)}, u32[]{:S(2)}, u32[]{:S(2)}) collective-permute-start(bf16[16,2048]{1,0:T(8,128)(2,1)S(1)} %fusion.4), channel_id=1, source_target_pairs={{16,0},{32,16},{48,32},{64,48},{80,64},{96,80},{112,96},{128,112},... | collective-permute-start | bytes 196616 | tf_op jit(solution)/shard_map/ppermute | solution.py:19
  464.4 5.8 %collective-permute-start.7 = (bf16[16,2048]{1,0:T(8,128)(2,1)S(1)}, bf16[16,2048]{1,0:T(8,128)(2,1)S(1)}, u32[]{:S(2)}, u32[]{:S(2)}) collective-permute-start(bf16[16,2048]{1,0:T(8,128)(2,1)S(1)} %fusion.5), channel_id=1, source_target_pairs={{16,0},{32,16},{48,32},{64,48},{80,64},{96,80},{112,96},{128,112},... | collective-permute-start | bytes 196616 | tf_op jit(solution)/shard_map/ppermute | solution.py:19
  475.7 6.9 %all-to-all-start.15 = ((bf16[16,2,16,128]{3,2,1,0:T(8,128)(2,1)}), bf16[16,2,16,128]{3,2,1,0:T(8,128)(2,1)S(1)}, u32[]{:S(2)}, u32[]{:S(2)}) async-start(bf16[16,2,16,128]{3,2,1,0:T(8,128)(2,1)} %maximum_bitcast_fusion.1), calls=%async_computation.16 | async-start | bytes 262144 | tf_op jit(solution)/shard_map/all_to_all | solution.py:23
  484.5 11.1 %all-to-all-done.15 = bf16[16,2,16,128]{3,2,1,0:T(8,128)(2,1)S(1)} async-done(((bf16[16,2,16,128]{3,2,1,0:T(8,128)(2,1)}), bf16[16,2,16,128]{3,2,1,0:T(8,128)(2,1)S(1)}, u32[]{:S(2)}, u32[]{:S(2)}) %all-to-all-start.15) | async-done | bytes 131104 | tf_op jit(solution)/shard_map/all_to_all | solution.py:23
  (184 shorter events, 111.7 us)
Async XLA Ops:
  11.2 12.0 %all-to-all-start = ((bf16[4,64,192]{2,1,0:T(8,128)(2,1)}), bf16[4,64,192]{2,1,0:T(8,128)(2,1)S(1)}, u32[]{:S(2)}, u32[]{:S(2)}) async-start(bf16[4,64,192]{2,1,0:T(8,128)(2,1)} %bitcast.9), calls=%async_computation | async-start | bytes 262144 | tf_op jit(solution)/shard_map/all_to_all | solution.py:23
  23.2 96.2 %copy-start.7 = (bf16[4,64,192]{2,1,0:T(8,128)(2,1)}, bf16[4,64,192]{2,1,0:T(8,128)(2,1)S(1)}, u32[]{:S(2)}) copy-start(bf16[4,64,192]{2,1,0:T(8,128)(2,1)S(1)} %all-to-all-done) | copy-start | bytes 294916
  23.2 28.1 %all-to-all-start.1 = ((bf16[4,64,2048]{2,1,0:T(8,128)(2,1)}), bf16[4,64,2048]{2,1,0:T(8,128)(2,1)S(1)}, u32[]{:S(2)}, u32[]{:S(2)}) async-start(bf16[4,64,2048]{2,1,0:T(8,128)(2,1)} %bitcast.14), calls=%async_computation.1 | async-start | bytes 2097152 | tf_op jit(solution)/shard_map/all_to_all | solution.py:23
  26.7 117.1 %all-gather.8.cloned.1.call-start = ((), (), s32[]{:S(2)}) async-start(), calls=%async_computation.19 | async-start | bytes 4456448 | tf_op jit(solution)/shard_map/all_gather | solution.py:101
  53.1 59.4 %copy-start.3 = (bf16[1,2,128,2048]{3,2,1,0:T(8,128)(2,1)S(1)}, bf16[1,2,128,2048]{3,2,1,0:T(8,128)(2,1)}, u32[]{:S(2)}) copy-start(bf16[1,2,128,2048]{3,2,1,0:T(8,128)(2,1)} %param.23) | copy-start | bytes 3145732
  115.9 32.8 %all-to-all-start.3 = ((bf16[4,128,512]{2,1,0:T(8,128)(2,1)}), bf16[4,128,512]{2,1,0:T(8,128)(2,1)S(1)}, u32[]{:S(2)}, u32[]{:S(2)}) async-start(bf16[4,128,512]{2,1,0:T(8,128)(2,1)} %add.277), calls=%async_computation.3 | async-start | bytes 1048576 | tf_op jit(solution)/shard_map/all_to_all | solution.py:23
  149.5 23.4 %all-to-all-start.5 = ((bf16[4,64,512]{2,1,0:T(8,128)(2,1)}), bf16[4,64,512]{2,1,0:T(8,128)(2,1)}, u32[]{:S(2)}, u32[]{:S(2)}) async-start(bf16[4,64,512]{2,1,0:T(8,128)(2,1)} %broadcast_in_dim.76), calls=%async_computation.5 | async-start | bytes 524288 | tf_op jit(solution)/shard_map/all_to_all | solution.py:23
  173.8 46.6 %copy-start.17 = (s32[1,1024]{1,0:T(1,128)S(1)}, s32[1,1024]{1,0:T(1,128)}, u32[]{:S(2)}) copy-start(s32[1,1024]{1,0:T(1,128)} %param.20) | copy-start | bytes 12292
  173.8 20.1 %all-to-all-start.4 = ((bf16[4,160,512]{2,1,0:T(8,128)(2,1)}), bf16[4,160,512]{2,1,0:T(8,128)(2,1)S(1)}, u32[]{:S(2)}, u32[]{:S(2)}) async-start(bf16[4,160,512]{2,1,0:T(8,128)(2,1)} %broadcast_in_dim.73), calls=%async_computation.4 | async-start | bytes 1310720 | tf_op jit(solution)/shard_map/all_to_all | solution.py:23
  180.1 36.5 %reduce-scatter.2.cloned.1.call-start = ((), (), s32[]{:S(2)}) async-start(), calls=%async_computation.17 | async-start | bytes 327680 | tf_op jit(solution)/shard_map/reduce_scatter | solution.py:140
  182.0 155.0 %all-gather.6.cloned.1.call-start = ((), (), s32[]{:S(2)}) async-start(), calls=%async_computation.18 | async-start | bytes 5570560 | tf_op jit(solution)/shard_map/all_gather | solution.py:142
  218.5 7.9 %collective-permute-start = (bf16[64,512]{1,0:T(8,128)(2,1)}, bf16[64,512]{1,0:T(8,128)(2,1)S(1)}, u32[]{:S(2)}, u32[]{:S(2)}) collective-permute-start(bf16[64,512]{1,0:T(8,128)(2,1)} %reduce_sum.82), channel_id=1, source_target_pairs={{496,0},{0,16},{16,32},{32,48},{48,64},{64,80},{80,96},{96,112},{1... | collective-permute-start | bytes 196616 | tf_op jit(solution)/shard_map/ppermute | solution.py:19
  256.2 45.8 %copy-start.18 = (s32[1,1024]{1,0:T(1,128)S(1)}, s32[1,1024]{1,0:T(1,128)}, u32[]{:S(2)}) copy-start(s32[1,1024]{1,0:T(1,128)} %param.20) | copy-start | bytes 12292
  256.3 4.7 collective-permute-start.2
  259.1 7.7 %collective-permute-start.1 = (bf16[64,512]{1,0:T(8,128)(2,1)S(1)}, bf16[64,512]{1,0:T(8,128)(2,1)S(1)}, u32[]{:S(2)}, u32[]{:S(2)}) collective-permute-start(bf16[64,512]{1,0:T(8,128)(2,1)S(1)} %reduce_sum.83), channel_id=1, source_target_pairs={{496,0},{0,16},{16,32},{32,48},{48,64},{64,80},{80,96},{96,112},{1... | collective-permute-start | bytes 196616 | tf_op jit(solution)/shard_map/ppermute | solution.py:19
  291.7 6.2 %collective-permute-start.3 = (bf16[64,512]{1,0:T(8,128)(2,1)S(1)}, bf16[64,512]{1,0:T(8,128)(2,1)S(1)}, u32[]{:S(2)}, u32[]{:S(2)}) collective-permute-start(bf16[64,512]{1,0:T(8,128)(2,1)S(1)} %reduce_sum.84), channel_id=1, source_target_pairs={{32,0},{48,16},{64,32},{80,48},{96,64},{112,80},{128,96},{144,112}... | collective-permute-start | bytes 196616 | tf_op jit(solution)/shard_map/ppermute | solution.py:19
  298.6 14.5 %all-to-all-start.8 = ((bf16[4,64,512]{2,1,0:T(8,128)(2,1)}), bf16[4,64,512]{2,1,0:T(8,128)(2,1)S(1)}, u32[]{:S(2)}, u32[]{:S(2)}) async-start(bf16[4,64,512]{2,1,0:T(8,128)(2,1)} %broadcast_in_dim.79), calls=%async_computation.8 | async-start | bytes 524288 | tf_op jit(solution)/shard_map/all_to_all | solution.py:23
  302.1 143.0 %all-gather.10.cloned.1.call-start = ((), (), s32[]{:S(2)}) async-start(), calls=%async_computation.20 | async-start | bytes 5570560 | tf_op jit(solution)/shard_map/all_gather | solution.py:167
  423.5 16.9 %all-to-all-start.14 = ((bf16[4,16,512]{2,1,0:T(8,128)(2,1)}), bf16[4,16,512]{2,1,0:T(8,128)(2,1)S(1)}, u32[]{:S(2)}, u32[]{:S(2)}) async-start(bf16[4,16,512]{2,1,0:T(8,128)(2,1)} %bitcast.59), calls=%async_computation.15 | async-start | bytes 131072 | tf_op jit(solution)/shard_map/all_to_all | solution.py:23
  440.4 8.5 %collective-permute-start.4 = (bf16[16,2048]{1,0:T(8,128)(2,1)S(1)}, bf16[16,2048]{1,0:T(8,128)(2,1)S(1)}, u32[]{:S(2)}, u32[]{:S(2)}) collective-permute-start(bf16[16,2048]{1,0:T(8,128)(2,1)S(1)} %bitcast.208), channel_id=1, source_target_pairs={{480,0},{496,16},{0,32},{16,48},{32,64},{48,80},{64,96},{80,112},{... | collective-permute-start | bytes 196616 | tf_op jit(solution)/shard_map/ppermute | solution.py:19
  451.9 7.7 %collective-permute-start.6 = (bf16[16,2048]{1,0:T(8,128)(2,1)S(1)}, bf16[16,2048]{1,0:T(8,128)(2,1)S(1)}, u32[]{:S(2)}, u32[]{:S(2)}) collective-permute-start(bf16[16,2048]{1,0:T(8,128)(2,1)S(1)} %fusion.4), channel_id=1, source_target_pairs={{496,0},{0,16},{16,32},{32,48},{48,64},{64,80},{80,96},{96,112},{1... | collective-permute-start | bytes 196616 | tf_op jit(solution)/shard_map/ppermute | solution.py:19
  453.8 7.6 %collective-permute-start.5 = (bf16[16,2048]{1,0:T(8,128)(2,1)S(1)}, bf16[16,2048]{1,0:T(8,128)(2,1)S(1)}, u32[]{:S(2)}, u32[]{:S(2)}) collective-permute-start(bf16[16,2048]{1,0:T(8,128)(2,1)S(1)} %fusion.4), channel_id=1, source_target_pairs={{16,0},{32,16},{48,32},{64,48},{80,64},{96,80},{112,96},{128,112},... | collective-permute-start | bytes 196616 | tf_op jit(solution)/shard_map/ppermute | solution.py:19
  464.4 7.7 %collective-permute-start.7 = (bf16[16,2048]{1,0:T(8,128)(2,1)S(1)}, bf16[16,2048]{1,0:T(8,128)(2,1)S(1)}, u32[]{:S(2)}, u32[]{:S(2)}) collective-permute-start(bf16[16,2048]{1,0:T(8,128)(2,1)S(1)} %fusion.5), channel_id=1, source_target_pairs={{16,0},{32,16},{48,32},{64,48},{80,64},{96,80},{112,96},{128,112},... | collective-permute-start | bytes 196616 | tf_op jit(solution)/shard_map/ppermute | solution.py:19
  475.7 20.0 %all-to-all-start.15 = ((bf16[16,2,16,128]{3,2,1,0:T(8,128)(2,1)}), bf16[16,2,16,128]{3,2,1,0:T(8,128)(2,1)S(1)}, u32[]{:S(2)}, u32[]{:S(2)}) async-start(bf16[16,2,16,128]{3,2,1,0:T(8,128)(2,1)} %maximum_bitcast_fusion.1), calls=%async_computation.16 | async-start | bytes 262144 | tf_op jit(solution)/shard_map/all_to_all | solution.py:23
  (18 other events, 279.5 us)
Sparse Core Ops, SparseCore 0:
  29.7 114.0 all-gather.7
  183.7 32.8 reduce-scatter.1
  218.9 110.9 all-gather.5
  344.0 100.9 all-gather.9

commit v6 on v3

--- a/solution.py
+++ b/solution.py
@@ -121,33 +121,36 @@
     unit = (rows[:, None] == K + jnp.arange(C, dtype=jnp.int32)[None]).astype(F32)
     section_rows = (after(unit, leaf_y) - product).astype(BF16)
 
-    gathered = lax.all_gather(jnp.concatenate([section_rows, coupling[0, 1]], axis=0), FRONT, axis=0)
-    section_all = gathered[:, :ks].reshape(fronts * ks, C)
-    node_coupling_all = gathered[:, ks:].reshape(K, C)
-
-    blocks = jnp.concatenate([node_w, node_v], axis=0).reshape(2 * ks, nb, K // nb).transpose(1, 0, 2)
+    section_all = lax.all_gather(section_rows, FRONT, axis=0, tiled=True)
+
+    blocks = node_w.reshape(ks, nb, K // nb).transpose(1, 0, 2)
     own_folded = folded(own)
     blocks = jnp.concatenate([blocks, jnp.broadcast_to(own_folded, (nb, *own_folded.shape))], axis=1)
     blocks = exchange(after(blocks, rest), "fb")
     w_block = blocks[:, :ks].reshape(nb * ks, K // nb)
-    v_block = blocks[:, ks : 2 * ks].reshape(nb * ks, K // nb)
-    own_block = unfolded(blocks[:, 2 * ks :]).reshape(nb * ks, R)
+    own_block = unfolded(blocks[:, ks:]).reshape(nb * ks, R)
+    v_parts = after(node_v, rest).reshape(ks, nb, K // nb).transpose(1, 0, 2)
+    v_parts = [lax.dynamic_index_in_dim(v_parts, (ib + d) % nb, keepdims=False) for d in range(nb)]
+    v_parts = [
+        lax.ppermute(part, "fb", [(i, (i + d) % nb) for i in range(nb)]) if d else part
+        for d, part in enumerate(v_parts)
+    ]
+    v_parts = jnp.stack([v_parts[-d % nb] for d in range(nb)])
 
     inverse_block = pivot_inverse[0, 1].reshape(kp, na, nb, kp).transpose(2, 0, 1, 3)
     inverse_block = exchange(inverse_block.reshape(nb, kp, na * kp), "fb")
     inverse_block = inverse_block.reshape(nb * kp, na * kp)
     block_rows = jnp.concatenate([stack_rows(ia * nb + b) for b in range(nb)])
     block_hit = (place[:C, None] == block_rows[None]).astype(BF16)
+    v_block = lax.dynamic_slice_in_dim(jnp.concatenate([v_parts, v_parts]), (nb - ib) % nb, nb)
     w_left = mm("cs,sk->ck", block_hit, w_block).astype(BF16)
     y_own = mm("sr,sk->rk", own_block, w_block)
 
     rest = after(rest, inverse_block)
-    node_reach = mm("pm,mc->pc", after(pivot_inverse[0, 1], rest), node_coupling_all).astype(BF16)
-    wide = jnp.concatenate([node_reach, coupling[0, 0], folded(leaf_y)], axis=0)
-    gathered = lax.all_gather(wide, FRONT, axis=0)
-    node_reach_all = gathered[:, :kp].reshape(K, C)
-    leaf_coupling_all = gathered[:, kp : 2 * kp].reshape(K, C)
-    leaf_y_all = unfolded(gathered[:, 2 * kp :]).reshape(na, nb, kp, R).transpose(1, 0, 2, 3).reshape(K, R)
+    wide = jnp.concatenate([coupling[0, 1], folded(leaf_y)], axis=0)
+    gathered = lax.all_gather(after(wide, rest), FRONT, axis=0)
+    node_coupling_all = gathered[:, :kp].reshape(K, C)
+    leaf_y_all = unfolded(gathered[:, kp:]).reshape(na, nb, kp, R).transpose(1, 0, 2, 3).reshape(K, R)
 
     device = jnp.where(place < K, place // kp, (place - K) // kc)
     within = jnp.where(place < K, place % kp, kp + (place - K) % kc)
@@ -163,10 +166,21 @@
     left = to_all(from_behind(rest, -(subtree // 2)), FRONT)
     left = left.reshape(na, nb, rc, C).transpose(1, 0, 2, 3).reshape(R, C)
 
-    partial_y = (y_own + mm("rc,ck->rk", left, w_left)).astype(BF16)
+    partial_y = (after(y_own, v_block) + mm("rc,ck->rk", left, w_left)).astype(BF16)
     part = total(exchange(partial_y.reshape(na, R // na, K // nb), "fa")).astype(BF16)
+    node_reach = mm("pm,mc->pc", after(pivot_inverse[0, 1], part), node_coupling_all).astype(BF16)
+    leaf_pivots = mm("pk,kr->pr", after(leaf_vectors_pivot[0, 0], part), leaf_y_all)
+    leaf_pivots = (leaf_pivot_block[0] - leaf_pivots).astype(BF16)
+    wide = jnp.concatenate([node_reach, coupling[0, 0], folded(leaf_pivots)], axis=0)
+    gathered = lax.all_gather(wide, FRONT, axis=0)
+    node_reach_all = gathered[:, :kp].reshape(K, C)
+    leaf_coupling_all = gathered[:, kp : 2 * kp].reshape(K, C)
+    leaf_pivots_all = unfolded(gathered[:, 2 * kp :]).reshape(K, R)
+    leaf_reach = mm("pm,mc->pc", pivot_inverse[0, 0], leaf_coupling_all).astype(BF16)
+    leaf_own = mm("pm,mr->pr", pivot_inverse[0, 0], leaf_pivots_all)
+
     y_block = to_all(part, "fa").reshape(R, K // nb)
-    part = mm("sk,rk->sr", v_block, y_block).astype(BF16).reshape(nb, ks, R)
+    part = mm("bsk,rk->bsr", v_block, y_block).astype(BF16)
     placed = mm("sc,rc->sr", own_hit[:, :C].astype(BF16), left)
     reflected = own.astype(F32) + placed - total(exchange(part, "fb"))
     reflected = reflected.astype(BF16)
@@ -177,21 +191,12 @@
     part = exchange(part.reshape(na, rc, nb * kp), "fa")
     top = part.transpose(1, 0, 2).reshape(rc, K)
 
-    leaf_reach = mm("pm,mc->pc", pivot_inverse[0, 0], leaf_coupling_all).astype(BF16)
-    leaf_pivots = leaf_pivot_block[0] - mm("pk,kr->pr", leaf_vectors_pivot[0, 0], leaf_y_all)
-    wide = jnp.concatenate([leaf_reach, folded(leaf_pivots.astype(BF16))], axis=0)
-    gathered = lax.all_gather(after(wide, y_block), FRONT, axis=0)
-    leaf_reach_all = gathered[:, :kp].reshape(K, C)
-    leaf_pivots_all = unfolded(gathered[:, kp:]).reshape(K, R)
-    leaf_own = mm("pm,mr->pr", pivot_inverse[0, 0], leaf_pivots_all)
-
     pivot_ids = jnp.arange(K, dtype=jnp.int32)[:, None]
     node_pick = (pivot_ids == parent_columns[0, 1][None]).astype(BF16)
     leaf_pick = (pivot_ids == parent_columns[0, 0][None]).astype(BF16)
 
-    def reached(parent, pick, reach):
-        chosen = mm("rp,pc->rc", parent, pick).astype(BF16)
-        return mm("rc,pc->rp", chosen, reach)
+    def chosen(parent, pick):
+        return mm("rp,pc->rc", parent, pick).astype(BF16)
 
     node = top
     for height in range(LEVELS, 0, -1):
@@ -200,14 +205,13 @@
         else:
             offset = 2 ** (height - 1)
             parent = added(from_behind(node, -offset), from_behind(node, offset))
-        node = (top - reached(parent, node_pick, node_reach_all)).astype(BF16)
-    parent = added(from_behind(node, -1), node)
-    leaf = reached(parent, leaf_pick, leaf_reach_all).astype(BF16)
-    both = jnp.stack([leaf, node]).reshape(2, rc, fronts, kp).transpose(2, 0, 1, 3)
-    both = exchange(both, FRONT).reshape(na, nb, 2, rc, kp)
-    both = both.transpose(2, 4, 1, 0, 3).reshape(2, kp, R)
-    leaf = (leaf_own - both[0]).astype(BF16)
-    return (jnp.stack([leaf, both[1]])[None], remainder[None])
+        node = (top - mm("rc,pc->rp", chosen(parent, node_pick), node_reach_all)).astype(BF16)
+    parent = chosen(added(from_behind(node, -1), node), leaf_pick)
+    both = node.reshape(rc, fronts, kp).transpose(1, 0, 2)
+    both = jnp.concatenate([both, jnp.broadcast_to(parent, (fronts, rc, C))], axis=2)
+    both = exchange(both, FRONT).reshape(na, nb, rc, kp + C).transpose(1, 0, 2, 3).reshape(R, kp + C)
+    leaf = (leaf_own - mm("pc,rc->pr", leaf_reach, both[:, kp:])).astype(BF16)
+    return (jnp.stack([leaf, both[:, :kp].T])[None], remainder[None])
 
 
 def solution(mesh):

time: 480 us -> 483 us (level)
  blocking collectives: 112 us -> 83.8 us
  starting transfers between devices: 83.1 us -> 101 us
  local copies, waits for them, and re-layouts: 33 us -> 42.1 us
  matrix products: 22.5 us -> 28.2 us
    all_to_all x6 -> x4, blocking collectives: 112 us -> 83.8 us  [exchange(): return lax.all_to_all(parts, axis, split_axis=0, concat_axis=0, tiled=True)]
    all_gather x2, waiting for transfers between devices: 27.1 us -> 0.02 us  [the longest x1 0.02 us: per_device(): gathered = lax.all_gather(after(wide, rest), FRONT, axis=0)]
    ppermute x0 -> x3, waiting for transfers between devices: none -> 20.2 us  [per_device(): lax.ppermute(part, 'fb', [(i, (i + d) % nb) for i in range(nb)])]
    all_to_all x8 -> x10, starting transfers between devices: 54.8 us -> 70.7 us  [exchange(): return lax.all_to_all(parts, axis, split_axis=0, concat_axis=0, tiled=True)]
    ppermute x0 -> x3, starting transfers between devices: none -> 10.7 us  [per_device(): lax.ppermute(part, 'fb', [(i, (i + d) % nb) for i in range(nb)])]
    ppermute x8, starting transfers between devices: 28.2 us -> 19.9 us  [from_behind(): lax.ppermute(block, 'leaf', [((i - distance) % count, i) for i in range(c...]
    dot_general x19, matrix products: 22.5 us -> 28.2 us  [mm(): return jnp.einsum(spec, a, b, preferred_element_type=F32)]
    all_to_all x8 -> x10, waiting for transfers between devices: 137 us -> 142 us  [exchange(): return lax.all_to_all(parts, axis, split_axis=0, concat_axis=0, tiled=True)]
  transfers between devices with their start and end apart: 20 -> 25, of which waited for: 14 -> 15; matrix products, arithmetic and copies ran while one was open for 9% -> 12% of each run, Pallas kernels for 0% -> 0%
where the time goes in v6:
time: 483 us; the launch traced here: 478 us
  waiting for transfers between devices  194 us (40%)
  starting transfers between devices  101 us (21%)
  blocking collectives  83.8 us (17%)
  local copies, waits for them, and re-layouts  42.1 us (9%)
  matrix products  28.2 us (6%)
  between operations  18.7 us (4%)
  other arithmetic  10.6 us (2%)
    all_to_all x10, waiting for transfers between devices, exchange(): return lax.all_to_all(parts, axis, split_axis=0, concat_axis=0, tiled=True)  142 us
    all_to_all x4, blocking collectives, exchange(): return lax.all_to_all(parts, axis, split_axis=0, concat_axis=0, tiled=True)  83.8 us
    all_to_all x10, starting transfers between devices, exchange(): return lax.all_to_all(parts, axis, split_axis=0, concat_axis=0, tiled=True)  70.7 us
    dot_general x19, matrix products, mm(): return jnp.einsum(spec, a, b, preferred_element_type=F32)  28.2 us
    all_gather x1, waiting for transfers between devices, per_device(): lax.all_gather(node_vectors_rest[0, 0], FRONT, axis=0, tiled=True)  20.5 us
    ppermute x3, waiting for transfers between devices, per_device(): lax.ppermute(part, 'fb', [(i, (i + d) % nb) for i in range(nb)])  20.2 us
    ppermute x8, starting transfers between devices, from_behind(): lax.ppermute(block, 'leaf', [((i - distance) % count, i) for i in range(c...  19.9 us
    ppermute x8, waiting for transfers between devices, from_behind(): lax.ppermute(block, 'leaf', [((i - distance) % count, i) for i in range(c...  11.3 us
  transfers between devices with their start and end apart: 25, of which 15 were waited for; matrix products, arithmetic and copies ran while one was open for 12% of the time, Pallas kernels for 0%

profile of v6, /device:TPU:24, one launch (start us, length us, event | category | flops | bytes accessed | tf_op | source)
XLA Modules:
  0.0 478.4 jit_solution(11090391346656051614)
XLA Ops:
  10.2 6.0 %all-to-all-start.1 = ((bf16[4,512,256]{2,1,0:T(8,128)(2,1)}), bf16[4,512,256]{2,1,0:T(8,128)(2,1)S(1)}, u32[]{:S(2)}, u32[]{:S(2)}) async-start(bf16[4,512,256]{2,1,0:T(8,128)(2,1)} %bitcast.16), calls=%async_computation.1 | async-start | bytes 2097152 | tf_op jit(solution)/shard_map/all_to_all | solution.py:23
  17.0 26.4 %all-to-all-done.1 = bf16[4,512,256]{2,1,0:T(8,128)(2,1)S(1)} async-done(((bf16[4,512,256]{2,1,0:T(8,128)(2,1)}), bf16[4,512,256]{2,1,0:T(8,128)(2,1)S(1)}, u32[]{:S(2)}, u32[]{:S(2)}) %all-to-all-start.1) | async-done | bytes 1048608 | tf_op jit(solution)/shard_map/all_to_all | solution.py:23
  44.3 14.5 %all-to-all-start.2 = ((bf16[4,128,256]{2,1,0:T(8,128)(2,1)}), bf16[4,128,256]{2,1,0:T(8,128)(2,1)S(1)}, u32[]{:S(2)}, u32[]{:S(2)}) async-start(bf16[4,128,256]{2,1,0:T(8,128)(2,1)} %bitcast.17), calls=%async_computation.2 | async-start | bytes 524288 | tf_op jit(solution)/shard_map/all_to_all | solution.py:23
  60.3 19.9 %all-to-all-done.2 = bf16[4,128,256]{2,1,0:T(8,128)(2,1)S(1)} async-done(((bf16[4,128,256]{2,1,0:T(8,128)(2,1)}), bf16[4,128,256]{2,1,0:T(8,128)(2,1)S(1)}, u32[]{:S(2)}, u32[]{:S(2)}) %all-to-all-start.2) | async-done | bytes 262176 | tf_op jit(solution)/shard_map/all_to_all | solution.py:23
  81.4 20.5 %all-gather.11.cloned.1.call-done = bf16[1,1,512,2048]{3,2,1,0:T(8,128)(2,1)} async-done(((bf16[1,1,32,2048]{3,2,1,0:T(8,128)(2,1)}), bf16[1,1,512,2048]{3,2,1,0:T(8,128)(2,1)}) %all-gather.11.cloned.1.call-update) | async-done | bytes 2097168 | tf_op jit(solution)/shard_map/all_gather | solution.py:100
  107.3 7.7 %all-to-all-start = ((bf16[16,16,448]{2,1,0:T(8,128)(2,1)}), bf16[16,16,448]{2,1,0:T(8,128)(2,1)S(1)}, u32[]{:S(2)}, u32[]{:S(2)}) async-start(bf16[16,16,448]{2,1,0:T(8,128)(2,1)} %bitcast.11), calls=%async_computation | async-start | bytes 524288 | tf_op jit(solution)/shard_map/all_to_all | solution.py:23
  116.1 12.8 %all-to-all-done = bf16[16,16,448]{2,1,0:T(8,128)(2,1)S(1)} async-done(((bf16[16,16,448]{2,1,0:T(8,128)(2,1)}), bf16[16,16,448]{2,1,0:T(8,128)(2,1)S(1)}, u32[]{:S(2)}, u32[]{:S(2)}) %all-to-all-start) | async-done | bytes 229408 | tf_op jit(solution)/shard_map/all_to_all | solution.py:23
  128.9 6.6 %all-to-all-start.5 = ((bf16[4,128,512]{1,2,0:T(8,128)(2,1)}), bf16[4,128,512]{1,2,0:T(8,128)(2,1)S(1)}, u32[]{:S(2)}, u32[]{:S(2)}) async-start(bf16[4,128,512]{1,2,0:T(8,128)(2,1)} %bitcast.35), calls=%async_computation.5 | async-start | bytes 1048576 | tf_op jit(solution)/shard_map/all_to_all | solution.py:23
  136.7 13.1 %all-to-all-done.5 = bf16[4,128,512]{1,2,0:T(8,128)(2,1)S(1)} async-done(((bf16[4,128,512]{1,2,0:T(8,128)(2,1)}), bf16[4,128,512]{1,2,0:T(8,128)(2,1)S(1)}, u32[]{:S(2)}, u32[]{:S(2)}) %all-to-all-start.5) | async-done | bytes 524320 | tf_op jit(solution)/shard_map/all_to_all | solution.py:23
  149.8 7.6 %all-to-all-start.3 = ((bf16[16,16,512]{2,1,0:T(8,128)(2,1)}), bf16[16,16,512]{2,1,0:T(8,128)(2,1)S(1)}, u32[]{:S(2)}, u32[]{:S(2)}) async-start(bf16[16,16,512]{2,1,0:T(8,128)(2,1)} %bitcast.22), calls=%async_computation.3 | async-start | bytes 524288 | tf_op jit(solution)/shard_map/all_to_all | solution.py:23
  160.8 12.4 %all-to-all-done.3 = bf16[16,16,512]{2,1,0:T(8,128)(2,1)S(1)} async-done(((bf16[16,16,512]{2,1,0:T(8,128)(2,1)}), bf16[16,16,512]{2,1,0:T(8,128)(2,1)S(1)}, u32[]{:S(2)}, u32[]{:S(2)}) %all-to-all-start.3) | async-done | bytes 262176 | tf_op jit(solution)/shard_map/all_to_all | solution.py:23
  190.9 5.7 %collective-permute-start = (bf16[160,512]{1,0:T(8,128)(2,1)}, bf16[160,512]{1,0:T(8,128)(2,1)S(1)}, u32[]{:S(2)}, u32[]{:S(2)}) collective-permute-start(bf16[160,512]{1,0:T(8,128)(2,1)} %get-tuple-element.28), channel_id=1, source_target_pairs={{0,3},{1,0},{2,1},{3,2},{4,7},{5,4},{6,5},{7,6},{8,11},{9,8},{10,9... | collective-permute-start | bytes 491528 | tf_op jit(solution)/shard_map/ppermute | solution.py:135
  203.8 20.2 %collective-permute-done.1 = bf16[160,512]{1,0:T(8,128)(2,1)S(1)} collective-permute-done((bf16[160,512]{1,0:T(8,128)(2,1)S(1)}, bf16[160,512]{1,0:T(8,128)(2,1)S(1)}, u32[]{:S(2)}, u32[]{:S(2)}) %collective-permute-start.1) | collective-permute-done | bytes 163872 | tf_op jit(solution)/shard_map/ppermute | solution.py:135
  237.0 5.8 %collective-permute-start.5 = (bf16[16,512]{1,0:T(8,128)(2,1)S(1)}, bf16[16,512]{1,0:T(8,128)(2,1)S(1)}, u32[]{:S(2)}, u32[]{:S(2)}) collective-permute-start(bf16[16,512]{1,0:T(8,128)(2,1)S(1)} %fusion.39), channel_id=1, source_target_pairs={{16,0},{32,16},{48,32},{64,48},{80,64},{96,80},{112,96},{128,112},... | collective-permute-start | bytes 49160 | tf_op jit(solution)/shard_map/ppermute | solution.py:19
  252.3 6.7 %all-to-all-start.6 = ((bf16[16,16,512]{2,1,0:T(8,128)(2,1)}), bf16[16,16,512]{2,1,0:T(8,128)(2,1)S(1)}, u32[]{:S(2)}, u32[]{:S(2)}) async-start(bf16[16,16,512]{2,1,0:T(8,128)(2,1)} %broadcast_in_dim.63), calls=%async_computation.6 | async-start | bytes 524288 | tf_op jit(solution)/shard_map/all_to_all | solution.py:23
  267.5 8.4 %all-to-all-done.6 = bf16[16,16,512]{2,1,0:T(8,128)(2,1)S(1)} async-done(((bf16[16,16,512]{2,1,0:T(8,128)(2,1)}), bf16[16,16,512]{2,1,0:T(8,128)(2,1)S(1)}, u32[]{:S(2)}, u32[]{:S(2)}) %all-to-all-start.6) | async-done | bytes 262176 | tf_op jit(solution)/shard_map/all_to_all | solution.py:23
  277.4 9.0 %all-to-all-start.7 = ((bf16[4,64,512]{2,1,0:T(8,128)(2,1)}), bf16[4,64,512]{2,1,0:T(8,128)(2,1)S(1)}, u32[]{:S(2)}, u32[]{:S(2)}) async-start(bf16[4,64,512]{2,1,0:T(8,128)(2,1)} %bitcast.51), calls=%async_computation.7 | async-start | bytes 524288 | tf_op jit(solution)/shard_map/all_to_all | solution.py:23
  286.7 18.4 %all-to-all-done.7 = bf16[4,64,512]{2,1,0:T(8,128)(2,1)S(1)} async-done(((bf16[4,64,512]{2,1,0:T(8,128)(2,1)}), bf16[4,64,512]{2,1,0:T(8,128)(2,1)S(1)}, u32[]{:S(2)}, u32[]{:S(2)}) %all-to-all-start.7) | async-done | bytes 262176 | tf_op jit(solution)/shard_map/all_to_all | solution.py:23
  311.2 24.8 %all_to_all.70 = bf16[4,64,512]{2,1,0:T(8,128)(2,1)S(1)} all-to-all(bf16[4,64,512]{2,1,0:T(8,128)(2,1)S(1)} %broadcast_in_dim.64), channel_id=1, replica_groups=mesh['leaf'=32,'fa'=4,'fb'=4] {'fa'}, dimensions={0} | all-to-all | bytes 524288 | tf_op jit(solution)/shard_map/all_to_all | solution.py:23
  337.4 18.9 %all_to_all.71 = bf16[4,160,256]{2,1,0:T(8,128)(2,1)S(1)} all-to-all(bf16[4,160,256]{2,1,0:T(8,128)(2,1)S(1)} %convolution_convert_fusion), channel_id=1, replica_groups=mesh['leaf'=32,'fa'=4,'fb'=4] {'fb'}, dimensions={0} | all-to-all | bytes 655360 | tf_op jit(solution)/shard_map/all_to_all | solution.py:23
  356.7 26.6 %all_to_all.72 = bf16[4,128,256]{2,1,0:T(8,128)(2,1)S(1)} all-to-all(bf16[4,128,256]{2,1,0:T(8,128)(2,1)S(1)} %broadcast_in_dim.65), channel_id=1, replica_groups=mesh['leaf'=32,'fa'=4,'fb'=4] {'fa'}, dimensions={0} | all-to-all | bytes 524288 | tf_op jit(solution)/shard_map/all_to_all | solution.py:23
  383.6 13.6 %all_to_all.73 = bf16[4,64,512]{2,1,0:T(8,128)(2,1)S(1)} all-to-all(bf16[4,64,512]{2,1,0:T(8,128)(2,1)S(1)} %bitcast.217), channel_id=1, replica_groups=mesh['leaf'=32,'fa'=4,'fb'=4] {'fb'}, dimensions={0} | all-to-all | bytes 524288 | tf_op jit(solution)/shard_map/all_to_all | solution.py:23
  401.2 13.2 %all-to-all-done.12 = bf16[4,16,512]{2,1,0:T(8,128)(2,1)S(1)} async-done(((bf16[4,16,512]{2,1,0:T(8,128)(2,1)}), bf16[4,16,512]{2,1,0:T(8,128)(2,1)S(1)}, u32[]{:S(2)}, u32[]{:S(2)}) %all-to-all-start.12) | async-done | bytes 65568 | tf_op jit(solution)/shard_map/all_to_all | solution.py:23
  451.3 17.0 %all-to-all-done.13 = bf16[16,16,640]{2,1,0:T(8,128)(2,1)S(1)} async-done(((bf16[16,16,640]{2,1,0:T(8,128)(2,1)}), bf16[16,16,640]{2,1,0:T(8,128)(2,1)S(1)}, u32[]{:S(2)}, u32[]{:S(2)}) %all-to-all-start.13) | async-done | bytes 327712 | tf_op jit(solution)/shard_map/all_to_all | solution.py:23
  (207 shorter events, 124.0 us)
Async XLA Ops:
  10.2 33.2 %all-to-all-start.1 = ((bf16[4,512,256]{2,1,0:T(8,128)(2,1)}), bf16[4,512,256]{2,1,0:T(8,128)(2,1)S(1)}, u32[]{:S(2)}, u32[]{:S(2)}) async-start(bf16[4,512,256]{2,1,0:T(8,128)(2,1)} %bitcast.16), calls=%async_computation.1 | async-start | bytes 2097152 | tf_op jit(solution)/shard_map/all_to_all | solution.py:23
  16.3 85.6 %all-gather.11.cloned.1.call-start = ((), (), s32[]{:S(2)}) async-start(), calls=%async_computation.16 | async-start | bytes 2228224 | tf_op jit(solution)/shard_map/all_gather | solution.py:100
  44.3 35.9 %all-to-all-start.2 = ((bf16[4,128,256]{2,1,0:T(8,128)(2,1)}), bf16[4,128,256]{2,1,0:T(8,128)(2,1)S(1)}, u32[]{:S(2)}, u32[]{:S(2)}) async-start(bf16[4,128,256]{2,1,0:T(8,128)(2,1)} %bitcast.17), calls=%async_computation.2 | async-start | bytes 524288 | tf_op jit(solution)/shard_map/all_to_all | solution.py:23
  58.8 166.3 %all-gather.7.cloned.1.call-start = ((), (), s32[]{:S(2)}) async-start(), calls=%async_computation.14 | async-start | bytes 2785280 | tf_op jit(solution)/shard_map/all_gather | solution.py:124
  107.3 21.6 %all-to-all-start = ((bf16[16,16,448]{2,1,0:T(8,128)(2,1)}), bf16[16,16,448]{2,1,0:T(8,128)(2,1)S(1)}, u32[]{:S(2)}, u32[]{:S(2)}) async-start(bf16[16,16,448]{2,1,0:T(8,128)(2,1)} %bitcast.11), calls=%async_computation | async-start | bytes 524288 | tf_op jit(solution)/shard_map/all_to_all | solution.py:23
  128.9 20.9 %all-to-all-start.5 = ((bf16[4,128,512]{1,2,0:T(8,128)(2,1)}), bf16[4,128,512]{1,2,0:T(8,128)(2,1)S(1)}, u32[]{:S(2)}, u32[]{:S(2)}) async-start(bf16[4,128,512]{1,2,0:T(8,128)(2,1)} %bitcast.35), calls=%async_computation.5 | async-start | bytes 1048576 | tf_op jit(solution)/shard_map/all_to_all | solution.py:23
  149.8 23.4 %all-to-all-start.3 = ((bf16[16,16,512]{2,1,0:T(8,128)(2,1)}), bf16[16,16,512]{2,1,0:T(8,128)(2,1)S(1)}, u32[]{:S(2)}, u32[]{:S(2)}) async-start(bf16[16,16,512]{2,1,0:T(8,128)(2,1)} %bitcast.22), calls=%async_computation.3 | async-start | bytes 524288 | tf_op jit(solution)/shard_map/all_to_all | solution.py:23
  157.4 149.0 %all-gather.9.cloned.1.call-start = ((), (), s32[]{:S(2)}) async-start(), calls=%async_computation.15 | async-start | bytes 3342336 | tf_op jit(solution)/shard_map/all_gather | solution.py:151
  182.6 67.1 %all-to-all-start.4 = ((bf16[4,240,512]{2,1,0:T(8,128)(2,1)}), bf16[4,240,512]{2,1,0:T(8,128)(2,1)}, u32[]{:S(2)}, u32[]{:S(2)}) async-start(bf16[4,240,512]{2,1,0:T(8,128)(2,1)} %maximum_add_fusion), calls=%async_computation.4 | async-start | bytes 1966080 | tf_op jit(solution)/shard_map/all_to_all | solution.py:23
  188.0 45.5 %collective-permute-start.3 = (bf16[16,512]{1,0:T(8,128)(2,1)}, bf16[16,512]{1,0:T(8,128)(2,1)}, u32[]{:S(2)}, u32[]{:S(2)}) collective-permute-start(bf16[16,512]{1,0:T(8,128)(2,1)} %get-tuple-element.14), channel_id=1, source_target_pairs={{496,0},{0,16},{16,32},{32,48},{48,64},{64,80},{80,96},{96,112},{1... | collective-permute-start | bytes 49160 | tf_op jit(solution)/shard_map/ppermute | solution.py:19
  190.9 12.9 %collective-permute-start = (bf16[160,512]{1,0:T(8,128)(2,1)}, bf16[160,512]{1,0:T(8,128)(2,1)S(1)}, u32[]{:S(2)}, u32[]{:S(2)}) collective-permute-start(bf16[160,512]{1,0:T(8,128)(2,1)} %get-tuple-element.28), channel_id=1, source_target_pairs={{0,3},{1,0},{2,1},{3,2},{4,7},{5,4},{6,5},{7,6},{8,11},{9,8},{10,9... | collective-permute-start | bytes 491528 | tf_op jit(solution)/shard_map/ppermute | solution.py:135
  198.8 25.2 %collective-permute-start.1 = (bf16[160,512]{1,0:T(8,128)(2,1)S(1)}, bf16[160,512]{1,0:T(8,128)(2,1)S(1)}, u32[]{:S(2)}, u32[]{:S(2)}) collective-permute-start(bf16[160,512]{1,0:T(8,128)(2,1)S(1)} %get-tuple-element.27), channel_id=1, source_target_pairs={{0,2},{1,3},{2,0},{3,1},{4,6},{5,7},{6,4},{7,5},{8,10},{9,11},{10,... | collective-permute-start | bytes 491528 | tf_op jit(solution)/shard_map/ppermute | solution.py:135
  200.7 42.0 %collective-permute-start.2 = (bf16[160,512]{1,0:T(8,128)(2,1)}, bf16[160,512]{1,0:T(8,128)(2,1)}, u32[]{:S(2)}, u32[]{:S(2)}) collective-permute-start(bf16[160,512]{1,0:T(8,128)(2,1)} %get-tuple-element.26), channel_id=1, source_target_pairs={{0,1},{1,2},{2,3},{3,0},{4,5},{5,6},{6,7},{7,4},{8,9},{9,10},{10,1... | collective-permute-start | bytes 491528 | tf_op jit(solution)/shard_map/ppermute | solution.py:135
  235.1 9.3 %collective-permute-start.4 = (bf16[16,512]{1,0:T(8,128)(2,1)S(1)}, bf16[16,512]{1,0:T(8,128)(2,1)S(1)}, u32[]{:S(2)}, u32[]{:S(2)}) collective-permute-start(bf16[16,512]{1,0:T(8,128)(2,1)S(1)} %fusion.39), channel_id=1, source_target_pairs={{496,0},{0,16},{16,32},{32,48},{48,64},{64,80},{80,96},{96,112},{1... | collective-permute-start | bytes 49160 | tf_op jit(solution)/shard_map/ppermute | solution.py:19
  237.0 7.4 %collective-permute-start.5 = (bf16[16,512]{1,0:T(8,128)(2,1)S(1)}, bf16[16,512]{1,0:T(8,128)(2,1)S(1)}, u32[]{:S(2)}, u32[]{:S(2)}) collective-permute-start(bf16[16,512]{1,0:T(8,128)(2,1)S(1)} %fusion.39), channel_id=1, source_target_pairs={{16,0},{32,16},{48,32},{64,48},{80,64},{96,80},{112,96},{128,112},... | collective-permute-start | bytes 49160 | tf_op jit(solution)/shard_map/ppermute | solution.py:19
  245.9 5.6 %collective-permute-start.6 = (bf16[16,512]{1,0:T(8,128)(2,1)S(1)}, bf16[16,512]{1,0:T(8,128)(2,1)S(1)}, u32[]{:S(2)}, u32[]{:S(2)}) collective-permute-start(bf16[16,512]{1,0:T(8,128)(2,1)S(1)} %fusion.40), channel_id=1, source_target_pairs={{32,0},{48,16},{64,32},{80,48},{96,64},{112,80},{128,96},{144,112}... | collective-permute-start | bytes 49160 | tf_op jit(solution)/shard_map/ppermute | solution.py:19
  252.3 23.6 %all-to-all-start.6 = ((bf16[16,16,512]{2,1,0:T(8,128)(2,1)}), bf16[16,16,512]{2,1,0:T(8,128)(2,1)S(1)}, u32[]{:S(2)}, u32[]{:S(2)}) async-start(bf16[16,16,512]{2,1,0:T(8,128)(2,1)} %broadcast_in_dim.63), calls=%async_computation.6 | async-start | bytes 524288 | tf_op jit(solution)/shard_map/all_to_all | solution.py:23
  277.4 27.7 %all-to-all-start.7 = ((bf16[4,64,512]{2,1,0:T(8,128)(2,1)}), bf16[4,64,512]{2,1,0:T(8,128)(2,1)S(1)}, u32[]{:S(2)}, u32[]{:S(2)}) async-start(bf16[4,64,512]{2,1,0:T(8,128)(2,1)} %bitcast.51), calls=%async_computation.7 | async-start | bytes 524288 | tf_op jit(solution)/shard_map/all_to_all | solution.py:23
  286.5 129.8 %all-gather.13.cloned.1.call-start = ((), (), s32[]{:S(2)}) async-start(), calls=%async_computation.17 | async-start | bytes 5570560 | tf_op jit(solution)/shard_map/all_gather | solution.py:175
  397.9 16.5 %all-to-all-start.12 = ((bf16[4,16,512]{2,1,0:T(8,128)(2,1)}), bf16[4,16,512]{2,1,0:T(8,128)(2,1)S(1)}, u32[]{:S(2)}, u32[]{:S(2)}) async-start(bf16[4,16,512]{2,1,0:T(8,128)(2,1)} %bitcast.71), calls=%async_computation.12 | async-start | bytes 131072 | tf_op jit(solution)/shard_map/all_to_all | solution.py:23
  414.4 8.3 %collective-permute-start.7 = (bf16[16,2048]{1,0:T(8,128)(2,1)S(1)}, bf16[16,2048]{1,0:T(8,128)(2,1)S(1)}, u32[]{:S(2)}, u32[]{:S(2)}) collective-permute-start(bf16[16,2048]{1,0:T(8,128)(2,1)S(1)} %bitcast.228), channel_id=1, source_target_pairs={{480,0},{496,16},{0,32},{16,48},{32,64},{48,80},{64,96},{80,112},{... | collective-permute-start | bytes 196616 | tf_op jit(solution)/shard_map/ppermute | solution.py:19
  425.5 4.4 collective-permute-start.8
  427.5 7.7 %collective-permute-start.9 = (bf16[16,2048]{1,0:T(8,128)(2,1)S(1)}, bf16[16,2048]{1,0:T(8,128)(2,1)S(1)}, u32[]{:S(2)}, u32[]{:S(2)}) collective-permute-start(bf16[16,2048]{1,0:T(8,128)(2,1)S(1)} %fusion.4), channel_id=1, source_target_pairs={{496,0},{0,16},{16,32},{32,48},{48,64},{64,80},{80,96},{96,112},{1... | collective-permute-start | bytes 196616 | tf_op jit(solution)/shard_map/ppermute | solution.py:19
  443.5 24.9 %all-to-all-start.13 = ((bf16[16,16,640]{2,1,0:T(8,128)(2,1)}), bf16[16,16,640]{2,1,0:T(8,128)(2,1)S(1)}, u32[]{:S(2)}, u32[]{:S(2)}) async-start(bf16[16,16,640]{2,1,0:T(8,128)(2,1)} %pad_maximum_fusion.2), calls=%async_computation.13 | async-start | bytes 655360 | tf_op jit(solution)/shard_map/all_to_all | solution.py:23
  (26 other events, 365.7 us)
Sparse Core Ops, SparseCore 0:
  19.2 82.6 all-gather.10
  105.2 86.3 all-gather.6
  193.7 83.0 all-gather.8
  311.2 103.5 all-gather.12

commit v7 on v6

--- a/solution.py
+++ b/solution.py
@@ -123,34 +123,28 @@
 
     section_all = lax.all_gather(section_rows, FRONT, axis=0, tiled=True)
 
-    blocks = node_w.reshape(ks, nb, K // nb).transpose(1, 0, 2)
+    blocks = jnp.concatenate([node_w, node_v], axis=0).reshape(2 * ks, nb, K // nb).transpose(1, 0, 2)
     own_folded = folded(own)
     blocks = jnp.concatenate([blocks, jnp.broadcast_to(own_folded, (nb, *own_folded.shape))], axis=1)
     blocks = exchange(after(blocks, rest), "fb")
     w_block = blocks[:, :ks].reshape(nb * ks, K // nb)
-    own_block = unfolded(blocks[:, ks:]).reshape(nb * ks, R)
-    v_parts = after(node_v, rest).reshape(ks, nb, K // nb).transpose(1, 0, 2)
-    v_parts = [lax.dynamic_index_in_dim(v_parts, (ib + d) % nb, keepdims=False) for d in range(nb)]
-    v_parts = [
-        lax.ppermute(part, "fb", [(i, (i + d) % nb) for i in range(nb)]) if d else part
-        for d, part in enumerate(v_parts)
-    ]
-    v_parts = jnp.stack([v_parts[-d % nb] for d in range(nb)])
+    v_block = blocks[:, ks : 2 * ks]
+    own_block = unfolded(blocks[:, 2 * ks :]).reshape(nb * ks, R)
 
     inverse_block = pivot_inverse[0, 1].reshape(kp, na, nb, kp).transpose(2, 0, 1, 3)
     inverse_block = exchange(inverse_block.reshape(nb, kp, na * kp), "fb")
     inverse_block = inverse_block.reshape(nb * kp, na * kp)
     block_rows = jnp.concatenate([stack_rows(ia * nb + b) for b in range(nb)])
     block_hit = (place[:C, None] == block_rows[None]).astype(BF16)
-    v_block = lax.dynamic_slice_in_dim(jnp.concatenate([v_parts, v_parts]), (nb - ib) % nb, nb)
     w_left = mm("cs,sk->ck", block_hit, w_block).astype(BF16)
     y_own = mm("sr,sk->rk", own_block, w_block)
 
     rest = after(rest, inverse_block)
-    wide = jnp.concatenate([coupling[0, 1], folded(leaf_y)], axis=0)
+    wide = jnp.concatenate([coupling[0, 1], coupling[0, 0], folded(leaf_y)], axis=0)
     gathered = lax.all_gather(after(wide, rest), FRONT, axis=0)
     node_coupling_all = gathered[:, :kp].reshape(K, C)
-    leaf_y_all = unfolded(gathered[:, kp:]).reshape(na, nb, kp, R).transpose(1, 0, 2, 3).reshape(K, R)
+    leaf_coupling_all = gathered[:, kp : 2 * kp].reshape(K, C)
+    leaf_y_all = unfolded(gathered[:, 2 * kp :]).reshape(na, nb, kp, R).transpose(1, 0, 2, 3).reshape(K, R)
 
     device = jnp.where(place < K, place // kp, (place - K) // kc)
     within = jnp.where(place < K, place % kp, kp + (place - K) % kc)
@@ -166,16 +160,15 @@
     left = to_all(from_behind(rest, -(subtree // 2)), FRONT)
     left = left.reshape(na, nb, rc, C).transpose(1, 0, 2, 3).reshape(R, C)
 
-    partial_y = (after(y_own, v_block) + mm("rc,ck->rk", left, w_left)).astype(BF16)
+    partial_y = (y_own + mm("rc,ck->rk", left, w_left)).astype(BF16)
     part = total(exchange(partial_y.reshape(na, R // na, K // nb), "fa")).astype(BF16)
     node_reach = mm("pm,mc->pc", after(pivot_inverse[0, 1], part), node_coupling_all).astype(BF16)
     leaf_pivots = mm("pk,kr->pr", after(leaf_vectors_pivot[0, 0], part), leaf_y_all)
     leaf_pivots = (leaf_pivot_block[0] - leaf_pivots).astype(BF16)
-    wide = jnp.concatenate([node_reach, coupling[0, 0], folded(leaf_pivots)], axis=0)
+    wide = jnp.concatenate([node_reach, folded(leaf_pivots)], axis=0)
     gathered = lax.all_gather(wide, FRONT, axis=0)
     node_reach_all = gathered[:, :kp].reshape(K, C)
-    leaf_coupling_all = gathered[:, kp : 2 * kp].reshape(K, C)
-    leaf_pivots_all = unfolded(gathered[:, 2 * kp :]).reshape(K, R)
+    leaf_pivots_all = unfolded(gathered[:, kp:]).reshape(K, R)
     leaf_reach = mm("pm,mc->pc", pivot_inverse[0, 0], leaf_coupling_all).astype(BF16)
     leaf_own = mm("pm,mr->pr", pivot_inverse[0, 0], leaf_pivots_all)
 

time: 483 us -> 466 us (0.965)
  starting transfers between devices: 101 us -> 88.7 us
  local copies, waits for them, and re-layouts: 42.1 us -> 30.9 us
  blocking collectives: 83.8 us -> 92.7 us
    ppermute x3 -> x0, waiting for transfers between devices: 20.2 us -> none  [per_device(): lax.ppermute(part, 'fb', [(i, (i + d) % nb) for i in range(nb)])]
    all_gather x1, waiting for transfers between devices: 0.02 us -> 19 us  [per_device(): gathered = lax.all_gather(after(wide, rest), FRONT, axis=0)]
    ppermute x3 -> x0, starting transfers between devices: 10.7 us -> none  [per_device(): lax.ppermute(part, 'fb', [(i, (i + d) % nb) for i in range(nb)])]
    all_to_all x10 -> x9, starting transfers between devices: 70.7 us -> 60.6 us  [exchange(): return lax.all_to_all(parts, axis, split_axis=0, concat_axis=0, tiled=True)]
    all_to_all x4 -> x5, blocking collectives: 83.8 us -> 92.7 us  [exchange(): return lax.all_to_all(parts, axis, split_axis=0, concat_axis=0, tiled=True)]
    ppermute x8, starting transfers between devices: 19.9 us -> 28 us  [from_behind(): lax.ppermute(block, 'leaf', [((i - distance) % count, i) for i in range(c...]
    all_to_all x10 -> x9, waiting for transfers between devices: 142 us -> 142 us  [exchange(): return lax.all_to_all(parts, axis, split_axis=0, concat_axis=0, tiled=True)]
  transfers between devices with their start and end apart: 25 -> 21, of which waited for: 15 -> 17; matrix products, arithmetic and copies ran while one was open for 12% -> 10% of each run, Pallas kernels for 0% -> 0%
where the time goes in v7:
time: 466 us; the launch traced here: 461 us
  waiting for transfers between devices  197 us (42%)
  blocking collectives  92.7 us (20%)
  starting transfers between devices  88.7 us (19%)
  local copies, waits for them, and re-layouts  30.9 us (7%)
  matrix products  24.4 us (5%)
  between operations  17.9 us (4%)
  other arithmetic  9.22 us (2%)
    all_to_all x9, waiting for transfers between devices, exchange(): return lax.all_to_all(parts, axis, split_axis=0, concat_axis=0, tiled=True)  142 us
    all_to_all x5, blocking collectives, exchange(): return lax.all_to_all(parts, axis, split_axis=0, concat_axis=0, tiled=True)  92.7 us
    all_to_all x9, starting transfers between devices, exchange(): return lax.all_to_all(parts, axis, split_axis=0, concat_axis=0, tiled=True)  60.6 us
    ppermute x8, starting transfers between devices, from_behind(): lax.ppermute(block, 'leaf', [((i - distance) % count, i) for i in range(c...  28 us
    dot_general x19, matrix products, mm(): return jnp.einsum(spec, a, b, preferred_element_type=F32)  24.4 us
    all_gather x1, waiting for transfers between devices, per_device(): lax.all_gather(node_vectors_rest[0, 0], FRONT, axis=0, tiled=True)  20 us
    all_gather x1, waiting for transfers between devices, per_device(): gathered = lax.all_gather(after(wide, rest), FRONT, axis=0)  19 us
    ppermute x8, waiting for transfers between devices, from_behind(): lax.ppermute(block, 'leaf', [((i - distance) % count, i) for i in range(c...  15 us
  transfers between devices with their start and end apart: 21, of which 17 were waited for; matrix products, arithmetic and copies ran while one was open for 10% of the time, Pallas kernels for 0%

profile of v7, /device:TPU:24, one launch (start us, length us, event | category | flops | bytes accessed | tf_op | source)
XLA Modules:
  0.0 460.5 jit_solution(1288394440011880166)
XLA Ops:
  10.2 5.9 %all-to-all-start.1 = ((bf16[4,512,256]{2,1,0:T(8,128)(2,1)}), bf16[4,512,256]{2,1,0:T(8,128)(2,1)S(1)}, u32[]{:S(2)}, u32[]{:S(2)}) async-start(bf16[4,512,256]{2,1,0:T(8,128)(2,1)} %bitcast.17), calls=%async_computation.1 | async-start | bytes 2097152 | tf_op jit(solution)/shard_map/all_to_all | solution.py:23
  17.1 26.1 %all-to-all-done.1 = bf16[4,512,256]{2,1,0:T(8,128)(2,1)S(1)} async-done(((bf16[4,512,256]{2,1,0:T(8,128)(2,1)}), bf16[4,512,256]{2,1,0:T(8,128)(2,1)S(1)}, u32[]{:S(2)}, u32[]{:S(2)}) %all-to-all-start.1) | async-done | bytes 1048608 | tf_op jit(solution)/shard_map/all_to_all | solution.py:23
  44.2 14.5 %all-to-all-start.2 = ((bf16[4,128,256]{2,1,0:T(8,128)(2,1)}), bf16[4,128,256]{2,1,0:T(8,128)(2,1)S(1)}, u32[]{:S(2)}, u32[]{:S(2)}) async-start(bf16[4,128,256]{2,1,0:T(8,128)(2,1)} %bitcast.18), calls=%async_computation.2 | async-start | bytes 524288 | tf_op jit(solution)/shard_map/all_to_all | solution.py:23
  60.3 20.0 %all-to-all-done.2 = bf16[4,128,256]{2,1,0:T(8,128)(2,1)S(1)} async-done(((bf16[4,128,256]{2,1,0:T(8,128)(2,1)}), bf16[4,128,256]{2,1,0:T(8,128)(2,1)S(1)}, u32[]{:S(2)}, u32[]{:S(2)}) %all-to-all-start.2) | async-done | bytes 262176 | tf_op jit(solution)/shard_map/all_to_all | solution.py:23
  81.5 20.0 %all-gather.11.cloned.1.call-done = bf16[1,1,512,2048]{3,2,1,0:T(8,128)(2,1)} async-done(((bf16[1,1,32,2048]{3,2,1,0:T(8,128)(2,1)}), bf16[1,1,512,2048]{3,2,1,0:T(8,128)(2,1)}) %all-gather.11.cloned.1.call-update) | async-done | bytes 2097168 | tf_op jit(solution)/shard_map/all_gather | solution.py:100
  107.0 7.5 %all-to-all-start = ((bf16[16,16,448]{2,1,0:T(8,128)(2,1)}), bf16[16,16,448]{2,1,0:T(8,128)(2,1)S(1)}, u32[]{:S(2)}, u32[]{:S(2)}) async-start(bf16[16,16,448]{2,1,0:T(8,128)(2,1)} %bitcast.12), calls=%async_computation | async-start | bytes 524288 | tf_op jit(solution)/shard_map/all_to_all | solution.py:23
  115.6 12.7 %all-to-all-done = bf16[16,16,448]{2,1,0:T(8,128)(2,1)S(1)} async-done(((bf16[16,16,448]{2,1,0:T(8,128)(2,1)}), bf16[16,16,448]{2,1,0:T(8,128)(2,1)S(1)}, u32[]{:S(2)}, u32[]{:S(2)}) %all-to-all-start) | async-done | bytes 229408 | tf_op jit(solution)/shard_map/all_to_all | solution.py:23
  128.4 6.5 %all-to-all-start.5 = ((bf16[4,128,512]{1,2,0:T(8,128)(2,1)}), bf16[4,128,512]{1,2,0:T(8,128)(2,1)S(1)}, u32[]{:S(2)}, u32[]{:S(2)}) async-start(bf16[4,128,512]{1,2,0:T(8,128)(2,1)} %bitcast.28), calls=%async_computation.5 | async-start | bytes 1048576 | tf_op jit(solution)/shard_map/all_to_all | solution.py:23
  136.0 12.2 %all-to-all-done.5 = bf16[4,128,512]{1,2,0:T(8,128)(2,1)S(1)} async-done(((bf16[4,128,512]{1,2,0:T(8,128)(2,1)}), bf16[4,128,512]{1,2,0:T(8,128)(2,1)S(1)}, u32[]{:S(2)}, u32[]{:S(2)}) %all-to-all-start.5) | async-done | bytes 524320 | tf_op jit(solution)/shard_map/all_to_all | solution.py:23
  148.2 8.7 %all-to-all-start.3 = ((bf16[16,16,512]{2,1,0:T(8,128)(2,1)}), bf16[16,16,512]{2,1,0:T(8,128)(2,1)}, u32[]{:S(2)}, u32[]{:S(2)}) async-start(bf16[16,16,512]{2,1,0:T(8,128)(2,1)} %bitcast.23), calls=%async_computation.3 | async-start | bytes 524288 | tf_op jit(solution)/shard_map/all_to_all | solution.py:23
  159.9 13.2 %all-to-all-done.3 = bf16[16,16,512]{2,1,0:T(8,128)(2,1)} async-done(((bf16[16,16,512]{2,1,0:T(8,128)(2,1)}), bf16[16,16,512]{2,1,0:T(8,128)(2,1)}, u32[]{:S(2)}, u32[]{:S(2)}) %all-to-all-start.3) | async-done | bytes 262176 | tf_op jit(solution)/shard_map/all_to_all | solution.py:23
  206.4 5.2 %collective-permute-done.1 = bf16[16,512]{1,0:T(8,128)(2,1)S(1)} collective-permute-done((bf16[16,512]{1,0:T(8,128)(2,1)S(1)}, bf16[16,512]{1,0:T(8,128)(2,1)S(1)}, u32[]{:S(2)}, u32[]{:S(2)}) %collective-permute-start.1) | collective-permute-done | bytes 16416 | tf_op jit(solution)/shard_map/ppermute | solution.py:19
  232.1 15.8 %all-to-all-done.6 = bf16[16,16,512]{2,1,0:T(8,128)(2,1)S(1)} async-done(((bf16[16,16,512]{2,1,0:T(8,128)(2,1)}), bf16[16,16,512]{2,1,0:T(8,128)(2,1)S(1)}, u32[]{:S(2)}, u32[]{:S(2)}) %all-to-all-start.6) | async-done | bytes 262176 | tf_op jit(solution)/shard_map/all_to_all | solution.py:23
  249.5 5.1 %all-to-all-start.7 = ((bf16[4,64,512]{2,1,0:T(8,128)(2,1)}), bf16[4,64,512]{2,1,0:T(8,128)(2,1)S(1)}, u32[]{:S(2)}, u32[]{:S(2)}) async-start(bf16[4,64,512]{2,1,0:T(8,128)(2,1)} %bitcast.44), calls=%async_computation.7 | async-start | bytes 524288 | tf_op jit(solution)/shard_map/all_to_all | solution.py:23
  254.9 21.9 %all-to-all-done.7 = bf16[4,64,512]{2,1,0:T(8,128)(2,1)S(1)} async-done(((bf16[4,64,512]{2,1,0:T(8,128)(2,1)}), bf16[4,64,512]{2,1,0:T(8,128)(2,1)S(1)}, u32[]{:S(2)}, u32[]{:S(2)}) %all-to-all-start.7) | async-done | bytes 262176 | tf_op jit(solution)/shard_map/all_to_all | solution.py:23
  278.1 19.0 %all-gather.9.cloned.1.call-done = bf16[16,320,512]{2,1,0:T(8,128)(2,1)} async-done(((bf16[1,320,512]{2,1,0:T(8,128)(2,1)}), bf16[16,320,512]{2,1,0:T(8,128)(2,1)}) %all-gather.9.cloned.1.call-update) | async-done | bytes 5242896 | tf_op jit(solution)/shard_map/all_gather | solution.py:144
  303.6 23.2 %all_to_all.70 = bf16[4,64,512]{2,1,0:T(8,128)(2,1)S(1)} all-to-all(bf16[4,64,512]{2,1,0:T(8,128)(2,1)S(1)} %broadcast_in_dim.62), channel_id=1, replica_groups=mesh['leaf'=32,'fa'=4,'fb'=4] {'fa'}, dimensions={0} | all-to-all | bytes 524288 | tf_op jit(solution)/shard_map/all_to_all | solution.py:23
  328.4 18.5 %all_to_all.71 = bf16[4,160,256]{2,1,0:T(8,128)(2,1)S(1)} all-to-all(bf16[4,160,256]{2,1,0:T(8,128)(2,1)S(1)} %convolution_convert_fusion), channel_id=1, replica_groups=mesh['leaf'=32,'fa'=4,'fb'=4] {'fb'}, dimensions={0} | all-to-all | bytes 655360 | tf_op jit(solution)/shard_map/all_to_all | solution.py:23
  347.2 23.6 %all_to_all.72 = bf16[4,128,256]{2,1,0:T(8,128)(2,1)S(1)} all-to-all(bf16[4,128,256]{2,1,0:T(8,128)(2,1)S(1)} %broadcast_in_dim.63), channel_id=1, replica_groups=mesh['leaf'=32,'fa'=4,'fb'=4] {'fa'}, dimensions={0} | all-to-all | bytes 524288 | tf_op jit(solution)/shard_map/all_to_all | solution.py:23
  371.1 11.7 %all_to_all.73 = bf16[4,64,512]{2,1,0:T(8,128)(2,1)S(1)} all-to-all(bf16[4,64,512]{2,1,0:T(8,128)(2,1)S(1)} %bitcast.194), channel_id=1, replica_groups=mesh['leaf'=32,'fa'=4,'fb'=4] {'fb'}, dimensions={0} | all-to-all | bytes 524288 | tf_op jit(solution)/shard_map/all_to_all | solution.py:23
  382.9 15.7 %all_to_all.74 = bf16[4,16,512]{2,1,0:T(8,128)(2,1)S(1)} all-to-all(bf16[4,16,512]{2,1,0:T(8,128)(2,1)S(1)} %bitcast.202), channel_id=1, replica_groups=mesh['leaf'=32,'fa'=4,'fb'=4] {'fa'}, dimensions={0} | all-to-all | bytes 131072 | tf_op jit(solution)/shard_map/all_to_all | solution.py:23
  410.1 5.8 %collective-permute-start.5 = (bf16[16,2048]{1,0:T(8,128)(2,1)S(1)}, bf16[16,2048]{1,0:T(8,128)(2,1)S(1)}, u32[]{:S(2)}, u32[]{:S(2)}) collective-permute-start(bf16[16,2048]{1,0:T(8,128)(2,1)S(1)} %fusion.4), channel_id=1, source_target_pairs={{16,0},{32,16},{48,32},{64,48},{80,64},{96,80},{112,96},{128,112},... | collective-permute-start | bytes 196616 | tf_op jit(solution)/shard_map/ppermute | solution.py:19
  419.1 5.8 %collective-permute-start.7 = (bf16[16,2048]{1,0:T(8,128)(2,1)S(1)}, bf16[16,2048]{1,0:T(8,128)(2,1)S(1)}, u32[]{:S(2)}, u32[]{:S(2)}) collective-permute-start(bf16[16,2048]{1,0:T(8,128)(2,1)S(1)} %fusion.5), channel_id=1, source_target_pairs={{16,0},{32,16},{48,32},{64,48},{80,64},{96,80},{112,96},{128,112},... | collective-permute-start | bytes 196616 | tf_op jit(solution)/shard_map/ppermute | solution.py:19
  436.0 14.5 %all-to-all-done.13 = bf16[16,16,640]{2,1,0:T(8,128)(2,1)S(1)} async-done(((bf16[16,16,640]{2,1,0:T(8,128)(2,1)}), bf16[16,16,640]{2,1,0:T(8,128)(2,1)S(1)}, u32[]{:S(2)}, u32[]{:S(2)}) %all-to-all-start.13) | async-done | bytes 327712 | tf_op jit(solution)/shard_map/all_to_all | solution.py:23
  (182 shorter events, 109.5 us)
Async XLA Ops:
  10.2 33.0 %all-to-all-start.1 = ((bf16[4,512,256]{2,1,0:T(8,128)(2,1)}), bf16[4,512,256]{2,1,0:T(8,128)(2,1)S(1)}, u32[]{:S(2)}, u32[]{:S(2)}) async-start(bf16[4,512,256]{2,1,0:T(8,128)(2,1)} %bitcast.17), calls=%async_computation.1 | async-start | bytes 2097152 | tf_op jit(solution)/shard_map/all_to_all | solution.py:23
  16.1 85.4 %all-gather.11.cloned.1.call-start = ((), (), s32[]{:S(2)}) async-start(), calls=%async_computation.16 | async-start | bytes 2228224 | tf_op jit(solution)/shard_map/all_gather | solution.py:100
  44.2 36.1 %all-to-all-start.2 = ((bf16[4,128,256]{2,1,0:T(8,128)(2,1)}), bf16[4,128,256]{2,1,0:T(8,128)(2,1)S(1)}, u32[]{:S(2)}, u32[]{:S(2)}) async-start(bf16[4,128,256]{2,1,0:T(8,128)(2,1)} %bitcast.18), calls=%async_computation.2 | async-start | bytes 524288 | tf_op jit(solution)/shard_map/all_to_all | solution.py:23
  58.7 131.9 %all-gather.7.cloned.1.call-start = ((), (), s32[]{:S(2)}) async-start(), calls=%async_computation.14 | async-start | bytes 2785280 | tf_op jit(solution)/shard_map/all_gather | solution.py:124
  107.0 21.4 %all-to-all-start = ((bf16[16,16,448]{2,1,0:T(8,128)(2,1)}), bf16[16,16,448]{2,1,0:T(8,128)(2,1)S(1)}, u32[]{:S(2)}, u32[]{:S(2)}) async-start(bf16[16,16,448]{2,1,0:T(8,128)(2,1)} %bitcast.12), calls=%async_computation | async-start | bytes 524288 | tf_op jit(solution)/shard_map/all_to_all | solution.py:23
  128.4 19.8 %all-to-all-start.5 = ((bf16[4,128,512]{1,2,0:T(8,128)(2,1)}), bf16[4,128,512]{1,2,0:T(8,128)(2,1)S(1)}, u32[]{:S(2)}, u32[]{:S(2)}) async-start(bf16[4,128,512]{1,2,0:T(8,128)(2,1)} %bitcast.28), calls=%async_computation.5 | async-start | bytes 1048576 | tf_op jit(solution)/shard_map/all_to_all | solution.py:23
  148.2 24.9 %all-to-all-start.3 = ((bf16[16,16,512]{2,1,0:T(8,128)(2,1)}), bf16[16,16,512]{2,1,0:T(8,128)(2,1)}, u32[]{:S(2)}, u32[]{:S(2)}) async-start(bf16[16,16,512]{2,1,0:T(8,128)(2,1)} %bitcast.23), calls=%async_computation.3 | async-start | bytes 524288 | tf_op jit(solution)/shard_map/all_to_all | solution.py:23
  156.9 140.2 %all-gather.9.cloned.1.call-start = ((), (), s32[]{:S(2)}) async-start(), calls=%async_computation.15 | async-start | bytes 5570560 | tf_op jit(solution)/shard_map/all_gather | solution.py:144
  182.6 41.4 %all-to-all-start.4 = ((bf16[4,400,512]{2,1,0:T(8,128)(2,1)}), bf16[4,400,512]{2,1,0:T(8,128)(2,1)}, u32[]{:S(2)}, u32[]{:S(2)}) async-start(bf16[4,400,512]{2,1,0:T(8,128)(2,1)} %maximum_add_fusion), calls=%async_computation.4 | async-start | bytes 3276800 | tf_op jit(solution)/shard_map/all_to_all | solution.py:23
  187.2 11.0 %collective-permute-start = (bf16[16,512]{1,0:T(8,128)(2,1)S(1)}, bf16[16,512]{1,0:T(8,128)(2,1)S(1)}, u32[]{:S(2)}, u32[]{:S(2)}) collective-permute-start(bf16[16,512]{1,0:T(8,128)(2,1)S(1)} %get-tuple-element.14), channel_id=1, source_target_pairs={{496,0},{0,16},{16,32},{32,48},{48,64},{64,80},{80,96},{96,112},{1... | collective-permute-start | bytes 49160 | tf_op jit(solution)/shard_map/ppermute | solution.py:19
  199.8 6.7 %collective-permute-start.2 = (bf16[16,512]{1,0:T(8,128)(2,1)S(1)}, bf16[16,512]{1,0:T(8,128)(2,1)S(1)}, u32[]{:S(2)}, u32[]{:S(2)}) collective-permute-start(bf16[16,512]{1,0:T(8,128)(2,1)S(1)} %fusion.38), channel_id=1, source_target_pairs={{16,0},{32,16},{48,32},{64,48},{80,64},{96,80},{112,96},{128,112},... | collective-permute-start | bytes 49160 | tf_op jit(solution)/shard_map/ppermute | solution.py:19
  204.5 7.2 %collective-permute-start.1 = (bf16[16,512]{1,0:T(8,128)(2,1)S(1)}, bf16[16,512]{1,0:T(8,128)(2,1)S(1)}, u32[]{:S(2)}, u32[]{:S(2)}) collective-permute-start(bf16[16,512]{1,0:T(8,128)(2,1)S(1)} %fusion.38), channel_id=1, source_target_pairs={{496,0},{0,16},{16,32},{32,48},{48,64},{64,80},{80,96},{96,112},{1... | collective-permute-start | bytes 49160 | tf_op jit(solution)/shard_map/ppermute | solution.py:19
  213.2 5.6 %collective-permute-start.3 = (bf16[16,512]{1,0:T(8,128)(2,1)S(1)}, bf16[16,512]{1,0:T(8,128)(2,1)S(1)}, u32[]{:S(2)}, u32[]{:S(2)}) collective-permute-start(bf16[16,512]{1,0:T(8,128)(2,1)S(1)} %fusion.39), channel_id=1, source_target_pairs={{32,0},{48,16},{64,32},{80,48},{96,64},{112,80},{128,96},{144,112}... | collective-permute-start | bytes 49160 | tf_op jit(solution)/shard_map/ppermute | solution.py:19
  224.7 23.2 %all-to-all-start.6 = ((bf16[16,16,512]{2,1,0:T(8,128)(2,1)}), bf16[16,16,512]{2,1,0:T(8,128)(2,1)S(1)}, u32[]{:S(2)}, u32[]{:S(2)}) async-start(bf16[16,16,512]{2,1,0:T(8,128)(2,1)} %broadcast_in_dim.61), calls=%async_computation.6 | async-start | bytes 524288 | tf_op jit(solution)/shard_map/all_to_all | solution.py:23
  249.5 27.4 %all-to-all-start.7 = ((bf16[4,64,512]{2,1,0:T(8,128)(2,1)}), bf16[4,64,512]{2,1,0:T(8,128)(2,1)S(1)}, u32[]{:S(2)}, u32[]{:S(2)}) async-start(bf16[4,64,512]{2,1,0:T(8,128)(2,1)} %bitcast.44), calls=%async_computation.7 | async-start | bytes 524288 | tf_op jit(solution)/shard_map/all_to_all | solution.py:23
  254.6 147.0 %all-gather.13.cloned.1.call-start = ((), (), s32[]{:S(2)}) async-start(), calls=%async_computation.17 | async-start | bytes 3342336 | tf_op jit(solution)/shard_map/all_gather | solution.py:169
  302.8 44.0 %copy-start.8 = (pred[160,1024]{1,0:T(32,128)(4,1)S(1)}, pred[160,1024]{1,0:T(32,128)(4,1)}, u32[]{:S(2)}) copy-start(pred[160,1024]{1,0:T(32,128)(4,1)} %get-tuple-element.36) | copy-start | bytes 491524
  326.8 43.9 %copy-start.3 = (bf16[4,128,512]{2,1,0:T(8,128)(2,1)S(1)}, bf16[4,128,512]{2,1,0:T(8,128)(2,1)}, u32[]{:S(2)}) copy-start(bf16[4,128,512]{2,1,0:T(8,128)(2,1)} %copy-done.2) | copy-start | bytes 1572868
  346.8 54.7 %copy-start.17 = (s32[1,2,512]{2,1,0:T(2,128)S(1)}, s32[1,2,512]{2,1,0:T(2,128)}, u32[]{:S(2)}) copy-start(s32[1,2,512]{2,1,0:T(2,128)} %param.21) | copy-start | bytes 12292
  398.5 8.3 %collective-permute-start.4 = (bf16[16,2048]{1,0:T(8,128)(2,1)S(1)}, bf16[16,2048]{1,0:T(8,128)(2,1)S(1)}, u32[]{:S(2)}, u32[]{:S(2)}) collective-permute-start(bf16[16,2048]{1,0:T(8,128)(2,1)S(1)} %bitcast.207), channel_id=1, source_target_pairs={{480,0},{496,16},{0,32},{16,48},{32,64},{48,80},{64,96},{80,112},{... | collective-permute-start | bytes 196616 | tf_op jit(solution)/shard_map/ppermute | solution.py:19
  408.1 7.7 %collective-permute-start.6 = (bf16[16,2048]{1,0:T(8,128)(2,1)S(1)}, bf16[16,2048]{1,0:T(8,128)(2,1)S(1)}, u32[]{:S(2)}, u32[]{:S(2)}) collective-permute-start(bf16[16,2048]{1,0:T(8,128)(2,1)S(1)} %fusion.4), channel_id=1, source_target_pairs={{496,0},{0,16},{16,32},{32,48},{48,64},{64,80},{80,96},{96,112},{1... | collective-permute-start | bytes 196616 | tf_op jit(solution)/shard_map/ppermute | solution.py:19
  410.1 7.6 %collective-permute-start.5 = (bf16[16,2048]{1,0:T(8,128)(2,1)S(1)}, bf16[16,2048]{1,0:T(8,128)(2,1)S(1)}, u32[]{:S(2)}, u32[]{:S(2)}) collective-permute-start(bf16[16,2048]{1,0:T(8,128)(2,1)S(1)} %fusion.4), channel_id=1, source_target_pairs={{16,0},{32,16},{48,32},{64,48},{80,64},{96,80},{112,96},{128,112},... | collective-permute-start | bytes 196616 | tf_op jit(solution)/shard_map/ppermute | solution.py:19
  419.1 7.7 %collective-permute-start.7 = (bf16[16,2048]{1,0:T(8,128)(2,1)S(1)}, bf16[16,2048]{1,0:T(8,128)(2,1)S(1)}, u32[]{:S(2)}, u32[]{:S(2)}) collective-permute-start(bf16[16,2048]{1,0:T(8,128)(2,1)S(1)} %fusion.5), channel_id=1, source_target_pairs={{16,0},{32,16},{48,32},{64,48},{80,64},{96,80},{112,96},{128,112},... | collective-permute-start | bytes 196616 | tf_op jit(solution)/shard_map/ppermute | solution.py:19
  428.4 22.1 %all-to-all-start.13 = ((bf16[16,16,640]{2,1,0:T(8,128)(2,1)}), bf16[16,16,640]{2,1,0:T(8,128)(2,1)S(1)}, u32[]{:S(2)}, u32[]{:S(2)}) async-start(bf16[16,16,640]{2,1,0:T(8,128)(2,1)} %pad_maximum_fusion.2), calls=%async_computation.13 | async-start | bytes 655360 | tf_op jit(solution)/shard_map/all_to_all | solution.py:23
  (18 other events, 136.8 us)
Sparse Core Ops, SparseCore 0:
  19.0 82.4 all-gather.10
  104.8 85.7 all-gather.6
  192.7 104.3 all-gather.8
  303.7 83.5 all-gather.12

commit v8 on v7

--- a/solution.py
+++ b/solution.py
@@ -162,8 +162,11 @@
 
     partial_y = (y_own + mm("rc,ck->rk", left, w_left)).astype(BF16)
     part = total(exchange(partial_y.reshape(na, R // na, K // nb), "fa")).astype(BF16)
-    node_reach = mm("pm,mc->pc", after(pivot_inverse[0, 1], part), node_coupling_all).astype(BF16)
-    leaf_pivots = mm("pk,kr->pr", after(leaf_vectors_pivot[0, 0], part), leaf_y_all)
+    y_block = to_all(part, "fa").reshape(R, K // nb)
+    part = mm("bsk,rk->bsr", v_block, y_block).astype(BF16)
+
+    node_reach = mm("pm,mc->pc", after(pivot_inverse[0, 1], y_block), node_coupling_all).astype(BF16)
+    leaf_pivots = mm("pk,kr->pr", after(leaf_vectors_pivot[0, 0], y_block), leaf_y_all)
     leaf_pivots = (leaf_pivot_block[0] - leaf_pivots).astype(BF16)
     wide = jnp.concatenate([node_reach, folded(leaf_pivots)], axis=0)
     gathered = lax.all_gather(wide, FRONT, axis=0)
@@ -172,8 +175,6 @@
     leaf_reach = mm("pm,mc->pc", pivot_inverse[0, 0], leaf_coupling_all).astype(BF16)
     leaf_own = mm("pm,mr->pr", pivot_inverse[0, 0], leaf_pivots_all)
 
-    y_block = to_all(part, "fa").reshape(R, K // nb)
-    part = mm("bsk,rk->bsr", v_block, y_block).astype(BF16)
     placed = mm("sc,rc->sr", own_hit[:, :C].astype(BF16), left)
     reflected = own.astype(F32) + placed - total(exchange(part, "fb"))
     reflected = reflected.astype(BF16)

time: 466 us -> 465 us (level)
  waiting for transfers between devices: 197 us -> 167 us
  blocking collectives: 92.7 us -> 120 us
  starting transfers between devices: 88.7 us -> 96.6 us
    all_to_all x5 -> x6, blocking collectives: 92.7 us -> 120 us  [exchange(): return lax.all_to_all(parts, axis, split_axis=0, concat_axis=0, tiled=True)]
    all_to_all x9 -> x8, waiting for transfers between devices: 142 us -> 117 us  [exchange(): return lax.all_to_all(parts, axis, split_axis=0, concat_axis=0, tiled=True)]
    all_gather x1, waiting for transfers between devices: 19 us -> 4.68 us  [per_device(): gathered = lax.all_gather(after(wide, rest), FRONT, axis=0)]
    all_gather x1, waiting for transfers between devices: 0.02 us -> 11.5 us  [per_device(): gathered = lax.all_gather(wide, FRONT, axis=0)]
    all_to_all x9 -> x8, starting transfers between devices: 60.6 us -> 69.6 us  [exchange(): return lax.all_to_all(parts, axis, split_axis=0, concat_axis=0, tiled=True)]
  transfers between devices with their start and end apart: 21 -> 20, of which waited for: 17 -> 15; matrix products, arithmetic and copies ran while one was open for 10% -> 8% of each run, Pallas kernels for 0% -> 0%
where the time goes in v8:
time: 465 us; the launch traced here: 462 us
  waiting for transfers between devices  167 us (36%)
  blocking collectives  120 us (26%)
  starting transfers between devices  96.6 us (21%)
  local copies, waits for them, and re-layouts  29.9 us (6%)
  matrix products  23.5 us (5%)
  between operations  17.9 us (4%)
  other arithmetic  6.5 us (1%)
    all_to_all x6, blocking collectives, exchange(): return lax.all_to_all(parts, axis, split_axis=0, concat_axis=0, tiled=True)  120 us
    all_to_all x8, waiting for transfers between devices, exchange(): return lax.all_to_all(parts, axis, split_axis=0, concat_axis=0, tiled=True)  117 us
    all_to_all x8, starting transfers between devices, exchange(): return lax.all_to_all(parts, axis, split_axis=0, concat_axis=0, tiled=True)  69.6 us
    ppermute x8, starting transfers between devices, from_behind(): lax.ppermute(block, 'leaf', [((i - distance) % count, i) for i in range(c...  26.8 us
    dot_general x19, matrix products, mm(): return jnp.einsum(spec, a, b, preferred_element_type=F32)  23.5 us
    all_gather x1, waiting for transfers between devices, per_device(): lax.all_gather(node_vectors_rest[0, 0], FRONT, axis=0, tiled=True)  21.4 us
    ppermute x8, waiting for transfers between devices, from_behind(): lax.ppermute(block, 'leaf', [((i - distance) % count, i) for i in range(c...  12.7 us
    all_gather x1, waiting for transfers between devices, per_device(): gathered = lax.all_gather(wide, FRONT, axis=0)  11.5 us
  transfers between devices with their start and end apart: 20, of which 15 were waited for; matrix products, arithmetic and copies ran while one was open for 8% of the time, Pallas kernels for 0%

profile of v8, /device:TPU:24, one launch (start us, length us, event | category | flops | bytes accessed | tf_op | source)
XLA Modules:
  0.0 462.0 jit_solution(8115652793433013957)
XLA Ops:
  10.2 5.9 %all-to-all-start.1 = ((bf16[4,512,256]{2,1,0:T(8,128)(2,1)}), bf16[4,512,256]{2,1,0:T(8,128)(2,1)S(1)}, u32[]{:S(2)}, u32[]{:S(2)}) async-start(bf16[4,512,256]{2,1,0:T(8,128)(2,1)} %bitcast.17), calls=%async_computation.1 | async-start | bytes 2097152 | tf_op jit(solution)/shard_map/all_to_all | solution.py:23
  17.1 25.9 %all-to-all-done.1 = bf16[4,512,256]{2,1,0:T(8,128)(2,1)S(1)} async-done(((bf16[4,512,256]{2,1,0:T(8,128)(2,1)}), bf16[4,512,256]{2,1,0:T(8,128)(2,1)S(1)}, u32[]{:S(2)}, u32[]{:S(2)}) %all-to-all-start.1) | async-done | bytes 1048608 | tf_op jit(solution)/shard_map/all_to_all | solution.py:23
  43.9 14.1 %all-to-all-start.2 = ((bf16[4,128,256]{2,1,0:T(8,128)(2,1)}), bf16[4,128,256]{2,1,0:T(8,128)(2,1)S(1)}, u32[]{:S(2)}, u32[]{:S(2)}) async-start(bf16[4,128,256]{2,1,0:T(8,128)(2,1)} %bitcast.18), calls=%async_computation.2 | async-start | bytes 524288 | tf_op jit(solution)/shard_map/all_to_all | solution.py:23
  59.6 19.8 %all-to-all-done.2 = bf16[4,128,256]{2,1,0:T(8,128)(2,1)S(1)} async-done(((bf16[4,128,256]{2,1,0:T(8,128)(2,1)}), bf16[4,128,256]{2,1,0:T(8,128)(2,1)S(1)}, u32[]{:S(2)}, u32[]{:S(2)}) %all-to-all-start.2) | async-done | bytes 262176 | tf_op jit(solution)/shard_map/all_to_all | solution.py:23
  80.6 21.4 %all-gather.11.cloned.1.call-done = bf16[1,1,512,2048]{3,2,1,0:T(8,128)(2,1)} async-done(((bf16[1,1,32,2048]{3,2,1,0:T(8,128)(2,1)}), bf16[1,1,512,2048]{3,2,1,0:T(8,128)(2,1)}) %all-gather.11.cloned.1.call-update) | async-done | bytes 2097168 | tf_op jit(solution)/shard_map/all_gather | solution.py:100
  107.5 8.0 %all-to-all-start = ((bf16[16,16,448]{2,1,0:T(8,128)(2,1)}), bf16[16,16,448]{2,1,0:T(8,128)(2,1)S(1)}, u32[]{:S(2)}, u32[]{:S(2)}) async-start(bf16[16,16,448]{2,1,0:T(8,128)(2,1)} %bitcast.12), calls=%async_computation | async-start | bytes 524288 | tf_op jit(solution)/shard_map/all_to_all | solution.py:23
  117.2 12.4 %all-to-all-done = bf16[16,16,448]{2,1,0:T(8,128)(2,1)S(1)} async-done(((bf16[16,16,448]{2,1,0:T(8,128)(2,1)}), bf16[16,16,448]{2,1,0:T(8,128)(2,1)S(1)}, u32[]{:S(2)}, u32[]{:S(2)}) %all-to-all-start) | async-done | bytes 229408 | tf_op jit(solution)/shard_map/all_to_all | solution.py:23
  129.6 6.5 %all-to-all-start.5 = ((bf16[4,128,512]{2,1,0:T(8,128)(2,1)}), bf16[4,128,512]{2,1,0:T(8,128)(2,1)S(1)}, u32[]{:S(2)}, u32[]{:S(2)}) async-start(bf16[4,128,512]{2,1,0:T(8,128)(2,1)} %reshape.409), calls=%async_computation.5 | async-start | bytes 1048576 | tf_op jit(solution)/shard_map/all_to_all | solution.py:23
  137.2 13.2 %all-to-all-done.5 = bf16[4,128,512]{2,1,0:T(8,128)(2,1)S(1)} async-done(((bf16[4,128,512]{2,1,0:T(8,128)(2,1)}), bf16[4,128,512]{2,1,0:T(8,128)(2,1)S(1)}, u32[]{:S(2)}, u32[]{:S(2)}) %all-to-all-start.5) | async-done | bytes 524320 | tf_op jit(solution)/shard_map/all_to_all | solution.py:23
  150.4 9.7 %all-to-all-start.3 = ((bf16[16,16,512]{2,1,0:T(8,128)(2,1)}), bf16[16,16,512]{2,1,0:T(8,128)(2,1)S(1)}, u32[]{:S(2)}, u32[]{:S(2)}) async-start(bf16[16,16,512]{2,1,0:T(8,128)(2,1)} %bitcast.23), calls=%async_computation.3 | async-start | bytes 524288 | tf_op jit(solution)/shard_map/all_to_all | solution.py:23
  162.5 14.1 %all-to-all-done.3 = bf16[16,16,512]{2,1,0:T(8,128)(2,1)S(1)} async-done(((bf16[16,16,512]{2,1,0:T(8,128)(2,1)}), bf16[16,16,512]{2,1,0:T(8,128)(2,1)S(1)}, u32[]{:S(2)}, u32[]{:S(2)}) %all-to-all-start.3) | async-done | bytes 262176 | tf_op jit(solution)/shard_map/all_to_all | solution.py:23
  219.6 14.4 %all-to-all-start.6 = ((bf16[16,16,512]{2,1,0:T(8,128)(2,1)}), bf16[16,16,512]{2,1,0:T(8,128)(2,1)S(1)}, u32[]{:S(2)}, u32[]{:S(2)}) async-start(bf16[16,16,512]{2,1,0:T(8,128)(2,1)} %broadcast_in_dim.61), calls=%async_computation.6 | async-start | bytes 524288 | tf_op jit(solution)/shard_map/all_to_all | solution.py:23
  237.9 16.0 %all-to-all-done.6 = bf16[16,16,512]{2,1,0:T(8,128)(2,1)S(1)} async-done(((bf16[16,16,512]{2,1,0:T(8,128)(2,1)}), bf16[16,16,512]{2,1,0:T(8,128)(2,1)S(1)}, u32[]{:S(2)}, u32[]{:S(2)}) %all-to-all-start.6) | async-done | bytes 262176 | tf_op jit(solution)/shard_map/all_to_all | solution.py:23
  254.7 27.1 %all_to_all.70 = bf16[4,64,512]{2,1,0:T(8,128)(2,1)S(1)} all-to-all(bf16[4,64,512]{2,1,0:T(8,128)(2,1)S(1)} %bitcast.204), channel_id=1, replica_groups=mesh['leaf'=32,'fa'=4,'fb'=4] {'fa'}, dimensions={0} | all-to-all | bytes 524288 | tf_op jit(solution)/shard_map/all_to_all | solution.py:23
  282.0 24.0 %all_to_all.71 = bf16[4,64,512]{2,1,0:T(8,128)(2,1)S(1)} all-to-all(bf16[4,64,512]{2,1,0:T(8,128)(2,1)S(1)} %broadcast_in_dim.62), channel_id=1, replica_groups=mesh['leaf'=32,'fa'=4,'fb'=4] {'fa'}, dimensions={0} | all-to-all | bytes 524288 | tf_op jit(solution)/shard_map/all_to_all | solution.py:23
  320.0 12.1 %all_to_all.72 = bf16[4,160,256]{2,1,0:T(8,128)(2,1)S(1)} all-to-all(bf16[4,160,256]{2,1,0:T(8,128)(2,1)S(1)} %convolution_convert_fusion), channel_id=1, replica_groups=mesh['leaf'=32,'fa'=4,'fb'=4] {'fb'}, dimensions={0} | all-to-all | bytes 655360 | tf_op jit(solution)/shard_map/all_to_all | solution.py:23
  332.4 28.3 %all_to_all.73 = bf16[4,128,256]{2,1,0:T(8,128)(2,1)S(1)} all-to-all(bf16[4,128,256]{2,1,0:T(8,128)(2,1)S(1)} %broadcast_in_dim.63), channel_id=1, replica_groups=mesh['leaf'=32,'fa'=4,'fb'=4] {'fa'}, dimensions={0} | all-to-all | bytes 524288 | tf_op jit(solution)/shard_map/all_to_all | solution.py:23
  361.1 13.2 %all_to_all.74 = bf16[4,64,512]{2,1,0:T(8,128)(2,1)S(1)} all-to-all(bf16[4,64,512]{2,1,0:T(8,128)(2,1)S(1)} %bitcast.193), channel_id=1, replica_groups=mesh['leaf'=32,'fa'=4,'fb'=4] {'fb'}, dimensions={0} | all-to-all | bytes 524288 | tf_op jit(solution)/shard_map/all_to_all | solution.py:23
  374.4 15.4 %all_to_all.75 = bf16[4,16,512]{2,1,0:T(8,128)(2,1)S(1)} all-to-all(bf16[4,16,512]{2,1,0:T(8,128)(2,1)S(1)} %bitcast.201), channel_id=1, replica_groups=mesh['leaf'=32,'fa'=4,'fb'=4] {'fa'}, dimensions={0} | all-to-all | bytes 131072 | tf_op jit(solution)/shard_map/all_to_all | solution.py:23
  392.0 11.5 %all-gather.13.cloned.1.call-done = bf16[3072,512]{1,0:T(8,128)(2,1)} async-done(((bf16[192,512]{1,0:T(8,128)(2,1)}), bf16[3072,512]{1,0:T(8,128)(2,1)}) %all-gather.13.cloned.1.call-update) | async-done | bytes 3145744 | tf_op jit(solution)/shard_map/all_gather | solution.py:172
  408.5 5.8 %collective-permute-start.5 = (bf16[16,2048]{1,0:T(8,128)(2,1)S(1)}, bf16[16,2048]{1,0:T(8,128)(2,1)S(1)}, u32[]{:S(2)}, u32[]{:S(2)}) collective-permute-start(bf16[16,2048]{1,0:T(8,128)(2,1)S(1)} %fusion.4), channel_id=1, source_target_pairs={{16,0},{32,16},{48,32},{64,48},{80,64},{96,80},{112,96},{128,112},... | collective-permute-start | bytes 196616 | tf_op jit(solution)/shard_map/ppermute | solution.py:19
  417.5 5.8 %collective-permute-start.7 = (bf16[16,2048]{1,0:T(8,128)(2,1)S(1)}, bf16[16,2048]{1,0:T(8,128)(2,1)S(1)}, u32[]{:S(2)}, u32[]{:S(2)}) collective-permute-start(bf16[16,2048]{1,0:T(8,128)(2,1)S(1)} %fusion.5), channel_id=1, source_target_pairs={{16,0},{32,16},{48,32},{64,48},{80,64},{96,80},{112,96},{128,112},... | collective-permute-start | bytes 196616 | tf_op jit(solution)/shard_map/ppermute | solution.py:19
  426.8 6.5 %all-to-all-start.13 = ((bf16[16,16,640]{2,1,0:T(8,128)(2,1)}), bf16[16,16,640]{2,1,0:T(8,128)(2,1)S(1)}, u32[]{:S(2)}, u32[]{:S(2)}) async-start(bf16[16,16,640]{2,1,0:T(8,128)(2,1)} %pad_maximum_fusion.2), calls=%async_computation.13 | async-start | bytes 655360 | tf_op jit(solution)/shard_map/all_to_all | solution.py:23
  436.5 15.4 %all-to-all-done.13 = bf16[16,16,640]{2,1,0:T(8,128)(2,1)S(1)} async-done(((bf16[16,16,640]{2,1,0:T(8,128)(2,1)}), bf16[16,16,640]{2,1,0:T(8,128)(2,1)S(1)}, u32[]{:S(2)}, u32[]{:S(2)}) %all-to-all-start.13) | async-done | bytes 327712 | tf_op jit(solution)/shard_map/all_to_all | solution.py:23
  (178 shorter events, 97.5 us)
Async XLA Ops:
  10.2 32.8 %all-to-all-start.1 = ((bf16[4,512,256]{2,1,0:T(8,128)(2,1)}), bf16[4,512,256]{2,1,0:T(8,128)(2,1)S(1)}, u32[]{:S(2)}, u32[]{:S(2)}) async-start(bf16[4,512,256]{2,1,0:T(8,128)(2,1)} %bitcast.17), calls=%async_computation.1 | async-start | bytes 2097152 | tf_op jit(solution)/shard_map/all_to_all | solution.py:23
  16.1 86.0 %all-gather.11.cloned.1.call-start = ((), (), s32[]{:S(2)}) async-start(), calls=%async_computation.16 | async-start | bytes 2228224 | tf_op jit(solution)/shard_map/all_gather | solution.py:100
  43.9 35.5 %all-to-all-start.2 = ((bf16[4,128,256]{2,1,0:T(8,128)(2,1)}), bf16[4,128,256]{2,1,0:T(8,128)(2,1)S(1)}, u32[]{:S(2)}, u32[]{:S(2)}) async-start(bf16[4,128,256]{2,1,0:T(8,128)(2,1)} %bitcast.18), calls=%async_computation.2 | async-start | bytes 524288 | tf_op jit(solution)/shard_map/all_to_all | solution.py:23
  58.0 131.8 %all-gather.7.cloned.1.call-start = ((), (), s32[]{:S(2)}) async-start(), calls=%async_computation.14 | async-start | bytes 2785280 | tf_op jit(solution)/shard_map/all_gather | solution.py:124
  107.5 22.0 %all-to-all-start = ((bf16[16,16,448]{2,1,0:T(8,128)(2,1)}), bf16[16,16,448]{2,1,0:T(8,128)(2,1)S(1)}, u32[]{:S(2)}, u32[]{:S(2)}) async-start(bf16[16,16,448]{2,1,0:T(8,128)(2,1)} %bitcast.12), calls=%async_computation | async-start | bytes 524288 | tf_op jit(solution)/shard_map/all_to_all | solution.py:23
  129.6 20.8 %all-to-all-start.5 = ((bf16[4,128,512]{2,1,0:T(8,128)(2,1)}), bf16[4,128,512]{2,1,0:T(8,128)(2,1)S(1)}, u32[]{:S(2)}, u32[]{:S(2)}) async-start(bf16[4,128,512]{2,1,0:T(8,128)(2,1)} %reshape.409), calls=%async_computation.5 | async-start | bytes 1048576 | tf_op jit(solution)/shard_map/all_to_all | solution.py:23
  136.2 42.5 %copy-start.5 = (bf16[1,1,32,2048]{3,2,1,0:T(8,128)(2,1)S(1)}, bf16[1,1,32,2048]{3,2,1,0:T(8,128)(2,1)}, u32[]{:S(2)}) copy-start(bf16[1,1,32,2048]{3,2,1,0:T(8,128)(2,1)} %get-tuple-element.27) | copy-start | bytes 393220
  150.4 26.3 %all-to-all-start.3 = ((bf16[16,16,512]{2,1,0:T(8,128)(2,1)}), bf16[16,16,512]{2,1,0:T(8,128)(2,1)S(1)}, u32[]{:S(2)}, u32[]{:S(2)}) async-start(bf16[16,16,512]{2,1,0:T(8,128)(2,1)} %bitcast.23), calls=%async_computation.3 | async-start | bytes 524288 | tf_op jit(solution)/shard_map/all_to_all | solution.py:23
  160.1 151.7 %all-gather.9.cloned.1.call-start = ((), (), s32[]{:S(2)}) async-start(), calls=%async_computation.15 | async-start | bytes 5570560 | tf_op jit(solution)/shard_map/all_gather | solution.py:144
  182.6 36.2 %all-to-all-start.4 = ((bf16[4,400,512]{2,1,0:T(8,128)(2,1)}), bf16[4,400,512]{2,1,0:T(8,128)(2,1)}, u32[]{:S(2)}, u32[]{:S(2)}) async-start(bf16[4,400,512]{2,1,0:T(8,128)(2,1)} %maximum_add_fusion), calls=%async_computation.4 | async-start | bytes 3276800 | tf_op jit(solution)/shard_map/all_to_all | solution.py:23
  187.1 10.3 %collective-permute-start = (bf16[16,512]{1,0:T(8,128)(2,1)S(1)}, bf16[16,512]{1,0:T(8,128)(2,1)S(1)}, u32[]{:S(2)}, u32[]{:S(2)}) collective-permute-start(bf16[16,512]{1,0:T(8,128)(2,1)S(1)} %get-tuple-element.14), channel_id=1, source_target_pairs={{496,0},{0,16},{16,32},{32,48},{48,64},{64,80},{80,96},{96,112},{1... | collective-permute-start | bytes 49160 | tf_op jit(solution)/shard_map/ppermute | solution.py:19
  199.0 7.4 %collective-permute-start.2 = (bf16[16,512]{1,0:T(8,128)(2,1)S(1)}, bf16[16,512]{1,0:T(8,128)(2,1)S(1)}, u32[]{:S(2)}, u32[]{:S(2)}) collective-permute-start(bf16[16,512]{1,0:T(8,128)(2,1)S(1)} %fusion.38), channel_id=1, source_target_pairs={{16,0},{32,16},{48,32},{64,48},{80,64},{96,80},{112,96},{128,112},... | collective-permute-start | bytes 49160 | tf_op jit(solution)/shard_map/ppermute | solution.py:19
  204.5 7.2 %collective-permute-start.1 = (bf16[16,512]{1,0:T(8,128)(2,1)S(1)}, bf16[16,512]{1,0:T(8,128)(2,1)S(1)}, u32[]{:S(2)}, u32[]{:S(2)}) collective-permute-start(bf16[16,512]{1,0:T(8,128)(2,1)S(1)} %fusion.38), channel_id=1, source_target_pairs={{496,0},{0,16},{16,32},{32,48},{48,64},{64,80},{80,96},{96,112},{1... | collective-permute-start | bytes 49160 | tf_op jit(solution)/shard_map/ppermute | solution.py:19
  213.2 5.6 %collective-permute-start.3 = (bf16[16,512]{1,0:T(8,128)(2,1)S(1)}, bf16[16,512]{1,0:T(8,128)(2,1)S(1)}, u32[]{:S(2)}, u32[]{:S(2)}) collective-permute-start(bf16[16,512]{1,0:T(8,128)(2,1)S(1)} %fusion.39), channel_id=1, source_target_pairs={{32,0},{48,16},{64,32},{80,48},{96,64},{112,80},{128,96},{144,112}... | collective-permute-start | bytes 49160 | tf_op jit(solution)/shard_map/ppermute | solution.py:19
  219.6 34.3 %all-to-all-start.6 = ((bf16[16,16,512]{2,1,0:T(8,128)(2,1)}), bf16[16,16,512]{2,1,0:T(8,128)(2,1)S(1)}, u32[]{:S(2)}, u32[]{:S(2)}) async-start(bf16[16,16,512]{2,1,0:T(8,128)(2,1)} %broadcast_in_dim.61), calls=%async_computation.6 | async-start | bytes 524288 | tf_op jit(solution)/shard_map/all_to_all | solution.py:23
  234.0 169.4 %all-gather.13.cloned.1.call-start = ((), (), s32[]{:S(2)}) async-start(), calls=%async_computation.17 | async-start | bytes 3342336 | tf_op jit(solution)/shard_map/all_gather | solution.py:172
  317.8 14.3 %copy-start.8 = (pred[160,1024]{1,0:T(32,128)(4,1)S(1)}, pred[160,1024]{1,0:T(32,128)(4,1)}, u32[]{:S(2)}) copy-start(pred[160,1024]{1,0:T(32,128)(4,1)} %get-tuple-element.36) | copy-start | bytes 491524
  332.1 59.9 %copy-start.17 = (s32[1,2,512]{2,1,0:T(2,128)S(1)}, s32[1,2,512]{2,1,0:T(2,128)}, u32[]{:S(2)}) copy-start(s32[1,2,512]{2,1,0:T(2,128)} %param.21) | copy-start | bytes 12292
  389.8 15.4 %collective-permute-start.4 = (bf16[16,2048]{1,0:T(8,128)(2,1)S(1)}, bf16[16,2048]{1,0:T(8,128)(2,1)S(1)}, u32[]{:S(2)}, u32[]{:S(2)}) collective-permute-start(bf16[16,2048]{1,0:T(8,128)(2,1)S(1)} %bitcast.208), channel_id=1, source_target_pairs={{480,0},{496,16},{0,32},{16,48},{32,64},{48,80},{64,96},{80,112},{... | collective-permute-start | bytes 196616 | tf_op jit(solution)/shard_map/ppermute | solution.py:19
  406.6 7.7 %collective-permute-start.6 = (bf16[16,2048]{1,0:T(8,128)(2,1)S(1)}, bf16[16,2048]{1,0:T(8,128)(2,1)S(1)}, u32[]{:S(2)}, u32[]{:S(2)}) collective-permute-start(bf16[16,2048]{1,0:T(8,128)(2,1)S(1)} %fusion.4), channel_id=1, source_target_pairs={{496,0},{0,16},{16,32},{32,48},{48,64},{64,80},{80,96},{96,112},{1... | collective-permute-start | bytes 196616 | tf_op jit(solution)/shard_map/ppermute | solution.py:19
  408.5 7.6 %collective-permute-start.5 = (bf16[16,2048]{1,0:T(8,128)(2,1)S(1)}, bf16[16,2048]{1,0:T(8,128)(2,1)S(1)}, u32[]{:S(2)}, u32[]{:S(2)}) collective-permute-start(bf16[16,2048]{1,0:T(8,128)(2,1)S(1)} %fusion.4), channel_id=1, source_target_pairs={{16,0},{32,16},{48,32},{64,48},{80,64},{96,80},{112,96},{128,112},... | collective-permute-start | bytes 196616 | tf_op jit(solution)/shard_map/ppermute | solution.py:19
  417.5 7.7 %collective-permute-start.7 = (bf16[16,2048]{1,0:T(8,128)(2,1)S(1)}, bf16[16,2048]{1,0:T(8,128)(2,1)S(1)}, u32[]{:S(2)}, u32[]{:S(2)}) collective-permute-start(bf16[16,2048]{1,0:T(8,128)(2,1)S(1)} %fusion.5), channel_id=1, source_target_pairs={{16,0},{32,16},{48,32},{64,48},{80,64},{96,80},{112,96},{128,112},... | collective-permute-start | bytes 196616 | tf_op jit(solution)/shard_map/ppermute | solution.py:19
  426.8 25.2 %all-to-all-start.13 = ((bf16[16,16,640]{2,1,0:T(8,128)(2,1)}), bf16[16,16,640]{2,1,0:T(8,128)(2,1)S(1)}, u32[]{:S(2)}, u32[]{:S(2)}) async-start(bf16[16,16,640]{2,1,0:T(8,128)(2,1)} %pad_maximum_fusion.2), calls=%async_computation.13 | async-start | bytes 655360 | tf_op jit(solution)/shard_map/all_to_all | solution.py:23
  435.3 17.4 %copy-start.4 = (bf16[16,128,512]{2,1,0:T(8,128)(2,1)S(1)}, bf16[16,128,512]{2,1,0:T(8,128)(2,1)}, u32[]{:S(2)}) copy-start(bf16[16,128,512]{2,1,0:T(8,128)(2,1)} %get-tuple-element.16) | copy-start | bytes 6291460
  (16 other events, 54.9 us)
Sparse Core Ops, SparseCore 0:
  19.6 82.4 all-gather.10
  105.4 84.3 all-gather.6
  191.9 119.8 all-gather.8
  318.7 84.7 all-gather.12

commit v9 on v7

--- a/solution.py
+++ b/solution.py
@@ -140,11 +140,10 @@
     y_own = mm("sr,sk->rk", own_block, w_block)
 
     rest = after(rest, inverse_block)
-    wide = jnp.concatenate([coupling[0, 1], coupling[0, 0], folded(leaf_y)], axis=0)
+    wide = jnp.concatenate([coupling[0, 1], folded(leaf_y)], axis=0)
     gathered = lax.all_gather(after(wide, rest), FRONT, axis=0)
     node_coupling_all = gathered[:, :kp].reshape(K, C)
-    leaf_coupling_all = gathered[:, kp : 2 * kp].reshape(K, C)
-    leaf_y_all = unfolded(gathered[:, 2 * kp :]).reshape(na, nb, kp, R).transpose(1, 0, 2, 3).reshape(K, R)
+    leaf_y_all = unfolded(gathered[:, kp:]).reshape(na, nb, kp, R).transpose(1, 0, 2, 3).reshape(K, R)
 
     device = jnp.where(place < K, place // kp, (place - K) // kc)
     within = jnp.where(place < K, place % kp, kp + (place - K) % kc)
@@ -169,8 +168,6 @@
     gathered = lax.all_gather(wide, FRONT, axis=0)
     node_reach_all = gathered[:, :kp].reshape(K, C)
     leaf_pivots_all = unfolded(gathered[:, kp:]).reshape(K, R)
-    leaf_reach = mm("pm,mc->pc", pivot_inverse[0, 0], leaf_coupling_all).astype(BF16)
-    leaf_own = mm("pm,mr->pr", pivot_inverse[0, 0], leaf_pivots_all)
 
     y_block = to_all(part, "fa").reshape(R, K // nb)
     part = mm("bsk,rk->bsr", v_block, y_block).astype(BF16)
@@ -183,6 +180,10 @@
     part = total(exchange(part.reshape(nb, R // nb, nb * kp), "fb")).astype(BF16)
     part = exchange(part.reshape(na, rc, nb * kp), "fa")
     top = part.transpose(1, 0, 2).reshape(rc, K)
+
+    leaf_coupling_all = lax.all_gather(after(coupling[0, 0], node_reach), FRONT, axis=0, tiled=True)
+    leaf_reach = mm("pm,mc->pc", pivot_inverse[0, 0], leaf_coupling_all).astype(BF16)
+    leaf_own = mm("pm,mr->pr", pivot_inverse[0, 0], leaf_pivots_all)
 
     pivot_ids = jnp.arange(K, dtype=jnp.int32)[:, None]
     node_pick = (pivot_ids == parent_columns[0, 1][None]).astype(BF16)

time: 466 us -> 487 us (1.045)
  waiting for transfers between devices: 197 us -> 222 us
  blocking collectives: 92.7 us -> 107 us
  starting transfers between devices: 88.7 us -> 76.3 us
    all_gather x1, waiting for transfers between devices: 1.02 us -> 40.3 us  [per_device(): section_all = lax.all_gather(section_rows, FRONT, axis=0, tiled=True)]
    all_to_all x9, waiting for transfers between devices: 142 us -> 122 us  [exchange(): return lax.all_to_all(parts, axis, split_axis=0, concat_axis=0, tiled=True)]
    all_gather x1, waiting for transfers between devices: 19 us -> 2.96 us  [per_device(): gathered = lax.all_gather(after(wide, rest), FRONT, axis=0)]
    all_gather x0 -> x1, waiting for transfers between devices: none -> 15.8 us  [per_device(): lax.all_gather(after(coupling[0, 0], node_reach), FRONT, axis=0, tiled=True)]
    all_to_all x5, blocking collectives: 92.7 us -> 107 us  [exchange(): return lax.all_to_all(parts, axis, split_axis=0, concat_axis=0, tiled=True)]
    ppermute x8, starting transfers between devices: 28 us -> 21.5 us  [from_behind(): lax.ppermute(block, 'leaf', [((i - distance) % count, i) for i in range(c...]
    all_to_all x9, starting transfers between devices: 60.6 us -> 54.6 us  [exchange(): return lax.all_to_all(parts, axis, split_axis=0, concat_axis=0, tiled=True)]
    all_gather x1, waiting for transfers between devices: 20 us -> 25.6 us  [per_device(): lax.all_gather(node_vectors_rest[0, 0], FRONT, axis=0, tiled=True)]
  transfers between devices with their start and end apart: 21 -> 22, of which waited for: 17 -> 16; matrix products, arithmetic and copies ran while one was open for 10% -> 10% of each run, Pallas kernels for 0% -> 0%
where the time goes in v9:
time: 487 us; the launch traced here: 486 us
  waiting for transfers between devices  222 us (46%)
  blocking collectives  107 us (22%)
  starting transfers between devices  76.3 us (16%)
  local copies, waits for them, and re-layouts  28.4 us (6%)
  matrix products  23.5 us (5%)
  between operations  18.7 us (4%)
  other arithmetic  9.74 us (2%)
    all_to_all x9, waiting for transfers between devices, exchange(): return lax.all_to_all(parts, axis, split_axis=0, concat_axis=0, tiled=True)  122 us
    all_to_all x5, blocking collectives, exchange(): return lax.all_to_all(parts, axis, split_axis=0, concat_axis=0, tiled=True)  107 us
    all_to_all x9, starting transfers between devices, exchange(): return lax.all_to_all(parts, axis, split_axis=0, concat_axis=0, tiled=True)  54.6 us
    all_gather x1, waiting for transfers between devices, per_device(): section_all = lax.all_gather(section_rows, FRONT, axis=0, tiled=True)  40.3 us
    all_gather x1, waiting for transfers between devices, per_device(): lax.all_gather(node_vectors_rest[0, 0], FRONT, axis=0, tiled=True)  25.6 us
    dot_general x19, matrix products, mm(): return jnp.einsum(spec, a, b, preferred_element_type=F32)  23.5 us
    ppermute x8, starting transfers between devices, from_behind(): lax.ppermute(block, 'leaf', [((i - distance) % count, i) for i in range(c...  21.5 us
    all_gather x1, waiting for transfers between devices, per_device(): lax.all_gather(after(coupling[0, 0], node_reach), FRONT, axis=0, tiled=True)  15.8 us
  transfers between devices with their start and end apart: 22, of which 16 were waited for; matrix products, arithmetic and copies ran while one was open for 10% of the time, Pallas kernels for 0%

profile of v9, /device:TPU:24, one launch (start us, length us, event | category | flops | bytes accessed | tf_op | source)
XLA Modules:
  0.0 485.6 jit_solution(14963326481200486663)
XLA Ops:
  10.2 6.0 %all-to-all-start.1 = ((bf16[4,512,256]{2,1,0:T(8,128)(2,1)}), bf16[4,512,256]{2,1,0:T(8,128)(2,1)S(1)}, u32[]{:S(2)}, u32[]{:S(2)}) async-start(bf16[4,512,256]{2,1,0:T(8,128)(2,1)} %bitcast.17), calls=%async_computation.1 | async-start | bytes 2097152 | tf_op jit(solution)/shard_map/all_to_all | solution.py:23
  18.0 25.1 %all-to-all-done.1 = bf16[4,512,256]{2,1,0:T(8,128)(2,1)S(1)} async-done(((bf16[4,512,256]{2,1,0:T(8,128)(2,1)}), bf16[4,512,256]{2,1,0:T(8,128)(2,1)S(1)}, u32[]{:S(2)}, u32[]{:S(2)}) %all-to-all-start.1) | async-done | bytes 1048608 | tf_op jit(solution)/shard_map/all_to_all | solution.py:23
  44.1 14.1 %all-to-all-start.2 = ((bf16[4,128,256]{2,1,0:T(8,128)(2,1)}), bf16[4,128,256]{2,1,0:T(8,128)(2,1)S(1)}, u32[]{:S(2)}, u32[]{:S(2)}) async-start(bf16[4,128,256]{2,1,0:T(8,128)(2,1)} %bitcast.18), calls=%async_computation.2 | async-start | bytes 524288 | tf_op jit(solution)/shard_map/all_to_all | solution.py:23
  60.2 19.4 %all-to-all-done.2 = bf16[4,128,256]{2,1,0:T(8,128)(2,1)S(1)} async-done(((bf16[4,128,256]{2,1,0:T(8,128)(2,1)}), bf16[4,128,256]{2,1,0:T(8,128)(2,1)S(1)}, u32[]{:S(2)}, u32[]{:S(2)}) %all-to-all-start.2) | async-done | bytes 262176 | tf_op jit(solution)/shard_map/all_to_all | solution.py:23
  84.4 25.6 %all-gather.13.cloned.1.call-done = bf16[1,1,512,2048]{3,2,1,0:T(8,128)(2,1)} async-done(((bf16[1,1,32,2048]{3,2,1,0:T(8,128)(2,1)}), bf16[1,1,512,2048]{3,2,1,0:T(8,128)(2,1)}) %all-gather.13.cloned.1.call-update) | async-done | bytes 2097168 | tf_op jit(solution)/shard_map/all_gather | solution.py:100
  119.4 9.2 %all-to-all-done.5 = bf16[4,128,512]{2,1,0:T(8,128)(2,1)S(1)} async-done(((bf16[4,128,512]{2,1,0:T(8,128)(2,1)}), bf16[4,128,512]{2,1,0:T(8,128)(2,1)S(1)}, u32[]{:S(2)}, u32[]{:S(2)}) %all-to-all-start.5) | async-done | bytes 524320 | tf_op jit(solution)/shard_map/all_to_all | solution.py:23
  128.6 7.6 %all-to-all-start.3 = ((bf16[16,16,512]{2,1,0:T(8,128)(2,1)}), bf16[16,16,512]{2,1,0:T(8,128)(2,1)}, u32[]{:S(2)}, u32[]{:S(2)}) async-start(bf16[16,16,512]{2,1,0:T(8,128)(2,1)} %bitcast.23), calls=%async_computation.3 | async-start | bytes 524288 | tf_op jit(solution)/shard_map/all_to_all | solution.py:23
  141.1 13.5 %all-to-all-done.3 = bf16[16,16,512]{2,1,0:T(8,128)(2,1)} async-done(((bf16[16,16,512]{2,1,0:T(8,128)(2,1)}), bf16[16,16,512]{2,1,0:T(8,128)(2,1)}, u32[]{:S(2)}, u32[]{:S(2)}) %all-to-all-start.3) | async-done | bytes 262176 | tf_op jit(solution)/shard_map/all_to_all | solution.py:23
  158.9 4.5 all-to-all-start.4
  168.6 40.3 %all-gather.9.cloned.1.call-done = bf16[2560,512]{1,0:T(8,128)(2,1)} async-done(((bf16[160,512]{1,0:T(8,128)(2,1)}), bf16[2560,512]{1,0:T(8,128)(2,1)}) %all-gather.9.cloned.1.call-update) | async-done | bytes 2621456 | tf_op jit(solution)/shard_map/all_gather | solution.py:124
  211.4 5.1 %gather_fusion = bf16[1024,512]{1,0:T(8,128)(2,1)} fusion(bf16[2560,512]{1,0:T(8,128)(2,1)S(1)} %copy-done, s32[1024]{0:T(1024)S(1)} %broadcast_clamp_fusion), kind=kCustom, calls=%fused_computation | custom fusion | bytes 2101248 | tf_op jit(solution)/shard_map/jit(_take)/gather | solution.py:150
  220.0 5.8 %collective-permute-start.2 = (bf16[16,512]{1,0:T(8,128)(2,1)S(1)}, bf16[16,512]{1,0:T(8,128)(2,1)S(1)}, u32[]{:S(2)}, u32[]{:S(2)}) collective-permute-start(bf16[16,512]{1,0:T(8,128)(2,1)S(1)} %fusion.51), channel_id=1, source_target_pairs={{16,0},{32,16},{48,32},{64,48},{80,64},{96,80},{112,96},{128,112},... | collective-permute-start | bytes 49160 | tf_op jit(solution)/shard_map/ppermute | solution.py:19
  235.1 8.2 %all-to-all-start.6 = ((bf16[16,16,512]{2,1,0:T(8,128)(2,1)}), bf16[16,16,512]{2,1,0:T(8,128)(2,1)S(1)}, u32[]{:S(2)}, u32[]{:S(2)}) async-start(bf16[16,16,512]{2,1,0:T(8,128)(2,1)} %broadcast_in_dim.62), calls=%async_computation.6 | async-start | bytes 524288 | tf_op jit(solution)/shard_map/all_to_all | solution.py:23
  247.2 18.0 %all-to-all-done.6 = bf16[16,16,512]{2,1,0:T(8,128)(2,1)S(1)} async-done(((bf16[16,16,512]{2,1,0:T(8,128)(2,1)}), bf16[16,16,512]{2,1,0:T(8,128)(2,1)S(1)}, u32[]{:S(2)}, u32[]{:S(2)}) %all-to-all-start.6) | async-done | bytes 262176 | tf_op jit(solution)/shard_map/all_to_all | solution.py:23
  266.0 30.9 %all_to_all.70 = bf16[4,64,512]{2,1,0:T(8,128)(2,1)S(1)} all-to-all(bf16[4,64,512]{2,1,0:T(8,128)(2,1)S(1)} %bitcast.211), channel_id=1, replica_groups=mesh['leaf'=32,'fa'=4,'fb'=4] {'fa'}, dimensions={0} | all-to-all | bytes 524288 | tf_op jit(solution)/shard_map/all_to_all | solution.py:23
  306.1 24.9 %all_to_all.71 = bf16[4,64,512]{2,1,0:T(8,128)(2,1)S(1)} all-to-all(bf16[4,64,512]{2,1,0:T(8,128)(2,1)S(1)} %broadcast_in_dim.63), channel_id=1, replica_groups=mesh['leaf'=32,'fa'=4,'fb'=4] {'fa'}, dimensions={0} | all-to-all | bytes 524288 | tf_op jit(solution)/shard_map/all_to_all | solution.py:23
  332.5 21.6 %all_to_all.72 = bf16[4,160,256]{2,1,0:T(8,128)(2,1)S(1)} all-to-all(bf16[4,160,256]{2,1,0:T(8,128)(2,1)S(1)} %convolution_convert_fusion), channel_id=1, replica_groups=mesh['leaf'=32,'fa'=4,'fb'=4] {'fb'}, dimensions={0} | all-to-all | bytes 655360 | tf_op jit(solution)/shard_map/all_to_all | solution.py:23
  355.2 3.6 all-to-all-start.10
  360.7 17.0 %all-to-all-done.10 = bf16[4,128,256]{2,1,0:T(8,128)(2,1)S(1)} async-done(((bf16[4,128,256]{2,1,0:T(8,128)(2,1)}), bf16[4,128,256]{2,1,0:T(8,128)(2,1)S(1)}, u32[]{:S(2)}, u32[]{:S(2)}) %all-to-all-start.10) | async-done | bytes 262176 | tf_op jit(solution)/shard_map/all_to_all | solution.py:23
  378.0 12.3 %all_to_all.73 = bf16[4,64,512]{2,1,0:T(8,128)(2,1)S(1)} all-to-all(bf16[4,64,512]{2,1,0:T(8,128)(2,1)S(1)} %bitcast.202), channel_id=1, replica_groups=mesh['leaf'=32,'fa'=4,'fb'=4] {'fb'}, dimensions={0} | all-to-all | bytes 524288 | tf_op jit(solution)/shard_map/all_to_all | solution.py:23
  390.3 17.0 %all_to_all.74 = bf16[4,16,512]{2,1,0:T(8,128)(2,1)S(1)} all-to-all(bf16[4,16,512]{2,1,0:T(8,128)(2,1)S(1)} %bitcast.210), channel_id=1, replica_groups=mesh['leaf'=32,'fa'=4,'fb'=4] {'fa'}, dimensions={0} | all-to-all | bytes 131072 | tf_op jit(solution)/shard_map/all_to_all | solution.py:23
  421.3 5.3 %collective-permute-done.6 = bf16[16,2048]{1,0:T(8,128)(2,1)S(1)} collective-permute-done((bf16[16,2048]{1,0:T(8,128)(2,1)S(1)}, bf16[16,2048]{1,0:T(8,128)(2,1)S(1)}, u32[]{:S(2)}, u32[]{:S(2)}) %collective-permute-start.6) | collective-permute-done | bytes 65568 | tf_op jit(solution)/shard_map/ppermute | solution.py:19
  439.6 20.2 %all-to-all-done.13 = bf16[16,16,640]{2,1,0:T(8,128)(2,1)S(1)} async-done(((bf16[16,16,640]{2,1,0:T(8,128)(2,1)}), bf16[16,16,640]{2,1,0:T(8,128)(2,1)S(1)}, u32[]{:S(2)}, u32[]{:S(2)}) %all-to-all-start.13) | async-done | bytes 327712 | tf_op jit(solution)/shard_map/all_to_all | solution.py:23
  459.8 15.8 %all-gather.17.cloned.1.call-done = bf16[1,1,2048,512]{3,2,1,0:T(8,128)(2,1)} async-done(((bf16[1,1,128,512]{3,2,1,0:T(8,128)(2,1)}), bf16[1,1,2048,512]{3,2,1,0:T(8,128)(2,1)}) %all-gather.17.cloned.1.call-update) | async-done | bytes 2097168 | tf_op jit(solution)/shard_map/all_gather | solution.py:184
  (187 shorter events, 95.8 us)
Async XLA Ops:
  10.2 32.9 %all-to-all-start.1 = ((bf16[4,512,256]{2,1,0:T(8,128)(2,1)}), bf16[4,512,256]{2,1,0:T(8,128)(2,1)S(1)}, u32[]{:S(2)}, u32[]{:S(2)}) async-start(bf16[4,512,256]{2,1,0:T(8,128)(2,1)} %bitcast.17), calls=%async_computation.1 | async-start | bytes 2097152 | tf_op jit(solution)/shard_map/all_to_all | solution.py:23
  16.3 93.7 %all-gather.13.cloned.1.call-start = ((), (), s32[]{:S(2)}) async-start(), calls=%async_computation.16 | async-start | bytes 2228224 | tf_op jit(solution)/shard_map/all_gather | solution.py:100
  44.1 35.5 %all-to-all-start.2 = ((bf16[4,128,256]{2,1,0:T(8,128)(2,1)}), bf16[4,128,256]{2,1,0:T(8,128)(2,1)S(1)}, u32[]{:S(2)}, u32[]{:S(2)}) async-start(bf16[4,128,256]{2,1,0:T(8,128)(2,1)} %bitcast.18), calls=%async_computation.2 | async-start | bytes 524288 | tf_op jit(solution)/shard_map/all_to_all | solution.py:23
  79.6 35.2 %all-to-all-start = ((bf16[16,16,448]{2,1,0:T(8,128)(2,1)}), bf16[16,16,448]{2,1,0:T(8,128)(2,1)S(1)}, u32[]{:S(2)}, u32[]{:S(2)}) async-start(bf16[16,16,448]{2,1,0:T(8,128)(2,1)} %bitcast.12), calls=%async_computation | async-start | bytes 524288 | tf_op jit(solution)/shard_map/all_to_all | solution.py:23
  83.1 125.8 %all-gather.9.cloned.1.call-start = ((), (), s32[]{:S(2)}) async-start(), calls=%async_computation.14 | async-start | bytes 2785280 | tf_op jit(solution)/shard_map/all_gather | solution.py:124
  114.8 13.8 %all-to-all-start.5 = ((bf16[4,128,512]{2,1,0:T(8,128)(2,1)}), bf16[4,128,512]{2,1,0:T(8,128)(2,1)S(1)}, u32[]{:S(2)}, u32[]{:S(2)}) async-start(bf16[4,128,512]{2,1,0:T(8,128)(2,1)} %reshape.398), calls=%async_computation.5 | async-start | bytes 1048576 | tf_op jit(solution)/shard_map/all_to_all | solution.py:23
  128.6 25.9 %all-to-all-start.3 = ((bf16[16,16,512]{2,1,0:T(8,128)(2,1)}), bf16[16,16,512]{2,1,0:T(8,128)(2,1)}, u32[]{:S(2)}, u32[]{:S(2)}) async-start(bf16[16,16,512]{2,1,0:T(8,128)(2,1)} %bitcast.23), calls=%async_computation.3 | async-start | bytes 524288 | tf_op jit(solution)/shard_map/all_to_all | solution.py:23
  158.9 75.4 %all-to-all-start.4 = ((bf16[4,400,512]{2,1,0:T(8,128)(2,1)}), bf16[4,400,512]{2,1,0:T(8,128)(2,1)}, u32[]{:S(2)}, u32[]{:S(2)}) async-start(bf16[4,400,512]{2,1,0:T(8,128)(2,1)} %maximum_add_fusion), calls=%async_computation.4 | async-start | bytes 3276800 | tf_op jit(solution)/shard_map/all_to_all | solution.py:23
  163.4 137.7 %all-gather.11.cloned.1.call-start = ((), (), s32[]{:S(2)}) async-start(), calls=%async_computation.15 | async-start | bytes 3342336 | tf_op jit(solution)/shard_map/all_gather | solution.py:144
  166.1 50.4 %collective-permute-start = (bf16[16,512]{1,0:T(8,128)(2,1)}, bf16[16,512]{1,0:T(8,128)(2,1)S(1)}, u32[]{:S(2)}, u32[]{:S(2)}) collective-permute-start(bf16[16,512]{1,0:T(8,128)(2,1)} %get-tuple-element.14), channel_id=1, source_target_pairs={{496,0},{0,16},{16,32},{32,48},{48,64},{64,80},{80,96},{96,112},{1... | collective-permute-start | bytes 49160 | tf_op jit(solution)/shard_map/ppermute | solution.py:19
  218.1 7.7 %collective-permute-start.1 = (bf16[16,512]{1,0:T(8,128)(2,1)S(1)}, bf16[16,512]{1,0:T(8,128)(2,1)S(1)}, u32[]{:S(2)}, u32[]{:S(2)}) collective-permute-start(bf16[16,512]{1,0:T(8,128)(2,1)S(1)} %fusion.51), channel_id=1, source_target_pairs={{496,0},{0,16},{16,32},{32,48},{48,64},{64,80},{80,96},{96,112},{1... | collective-permute-start | bytes 49160 | tf_op jit(solution)/shard_map/ppermute | solution.py:19
  220.0 7.2 %collective-permute-start.2 = (bf16[16,512]{1,0:T(8,128)(2,1)S(1)}, bf16[16,512]{1,0:T(8,128)(2,1)S(1)}, u32[]{:S(2)}, u32[]{:S(2)}) collective-permute-start(bf16[16,512]{1,0:T(8,128)(2,1)S(1)} %fusion.51), channel_id=1, source_target_pairs={{16,0},{32,16},{48,32},{64,48},{80,64},{96,80},{112,96},{128,112},... | collective-permute-start | bytes 49160 | tf_op jit(solution)/shard_map/ppermute | solution.py:19
  228.7 5.6 %collective-permute-start.3 = (bf16[16,512]{1,0:T(8,128)(2,1)S(1)}, bf16[16,512]{1,0:T(8,128)(2,1)S(1)}, u32[]{:S(2)}, u32[]{:S(2)}) collective-permute-start(bf16[16,512]{1,0:T(8,128)(2,1)S(1)} %fusion.52), channel_id=1, source_target_pairs={{32,0},{48,16},{64,32},{80,48},{96,64},{112,80},{128,96},{144,112}... | collective-permute-start | bytes 49160 | tf_op jit(solution)/shard_map/ppermute | solution.py:19
  235.1 30.1 %all-to-all-start.6 = ((bf16[16,16,512]{2,1,0:T(8,128)(2,1)}), bf16[16,16,512]{2,1,0:T(8,128)(2,1)S(1)}, u32[]{:S(2)}, u32[]{:S(2)}) async-start(bf16[16,16,512]{2,1,0:T(8,128)(2,1)} %broadcast_in_dim.62), calls=%async_computation.6 | async-start | bytes 524288 | tf_op jit(solution)/shard_map/all_to_all | solution.py:23
  243.3 167.2 %all-gather.15.cloned.1.call-start = ((), (), s32[]{:S(2)}) async-start(), calls=%async_computation.17 | async-start | bytes 3342336 | tf_op jit(solution)/shard_map/all_gather | solution.py:168
  305.3 48.9 %copy-start.6 = (pred[160,1024]{1,0:T(32,128)(4,1)S(1)}, pred[160,1024]{1,0:T(32,128)(4,1)}, u32[]{:S(2)}) copy-start(pred[160,1024]{1,0:T(32,128)(4,1)} %get-tuple-element.32) | copy-start | bytes 491524
  354.2 56.3 %copy-start.18 = (s32[1,2,512]{2,1,0:T(2,128)S(1)}, s32[1,2,512]{2,1,0:T(2,128)}, u32[]{:S(2)}) copy-start(s32[1,2,512]{2,1,0:T(2,128)} %param.21) | copy-start | bytes 12292
  355.2 22.5 %all-to-all-start.10 = ((bf16[4,128,256]{2,1,0:T(8,128)(2,1)}), bf16[4,128,256]{2,1,0:T(8,128)(2,1)S(1)}, u32[]{:S(2)}, u32[]{:S(2)}) async-start(bf16[4,128,256]{2,1,0:T(8,128)(2,1)} %broadcast_in_dim.64), calls=%async_computation.10 | async-start | bytes 524288 | tf_op jit(solution)/shard_map/all_to_all | solution.py:23
  358.8 116.9 %all-gather.17.cloned.1.call-start = ((), (), s32[]{:S(2)}) async-start(), calls=%async_computation.18 | async-start | bytes 2228224 | tf_op jit(solution)/shard_map/all_gather | solution.py:184
  407.3 8.3 %collective-permute-start.4 = (bf16[16,2048]{1,0:T(8,128)(2,1)S(1)}, bf16[16,2048]{1,0:T(8,128)(2,1)S(1)}, u32[]{:S(2)}, u32[]{:S(2)}) collective-permute-start(bf16[16,2048]{1,0:T(8,128)(2,1)S(1)} %bitcast.216), channel_id=1, source_target_pairs={{480,0},{496,16},{0,32},{16,48},{32,64},{48,80},{64,96},{80,112},{... | collective-permute-start | bytes 196616 | tf_op jit(solution)/shard_map/ppermute | solution.py:19
  416.9 4.4 collective-permute-start.5
  418.9 7.7 %collective-permute-start.6 = (bf16[16,2048]{1,0:T(8,128)(2,1)S(1)}, bf16[16,2048]{1,0:T(8,128)(2,1)S(1)}, u32[]{:S(2)}, u32[]{:S(2)}) collective-permute-start(bf16[16,2048]{1,0:T(8,128)(2,1)S(1)} %fusion.4), channel_id=1, source_target_pairs={{496,0},{0,16},{16,32},{32,48},{48,64},{64,80},{80,96},{96,112},{1... | collective-permute-start | bytes 196616 | tf_op jit(solution)/shard_map/ppermute | solution.py:19
  427.9 3.8 collective-permute-start.7
  433.3 26.5 %all-to-all-start.13 = ((bf16[16,16,640]{2,1,0:T(8,128)(2,1)}), bf16[16,16,640]{2,1,0:T(8,128)(2,1)S(1)}, u32[]{:S(2)}, u32[]{:S(2)}) async-start(bf16[16,16,640]{2,1,0:T(8,128)(2,1)} %pad_maximum_fusion.2), calls=%async_computation.13 | async-start | bytes 655360 | tf_op jit(solution)/shard_map/all_to_all | solution.py:23
  (20 other events, 224.1 us)
Sparse Core Ops, SparseCore 0:
  19.7 90.1 all-gather.12
  113.3 95.5 all-gather.8
  211.0 90.1 all-gather.10
  306.2 85.9 all-gather.14
  394.7 80.9 all-gather.16
